TPU v7x, 32 devices: a whole 2x2x4 slice. The times are simulated.
32 devices in a mesh: cluster: 8 (over y, x, core), blk: 4 (over z).
Axes of the slice: x: 2, y: 2, z: 4, core: 2. Of those that a mesh axis runs over, the one named last changes fastest.
Arguments:
- codes: int32 [8, 4, 64, 512], P('cluster', 'blk'), may hold values from 0 to 255
- routes: int32 [8, 4, 512, 1], P('cluster', 'blk'), may hold values from 0 to 31; in each aligned block of 512 rows (0 to 511, 512 to 1023, ..., all dimensions but the last counted through in order) at most 32 rows name the same one
- codebook: bfloat16 [256, 1024], replicated, may hold values from -6 to 6
- centroids: bfloat16 [8, 1024], replicated, may hold values from -3 to 3
Outputs:
- nearest: float32 [8, 4, 1024], P('cluster', 'blk')
Inputs may be any that keep to these rules, and one draw needn't show every extreme that they name: `routes`: within the rows of one device no destination is named more than 32 times, and in every draw some device names some destination exactly 32 times; every destination is named somewhere.
All inputs are finite; a program needn't handle non-finite values.
Results may differ from a plain program's by a relative error of at most 0.00043.
Values may be sent and summed in bfloat16 or wider, within the bound.
No kernel may reach another device: no remote copies, remote signals or barrier semaphores. Data moves between devices by JAX's collectives and lax.ppermute only.
A program may use at most 64 MiB of HBM per device.

v0:
```python
import jax
import jax.numpy as jnp
from jax import lax
from jax.sharding import PartitionSpec as P


def tile_scores(left_rows, right_rows):
    return lax.dot_general(
        left_rows, right_rows, (((1,), (1,)), ((), ())), preferred_element_type=jnp.float32
    )


def decode_rows(code_matrix, centre, codebook):
    subspaces = code_matrix.shape[0]
    row_count = code_matrix.shape[1]
    words = codebook.shape[0]
    width = codebook.shape[1]
    sub_width = width // subspaces
    onehot = (code_matrix[:, :, None] == jnp.arange(words, dtype=jnp.int32)[None, None, :]).astype(
        jnp.bfloat16
    )
    residual = jnp.einsum(
        "mrk,kmd->rmd",
        onehot,
        codebook.reshape(words, subspaces, sub_width),
        preferred_element_type=jnp.float32,
    ).reshape(row_count, width)
    embed = centre + residual
    return (embed / jnp.sqrt(jnp.sum(embed * embed, axis=1, keepdims=True) + 1e-06)).astype(
        jnp.bfloat16
    )


def on_device(codes, routes, codebook, centroids):
    groups = lax.axis_size("cluster")
    members = lax.axis_size("blk")
    devices = groups * members
    codes_here = codes[0, 0]
    targets = routes[0, 0, :, 0]
    in_rows = targets.shape[0]
    capacity = 2 * in_rows // devices
    slot_count = devices * capacity
    width = codebook.shape[1]
    target_hot = (targets[:, None] == jnp.arange(devices, dtype=jnp.int32)[None, :]).astype(
        jnp.int32
    )
    running = jnp.cumsum(target_hot, axis=0)
    position = jnp.sum(target_hot * (running - 1), axis=1)
    out_marks = jnp.zeros((devices, capacity), jnp.bfloat16).at[targets, position].set(1.0)
    select = ((targets // members)[:, None] == jnp.arange(groups, dtype=jnp.int32)[None, :]).astype(
        jnp.bfloat16
    )
    centre = jnp.dot(select, centroids, preferred_element_type=jnp.float32)
    units = decode_rows(codes_here, centre, codebook)
    outgoing = jnp.zeros((devices, capacity, width), jnp.bfloat16).at[targets, position].set(units)
    arrived, arrived_marks = (
        lax.all_to_all(outgoing, ("cluster", "blk"), split_axis=0, concat_axis=0, tiled=True),
        lax.all_to_all(out_marks, ("cluster", "blk"), split_axis=0, concat_axis=0, tiled=True),
    )
    my_rows = arrived.reshape(slot_count, width)
    my_marks = arrived_marks.reshape(slot_count)
    my_valid = my_marks.astype(jnp.float32) > 0
    row_ids = lax.axis_index("blk") * slot_count + jnp.arange(slot_count, dtype=jnp.int32)
    initial = jnp.full((slot_count,), -4.0, jnp.float32)
    rows_in = lax.all_gather(my_rows, "blk", axis=0, tiled=True)
    marks_in = lax.all_gather(my_marks, "blk", axis=0, tiled=True)
    scores = tile_scores(my_rows, rows_in)
    col_ids = jnp.arange(rows_in.shape[0], dtype=jnp.int32)
    keep = (marks_in.astype(jnp.float32)[None, :] > 0) & (col_ids[None, :] != row_ids[:, None])
    best = jnp.maximum(initial, jnp.max(jnp.where(keep, scores, -4.0), axis=1))
    nearest = jnp.where(my_valid, best, 0.0)
    return nearest.reshape(1, 1, slot_count)


def solution(mesh):
    in_specs = (P("cluster", "blk", None, None), P("cluster", "blk", None, None), P(), P())
    out_specs = P("cluster", "blk", None)
    return jax.shard_map(
        on_device, mesh=mesh, in_specs=in_specs, out_specs=out_specs, check_vma=False
    )
```

profile of v0, /device:TPU:0, one launch (start us, length us, event | category | flops | bytes accessed | tf_op | source)
XLA Modules:
  0.0 282.1 jit_solution(8713793023342042385)
XLA Ops:
  6.5 0.0 copy-start
  6.5 0.0 all-gather.2.cloned.1.call-start
  6.5 0.7 add_select_fusion
  7.2 0.7 fusion.6
  7.9 1.2 reduce-window.6
  9.1 0.2 slice_reduce_fusion
  9.4 0.8 fusion.5
  10.1 0.7 or_select_fusion
  10.8 1.2 copy.16
  12.1 9.4 %fusion = f32[64,512,16]{1,2,0:T(8,128)} fusion(bf16[256,64,16]{0,2,1:T(8,128)(2,1)S(1)} %bitcast.41, s32[64,512]{1,0:T(8,128)} %bitcast.47), kind=kOutput, calls=%fused_computation.3 | convolution fusion | flops 276824064 | bytes 2752512 | tf_op jit(solution)/shard_map/mrk,kmd->rmd/dot_general | solution.py:22
  21.5 1.9 copy.17
  23.4 0.0 copy-done
  23.4 0.6 multiply_reduce_fusion
  24.0 0.3 divide_convert_fusion
  24.3 0.3 broadcast_in_dim.14
  24.6 32.8 %scatter_fusion.1 = bf16[32,32,1024]{2,1,0:T(8,128)(2,1)S(1)} fusion(bf16[32,32,1024]{2,1,0:T(8,128)(2,1)S(1)} %broadcast_in_dim.14, s32[512]{0:T(512)S(1)} %bitcast.36, bf16[512,1024]{1,0:T(8,128)(2,1)S(1)} %divide_convert_fusion), kind=kCustom, calls=%fused_computation.1 | custom fusion | bytes 3149824 | tf_op jit(solution)/shard_map/scatter | solution.py:55
  57.3 54.8 %all_to_all.14 = bf16[32,32,1024]{2,1,0:T(8,128)(2,1)} all-to-all(bf16[32,32,1024]{2,1,0:T(8,128)(2,1)S(1)} %scatter_fusion.1), channel_id=1, replica_groups=mesh['cluster'=8,'blk'=4] {'cluster','blk'}, dimensions={0} | all-to-all | bytes 4194304 | tf_op jit(solution)/shard_map/all_to_all | solution.py:57
  112.1 0.0 copy-start.1
  112.1 0.0 all-gather.2.cloned.1.call-update
  112.1 25.2 %scatter_fusion = bf16[32,32]{1,0:T(8,128)(2,1)S(1)} fusion(bf16[32,32]{1,0:T(8,128)(2,1)S(1)} %broadcast_in_dim.12, s32[512]{0:T(512)S(1)} %bitcast.37, bf16[512]{0:T(512)(128)(2,1)S(1)} %broadcast.163), kind=kCustom, calls=%fused_computation | custom fusion | bytes 7168 | tf_op jit(solution)/shard_map/scatter | solution.py:49
  137.4 0.6 copy.15
  138.0 4.5 %all-to-all-start = ((bf16[32,1,32]{2,1,0:T(2,128)(2,1)}), bf16[32,1,32]{2,1,0:T(2,128)(2,1)S(1)}, u32[]{:S(2)}, u32[]{:S(2)}) async-start(bf16[32,1,32]{2,1,0:T(2,128)(2,1)} %copy.15), calls=%async_computation | async-start | bytes 32768 | tf_op jit(solution)/shard_map/all_to_all | solution.py:58
  142.5 8.1 %all-to-all-done = bf16[32,1,32]{2,1,0:T(2,128)(2,1)S(1)} async-done(((bf16[32,1,32]{2,1,0:T(2,128)(2,1)}), bf16[32,1,32]{2,1,0:T(2,128)(2,1)S(1)}, u32[]{:S(2)}, u32[]{:S(2)}) %all-to-all-start) | async-done | bytes 2080 | tf_op jit(solution)/shard_map/all_to_all | solution.py:58
  150.5 0.1 reduce.2
  150.6 0.1 reshape.145
  150.7 0.1 compare_reduce_fusion
  150.7 0.1 gt.27
  150.8 12.0 %all_gather.6 = bf16[4096]{0:T(1024)(128)(2,1)S(1)} all-gather(bf16[1024]{0:T(1024)(128)(2,1)S(1)} %reshape.145), channel_id=1, replica_groups=mesh['cluster'=8,'blk'=4] {'blk'}, dimensions={0}, use_global_device_ids=true | all-gather | bytes 10240 | tf_op jit(solution)/shard_map/all_gather | solution.py:66
  162.9 99.3 %all-gather.2.cloned.1.call-done = bf16[4096,1024]{1,0:T(8,128)(2,1)} async-done(((bf16[1024,1024]{1,0:T(8,128)(2,1)}), bf16[4096,1024]{1,0:T(8,128)(2,1)}) %all-gather.2.cloned.1.call-update) | async-done | bytes 8388624 | tf_op jit(solution)/shard_map/all_gather | solution.py:65
  262.2 0.0 copy-done.1
  262.2 12.4 %select_reduce_fusion = f32[1024]{0:T(1024)S(1)} fusion(s32[1024]{0:T(1024)S(1)} %iota_add_fusion, pred[4096]{0:T(1024)(128)(4,1)S(1)} %convert_compare_fusion, bf16[1024,1024]{1,0:T(8,128)(2,1)S(1)} %bitcast.39, bf16[4096,1024]{1,0:T(8,128)(2,1)} %all-gather.2.cloned.1.call-done), kind=kOutput, calls=%fused_computation.4 | convolution fusion | flops 8606710784 | bytes 10498048 | tf_op jit(solution)/shard_map/dot_general | solution.py:8
  274.6 0.6 broadcast_select_fusion
  (8 shorter events, 0.1 us)
Async XLA Ops:
  6.5 16.9 %copy-start = (bf16[8,1024]{1,0:T(8,128)(2,1)S(1)}, bf16[8,1024]{1,0:T(8,128)(2,1)}, u32[]{:S(2)}) copy-start(bf16[8,1024]{1,0:T(8,128)(2,1)} %param.7) | copy-start | bytes 49156
  6.5 255.7 %all-gather.2.cloned.1.call-start = ((), (), s32[]{:S(2)}) async-start(), calls=%async_computation.2 | async-start | bytes 10485760 | tf_op jit(solution)/shard_map/all_gather | solution.py:65
  112.1 150.1 %copy-start.1 = (bf16[32,32,1024]{2,1,0:T(8,128)(2,1)S(1)}, bf16[32,32,1024]{2,1,0:T(8,128)(2,1)}, u32[]{:S(2)}) copy-start(bf16[32,32,1024]{2,1,0:T(8,128)(2,1)} %all_to_all.14) | copy-start | bytes 6291460
  138.0 12.6 %all-to-all-start = ((bf16[32,1,32]{2,1,0:T(2,128)(2,1)}), bf16[32,1,32]{2,1,0:T(2,128)(2,1)S(1)}, u32[]{:S(2)}, u32[]{:S(2)}) async-start(bf16[32,1,32]{2,1,0:T(2,128)(2,1)} %copy.15), calls=%async_computation | async-start | bytes 32768 | tf_op jit(solution)/shard_map/all_to_all | solution.py:58
Sparse Core Ops, SparseCore 0:
  112.2 149.9 all-gather.1
where the time goes:
time: 282 us
  waiting for transfers between devices  107 us (38%)
  blocking collectives  66.8 us (24%)
  local copies, waits for them, and re-layouts  62.4 us (22%)
  matrix products  22.4 us (8%)
  between operations  13.5 us (5%)
  other arithmetic  5.13 us (2%)
  starting transfers between devices  4.47 us (2%)
    all_gather x1, waiting for transfers between devices, on_device(): rows_in = lax.all_gather(my_rows, 'blk', axis=0, tiled=True)  99.3 us
    all_to_all x1, blocking collectives, on_device(): lax.all_to_all(outgoing, ('cluster', 'blk'), split_axis=0, concat_axis=0,...  54.8 us
    scatter x1, local copies, waits for them, and re-layouts, on_device(): jnp.zeros((devices, capacity, width), jnp.bfloat16).at[targets, position]  32.8 us
    scatter x1, local copies, waits for them, and re-layouts, on_device(): jnp.zeros((devices, capacity), jnp.bfloat16).at[targets, position].set(1.0)  25.2 us
    dot_general x1, matrix products, tile_scores(): lax.dot_general(left_rows, right_rows, (((1,), (1,)), ((), ())), preferre...  12.4 us
    all_gather x1, blocking collectives, on_device(): marks_in = lax.all_gather(my_marks, 'blk', axis=0, tiled=True)  12 us
    dot_general x1, matrix products, decode_rows(): jnp.einsum('mrk,kmd->rmd', onehot, codebook.reshape(words, subspaces, sub...  9.37 us
    all_to_all x1, waiting for transfers between devices, on_device(): lax.all_to_all(out_marks, ('cluster', 'blk'), split_axis=0, concat_axis=0...  8.08 us
  transfers between devices with their start and end apart: 2, of which 2 were waited for; matrix products, arithmetic and copies ran while one was open for 9% of the time, Pallas kernels for 0%

commit v1 on v0

v1 whole, which is shorter than its diff:
```python
import functools

import jax
import jax.numpy as jnp
from jax import lax
from jax.experimental import pallas as pl
from jax.experimental.pallas import tpu as pltpu
from jax.sharding import PartitionSpec as P

LANES = 128
COLS = 256
LOW = -4.0
VMEM_LIMIT = 48 * 1024 * 1024


def take_lanes(table, index):
    return jnp.take_along_axis(table, index, axis=1, mode="promise_in_bounds")


def pack_kernel(devices, capacity, codes_ref, routes_ref, out_ref):
    subspaces, in_rows = codes_ref.shape
    half_rows = capacity // 2
    targets = routes_ref[...]
    hot = lax.broadcasted_iota(jnp.int32, (devices, in_rows), 0) == targets
    hot32 = jnp.where(hot, 1.0, 0.0)
    earlier = (
        lax.broadcasted_iota(jnp.int32, (in_rows, in_rows), 0)
        < lax.broadcasted_iota(jnp.int32, (in_rows, in_rows), 1)
    )
    running = jnp.dot(
        hot32.astype(jnp.bfloat16),
        jnp.where(earlier, 1.0, 0.0).astype(jnp.bfloat16),
        preferred_element_type=jnp.float32,
    )
    position = jnp.sum(hot32 * running, axis=0, keepdims=True).astype(jnp.int32)
    second = position >= half_rows
    key = targets * half_rows + jnp.where(second, position - half_rows, position)
    out_rows = devices * half_rows
    row_ids = lax.broadcasted_iota(jnp.int32, (out_rows, in_rows), 0)
    values = (codes_ref[...] + 1).astype(jnp.bfloat16)
    halves = []
    for wanted in (jnp.where(second, -1, key), jnp.where(second, key, -1)):
        move = jnp.where(row_ids == wanted, 1.0, 0.0).astype(jnp.bfloat16)
        halves.append(
            lax.dot_general(
                move, values, (((1,), (1,)), ((), ())), preferred_element_type=jnp.float32
            )
        )
    out_ref[...] = jnp.concatenate(halves, axis=1).astype(jnp.bfloat16)


def unpack_codes(block, lo_ref, hi_ref, mark_ref, tile):
    turned = jnp.transpose(block.astype(jnp.float32)).astype(jnp.int32)
    subspaces = turned.shape[0] // 2
    for half in range(2):
        part = turned[half * subspaces : (half + 1) * subspaces]
        index = jnp.maximum(part - 1, 0)
        lo_ref[tile + half] = index & (LANES - 1)
        hi_ref[tile + half] = index // LANES
        mark_ref[tile + half] = jnp.where(part[0:8] > 0, 1.0, 0.0)


def decode_tile(lo_ref, hi_ref, tile, table_ref, norms_ref, store):
    subspaces = norms_ref.shape[0]
    sub_width = table_ref.shape[0] // subspaces
    lo_all = lo_ref[tile]
    hi_all = hi_ref[tile] > 0
    squares = jnp.where(
        hi_all,
        take_lanes(norms_ref[:, LANES:], lo_all),
        take_lanes(norms_ref[:, :LANES], lo_all),
    )
    scale = lax.rsqrt(jnp.sum(squares, axis=0, keepdims=True) + 1e-06)
    for sub in range(subspaces):
        lo = jnp.broadcast_to(lo_ref[tile, sub : sub + 1, :], (sub_width, LANES))
        hi = jnp.broadcast_to(hi_ref[tile, sub : sub + 1, :], (sub_width, LANES)) > 0
        rows = slice(sub * sub_width, (sub + 1) * sub_width)
        word = jnp.where(
            hi,
            take_lanes(table_ref[rows, LANES:], lo),
            take_lanes(table_ref[rows, :LANES], lo),
        )
        store(rows, (word * scale).astype(jnp.bfloat16))


def own_kernel(
    codes_ref, codebook_ref, centroids_ref, group_ref,
    left_ref, best_ref, table_ref, norms_ref,
    units_ref, lo_ref, hi_ref, mark_ref,
):
    slots, width = left_ref.shape
    subspaces = norms_ref.shape[0]
    tiles = slots // LANES
    words = codebook_ref.shape[0]
    pick = lax.broadcasted_iota(jnp.int32, (centroids_ref.shape[0], 1), 0) == group_ref[0, 0]
    centre = jnp.sum(
        jnp.where(pick, centroids_ref[...].astype(jnp.float32), 0.0), axis=0, keepdims=True
    )
    embeds = codebook_ref[...].astype(jnp.float32) + centre
    table = jnp.transpose(embeds)
    table_ref[...] = table
    norms_ref[...] = jnp.sum((table * table).reshape(subspaces, width // subspaces, words), axis=1)
    for group in range(tiles // 2):
        unpack_codes(
            codes_ref[group * LANES : (group + 1) * LANES, :], lo_ref, hi_ref, mark_ref, 2 * group
        )

    def one_tile(tile, _):
        start = pl.multiple_of(tile * LANES, LANES)

        def store(rows, value):
            units_ref[rows, pl.ds(start, LANES)] = value

        decode_tile(lo_ref, hi_ref, tile, table_ref, norms_ref, store)
        left_ref[pl.ds(start, LANES), :] = jnp.transpose(units_ref[:, pl.ds(start, LANES)])
        return 0

    lax.fori_loop(0, tiles, one_tile, 0)

    best_ref[...] = jnp.full(best_ref.shape, LOW, jnp.float32)
    row_ids = lax.broadcasted_iota(jnp.int32, (slots, LANES), 0)
    lane_ids = lax.broadcasted_iota(jnp.int32, (slots, LANES), 1)

    def score(step, _):
        start = pl.multiple_of(step * COLS, COLS)
        scores = jnp.dot(
            left_ref[...], units_ref[:, pl.ds(start, COLS)], preferred_element_type=jnp.float32
        )
        best = best_ref[...]
        for part in range(COLS // LANES):
            filled = mark_ref[step * (COLS // LANES) + part][0:1, :] > 0
            keep = filled & (row_ids != lane_ids + (start + part * LANES))
            best = jnp.maximum(
                best, jnp.where(keep, scores[:, part * LANES : (part + 1) * LANES], LOW)
            )
        best_ref[...] = best
        return 0

    lax.fori_loop(0, slots // COLS, score, 0)


def rest_kernel(
    capacity, codes_ref, others_ref, left_ref, start_ref, table_ref, norms_ref,
    out_ref,
    units_ref, lo_ref, hi_ref, mark_ref, best_ref,
):
    slots, width = left_ref.shape
    tiles = slots // LANES
    columns = units_ref.shape[1]
    best_ref[...] = start_ref[...]

    def unpack(group, _):
        start = pl.multiple_of(group * LANES, LANES)
        unpack_codes(others_ref[pl.ds(start, LANES), :], lo_ref, hi_ref, mark_ref, 2 * group)
        return 0

    lax.fori_loop(0, others_ref.shape[0] // LANES, unpack, 0)

    def one_tile(tile, _):
        start = pl.multiple_of(tile * LANES, LANES)

        def store(rows, value):
            units_ref[rows, pl.ds(start, LANES)] = value

        decode_tile(lo_ref, hi_ref, tile, table_ref, norms_ref, store)
        return 0

    lax.fori_loop(0, columns // LANES, one_tile, 0)

    def score(step, _):
        start = pl.multiple_of(step * COLS, COLS)
        scores = jnp.dot(
            left_ref[...], units_ref[:, pl.ds(start, COLS)], preferred_element_type=jnp.float32
        )
        best = best_ref[...]
        for part in range(COLS // LANES):
            filled = mark_ref[step * (COLS // LANES) + part][0:1, :] > 0
            best = jnp.maximum(
                best, jnp.where(filled, scores[:, part * LANES : (part + 1) * LANES], LOW)
            )
        best_ref[...] = best
        return 0

    lax.fori_loop(0, columns // COLS, score, 0)

    half_rows = capacity // 2
    maxima = []
    for group in range(tiles // 2):
        turned = jnp.transpose(codes_ref[group * LANES : (group + 1) * LANES, :].astype(jnp.float32))
        subspaces = turned.shape[0] // 2
        for half in range(2):
            tile = 2 * group + half
            best = jnp.max(
                jnp.transpose(best_ref[tile * LANES : (tile + 1) * LANES, :]),
                axis=0, keepdims=True,
            )
            filled = turned[half * subspaces : half * subspaces + 1] > 0
            maxima.append(jnp.where(filled, best, 0.0))
    spread = [
        jnp.concatenate([maxima[2 * (row // 2) + half] for row in range(tiles)], axis=0)
        for half in range(2)
    ]
    lane = lax.broadcasted_iota(jnp.int32, (tiles, LANES), 1)
    row = lax.broadcasted_iota(jnp.int32, (tiles, LANES), 0)
    source = (LANES // 2) * (row % 2) + half_rows * (lane // capacity) + lane % half_rows
    upper = (lane % capacity) >= half_rows
    out_ref[...] = jnp.where(
        upper, take_lanes(spread[1], source), take_lanes(spread[0], source)
    )


def on_device(codes, routes, codebook, centroids):
    groups = lax.axis_size("cluster")
    members = lax.axis_size("blk")
    devices = groups * members
    subspaces, in_rows = codes.shape[2:]
    capacity = 2 * in_rows // devices
    slots = devices * capacity
    tiles = slots // LANES
    words, width = codebook.shape
    bf16, f32, i32 = jnp.bfloat16, jnp.float32, jnp.int32
    params = pltpu.CompilerParams(vmem_limit_bytes=VMEM_LIMIT)

    packed = pl.pallas_call(
        functools.partial(pack_kernel, devices, capacity),
        out_shape=jax.ShapeDtypeStruct((in_rows, 2 * subspaces), bf16),
        compiler_params=params,
        name="pack_rows",
    )(codes[0, 0], routes.reshape(1, in_rows))
    own = lax.all_to_all(packed, ("cluster", "blk"), split_axis=0, concat_axis=0, tiled=True)
    others = [
        lax.ppermute(own, "blk", [(i, (i + shift) % members) for i in range(members)])
        for shift in range(1, members)
    ]
    group = lax.axis_index("cluster").astype(i32).reshape(1, 1)
    left, best, table, norms = pl.pallas_call(
        own_kernel,
        out_shape=(
            jax.ShapeDtypeStruct((slots, width), bf16),
            jax.ShapeDtypeStruct((slots, LANES), f32),
            jax.ShapeDtypeStruct((width, words), f32),
            jax.ShapeDtypeStruct((subspaces, words), f32),
        ),
        in_specs=[pl.BlockSpec(memory_space=pltpu.VMEM)] * 3
        + [pl.BlockSpec(memory_space=pltpu.SMEM)],
        scratch_shapes=[
            pltpu.VMEM((width, slots), bf16),
            pltpu.VMEM((tiles, subspaces, LANES), i32),
            pltpu.VMEM((tiles, subspaces, LANES), i32),
            pltpu.VMEM((tiles, 8, LANES), f32),
        ],
        compiler_params=params,
        cost_estimate=pl.CostEstimate(
            flops=2 * slots * slots * width, bytes_accessed=8 * slots * width, transcendentals=0
        ),
        name="own_rows",
    )(own, codebook, centroids, group)
    columns = (members - 1) * slots
    nearest = pl.pallas_call(
        functools.partial(rest_kernel, capacity),
        out_shape=jax.ShapeDtypeStruct((tiles, LANES), f32),
        scratch_shapes=[
            pltpu.VMEM((width, columns), bf16),
            pltpu.VMEM((columns // LANES, subspaces, LANES), i32),
            pltpu.VMEM((columns // LANES, subspaces, LANES), i32),
            pltpu.VMEM((columns // LANES, 8, LANES), f32),
            pltpu.VMEM((slots, LANES), f32),
        ],
        compiler_params=params,
        cost_estimate=pl.CostEstimate(
            flops=2 * slots * columns * width, bytes_accessed=8 * slots * width, transcendentals=0
        ),
        name="rest_rows",
    )(own, jnp.concatenate(others, axis=0), left, best, table, norms)
    return nearest.reshape(1, 1, slots)


def solution(mesh):
    in_specs = (P("cluster", "blk", None, None), P("cluster", "blk", None, None), P(), P())
    out_specs = P("cluster", "blk", None)
    return jax.shard_map(
        on_device, mesh=mesh, in_specs=in_specs, out_specs=out_specs, check_vma=False
    )
```

time: 282 us -> 58.1 us (0.21)
  waiting for transfers between devices: 107 us -> 8.9 us
  blocking collectives: 66.8 us -> 0 us
  local copies, waits for them, and re-layouts: 62.4 us -> 3.34 us
  Pallas kernels: 0 us -> 35.7 us
  matrix products: 22.4 us -> 0 us
  between operations: 13.5 us -> 0.04 us
  starting transfers between devices: 4.47 us -> 9.7 us
  other arithmetic: 5.13 us -> 0.03 us
    all_gather x1 -> x0, waiting for transfers between devices: 99.3 us -> none  [on_device(): rows_in = lax.all_gather(my_rows, 'blk', axis=0, tiled=True)]
    scatter x2 -> x0, local copies, waits for them, and re-layouts: 58 us -> none  [the longest x1 32.8 us: on_device(): jnp.zeros((devices, capacity, width), jnp.bfloat16).at[targets, position]]
    all_to_all x1 -> x0, blocking collectives: 54.8 us -> none  [on_device(): lax.all_to_all(outgoing, ('cluster', 'blk'), split_axis=0, concat_axis=0,...]
    pallas_call x0 -> x3, Pallas kernels: none -> 35.7 us  [the longest x1 25.5 us: on_device(): pl.pallas_call(functools.partial(rest_kernel, capacity), out_shape=jax.Sh...]
    dot_general x3 -> x0, matrix products: 22.4 us -> none  [the longest x1 12.4 us: tile_scores(): lax.dot_general(left_rows, right_rows, (((1,), (1,)), ((), ())), preferre...]
    all_gather x1 -> x0, blocking collectives: 12 us -> none  [on_device(): marks_in = lax.all_gather(my_marks, 'blk', axis=0, tiled=True)]
    all_to_all x1, starting transfers between devices: 4.46 us -> 7.3 us  [on_device(): lax.all_to_all(packed, ('cluster', 'blk'), split_axis=0, concat_axis=0, t...]
  transfers between devices with their start and end apart: 2 -> 4, of which waited for: 2 -> 2; matrix products, arithmetic and copies ran while one was open for 9% -> 0% of each run, Pallas kernels for 0% -> 15%
where the time goes in v1:
time: 58.1 us; the launch traced here: 57.8 us
  Pallas kernels  35.7 us (61%)
  starting transfers between devices  9.7 us (17%)
  waiting for transfers between devices  8.9 us (15%)
  local copies, waits for them, and re-layouts  3.34 us (6%)
    pallas_call x1, Pallas kernels, on_device(): pl.pallas_call(functools.partial(rest_kernel, capacity), out_shape=jax.Sh...  25.5 us
    pallas_call x1, Pallas kernels, on_device(): pl.pallas_call(own_kernel, out_shape=(jax.ShapeDtypeStruct((slots, width)...  8.89 us
    all_to_all x1, waiting for transfers between devices, on_device(): lax.all_to_all(packed, ('cluster', 'blk'), split_axis=0, concat_axis=0, t...  8.4 us
    all_to_all x1, starting transfers between devices, on_device(): lax.all_to_all(packed, ('cluster', 'blk'), split_axis=0, concat_axis=0, t...  7.3 us
    unnamed x8, local copies, waits for them, and re-layouts  3.34 us
    ppermute x3, starting transfers between devices, on_device(): lax.ppermute(own, 'blk', [(i, (i + shift) % members) for i in range(membe...  2.4 us
    pallas_call x1, Pallas kernels, on_device(): pl.pallas_call(functools.partial(pack_kernel, devices, capacity), out_sha...  1.35 us
  transfers between devices with their start and end apart: 4, of which 2 were waited for; matrix products, arithmetic and copies ran while one was open for 0% of the time, Pallas kernels for 15%

profile of v1, /device:TPU:0, one launch (start us, length us, event | category | flops | bytes accessed | tf_op | source)
XLA Modules:
  0.0 57.8 jit_solution(10624873676021635265)
XLA Ops:
  0.0 0.0 copy-start
  0.0 0.9 %copy-done = s32[1,1,64,512]{3,2,1,0:T(8,128)S(1)} copy-done((s32[1,1,64,512]{3,2,1,0:T(8,128)S(1)}, s32[1,1,64,512]{3,2,1,0:T(8,128)}, u32[]{:S(2)}) %copy-start) | copy-done | bytes 131096
  0.9 0.0 copy-start.1
  0.9 0.7 %copy-done.1 = s32[1,1,512,1]{2,3,1,0:T(1,128)S(1)} copy-done((s32[1,1,512,1]{2,3,1,0:T(1,128)S(1)}, s32[1,1,512,1]{2,3,1,0:T(1,128)}, u32[]{:S(2)}) %copy-start.1) | copy-done | bytes 2072
  1.6 1.3 %pack_rows.1 = bf16[512,128]{1,0:T(8,128)(2,1)} custom-call(s32[64,512]{1,0:T(8,128)S(1)} %bitcast.6, s32[1,512]{1,0:T(1,128)S(1)} %bitcast.12), custom_call_target="tpu_custom_call" | custom-call | tf_op jit(solution)/shard_map/pack_rows/pallas_call | solution.py:224
  2.9 7.3 %all-to-all-start = ((bf16[32,16,128]{2,1,0:T(8,128)(2,1)}), bf16[32,16,128]{2,1,0:T(8,128)(2,1)S(1)}, u32[]{:S(2)}, u32[]{:S(2)}) async-start(bf16[32,16,128]{2,1,0:T(8,128)(2,1)} %bitcast.2), calls=%async_computation | async-start | bytes 262144 | tf_op jit(solution)/shard_map/all_to_all | solution.py:230
  10.2 8.4 %all-to-all-done = bf16[32,16,128]{2,1,0:T(8,128)(2,1)S(1)} async-done(((bf16[32,16,128]{2,1,0:T(8,128)(2,1)}), bf16[32,16,128]{2,1,0:T(8,128)(2,1)S(1)}, u32[]{:S(2)}, u32[]{:S(2)}) %all-to-all-start) | async-done | bytes 131104 | tf_op jit(solution)/shard_map/all_to_all | solution.py:230
  18.6 1.2 %collective-permute-start.2 = (bf16[512,128]{1,0:T(8,128)(2,1)S(1)}, bf16[512,128]{1,0:T(8,128)(2,1)S(1)}, u32[]{:S(2)}, u32[]{:S(2)}) collective-permute-start(bf16[512,128]{1,0:T(8,128)(2,1)S(1)} %bitcast.7), channel_id=1, source_target_pairs={{0,3},{1,0},{2,1},{3,2},{4,7},{5,4},{6,5},{7,6},{8,11},{9,8},{10,9... | collective-permute-start | bytes 393224 | tf_op jit(solution)/shard_map/ppermute | solution.py:232
  19.8 0.0 collective-permute-start.1
  19.9 1.2 %collective-permute-start = (bf16[512,128]{1,0:T(8,128)(2,1)S(1)}, bf16[512,128]{1,0:T(8,128)(2,1)S(1)}, u32[]{:S(2)}, u32[]{:S(2)}) collective-permute-start(bf16[512,128]{1,0:T(8,128)(2,1)S(1)} %bitcast.9), channel_id=1, source_target_pairs={{0,1},{1,2},{2,3},{3,0},{4,5},{5,6},{6,7},{7,4},{8,9},{9,10},{10,1... | collective-permute-start | bytes 393224 | tf_op jit(solution)/shard_map/ppermute | solution.py:232
  21.0 0.0 copy-start.2
  21.0 1.0 %copy-done.2 = bf16[256,1024]{1,0:T(8,128)(2,1)S(1)} copy-done((bf16[256,1024]{1,0:T(8,128)(2,1)S(1)}, bf16[256,1024]{1,0:T(8,128)(2,1)}, u32[]{:S(2)}) %copy-start.2) | copy-done | bytes 524312
  22.1 0.0 copy-start.3
  22.1 0.7 %copy-done.3 = bf16[8,1024]{1,0:T(8,128)(2,1)S(1)} copy-done((bf16[8,1024]{1,0:T(8,128)(2,1)S(1)}, bf16[8,1024]{1,0:T(8,128)(2,1)}, u32[]{:S(2)}) %copy-start.3) | copy-done | bytes 16408
  22.8 8.9 %own_rows.1 = (bf16[1024,1024]{1,0:T(8,128)(2,1)S(1)}, f32[1024,128]{1,0:T(8,128)S(1)}, f32[1024,256]{1,0:T(8,128)S(1)}, f32[64,256]{1,0:T(8,128)S(1)}) custom-call(bf16[512,128]{1,0:T(8,128)(2,1)S(1)} %bitcast.10, bf16[256,1024]{1,0:T(8,128)(2,1)S(1)} %copy-done.2, bf16[8,1024]{1,0:T(8,128)(2,1)S(1)} %copy-done.3, s32[1,1]{1,0:T(1,128)} %bitcast.4.group_ref), custom_call_target="tpu_custom_call" | custom-call | flops 2147483648 | bytes 8388608 | tf_op jit(solution)/shard_map/own_rows/pallas_call | solution.py:236
  31.7 0.0 collective-permute-done.2
  31.7 0.5 collective-permute-done.1
  32.2 0.0 collective-permute-done
  32.2 25.5 %rest_rows.1 = f32[8,128]{1,0:T(8,128)} custom-call(bf16[512,128]{1,0:T(8,128)(2,1)S(1)} %bitcast.11, bf16[1536,128]{1,0:T(8,128)(2,1)S(1)} %pad_maximum_fusion.others_ref, bf16[1024,1024]{1,0:T(8,128)(2,1)S(1)} %get-tuple-element.9.left_ref, f32[1024,128]{1,0:T(8,128)S(1)} %get-tuple-element.10.start_ref, f32[1024,256]{1,0:T(8,128)S(1)} %get-tuple-element.11.table_ref, ...), custom_call_target="tpu_custom_call" | custom-call | flops 6442450944 | bytes 8388608 | tf_op jit(solution)/shard_map/rest_rows/pallas_call | solution.py:259
  (1 shorter events, 0.0 us)
Async XLA Ops:
  0.0 0.9 %copy-start = (s32[1,1,64,512]{3,2,1,0:T(8,128)S(1)}, s32[1,1,64,512]{3,2,1,0:T(8,128)}, u32[]{:S(2)}) copy-start(s32[1,1,64,512]{3,2,1,0:T(8,128)} %param.4) | copy-start | bytes 393220
  0.9 0.7 %copy-start.1 = (s32[1,1,512,1]{2,3,1,0:T(1,128)S(1)}, s32[1,1,512,1]{2,3,1,0:T(1,128)}, u32[]{:S(2)}) copy-start(s32[1,1,512,1]{2,3,1,0:T(1,128)} %param.5) | copy-start | bytes 6148
  2.9 15.7 %all-to-all-start = ((bf16[32,16,128]{2,1,0:T(8,128)(2,1)}), bf16[32,16,128]{2,1,0:T(8,128)(2,1)S(1)}, u32[]{:S(2)}, u32[]{:S(2)}) async-start(bf16[32,16,128]{2,1,0:T(8,128)(2,1)} %bitcast.2), calls=%async_computation | async-start | bytes 262144 | tf_op jit(solution)/shard_map/all_to_all | solution.py:230
  18.6 13.1 %collective-permute-start.2 = (bf16[512,128]{1,0:T(8,128)(2,1)S(1)}, bf16[512,128]{1,0:T(8,128)(2,1)S(1)}, u32[]{:S(2)}, u32[]{:S(2)}) collective-permute-start(bf16[512,128]{1,0:T(8,128)(2,1)S(1)} %bitcast.7), channel_id=1, source_target_pairs={{0,3},{1,0},{2,1},{3,2},{4,7},{5,4},{6,5},{7,6},{8,11},{9,8},{10,9... | collective-permute-start | bytes 393224 | tf_op jit(solution)/shard_map/ppermute | solution.py:232
  19.8 12.4 %collective-permute-start.1 = (bf16[512,128]{1,0:T(8,128)(2,1)S(1)}, bf16[512,128]{1,0:T(8,128)(2,1)S(1)}, u32[]{:S(2)}, u32[]{:S(2)}) collective-permute-start(bf16[512,128]{1,0:T(8,128)(2,1)S(1)} %bitcast.8), channel_id=1, source_target_pairs={{0,2},{1,3},{2,0},{3,1},{4,6},{5,7},{6,4},{7,5},{8,10},{9,11},{10,... | collective-permute-start | bytes 393224 | tf_op jit(solution)/shard_map/ppermute | solution.py:232
  19.9 12.4 %collective-permute-start = (bf16[512,128]{1,0:T(8,128)(2,1)S(1)}, bf16[512,128]{1,0:T(8,128)(2,1)S(1)}, u32[]{:S(2)}, u32[]{:S(2)}) collective-permute-start(bf16[512,128]{1,0:T(8,128)(2,1)S(1)} %bitcast.9), channel_id=1, source_target_pairs={{0,1},{1,2},{2,3},{3,0},{4,5},{5,6},{6,7},{7,4},{8,9},{9,10},{10,1... | collective-permute-start | bytes 393224 | tf_op jit(solution)/shard_map/ppermute | solution.py:232
  21.0 1.0 %copy-start.2 = (bf16[256,1024]{1,0:T(8,128)(2,1)S(1)}, bf16[256,1024]{1,0:T(8,128)(2,1)}, u32[]{:S(2)}) copy-start(bf16[256,1024]{1,0:T(8,128)(2,1)} %codebook_ref.1) | copy-start | bytes 1572868
  22.1 0.7 %copy-start.3 = (bf16[8,1024]{1,0:T(8,128)(2,1)S(1)}, bf16[8,1024]{1,0:T(8,128)(2,1)}, u32[]{:S(2)}) copy-start(bf16[8,1024]{1,0:T(8,128)(2,1)} %centroids_ref.1) | copy-start | bytes 49156

commit v2 on v1

v2 whole, which is shorter than its diff:
```python
import functools

import jax
import jax.numpy as jnp
from jax import lax
from jax.experimental import pallas as pl
from jax.experimental.pallas import tpu as pltpu
from jax.sharding import PartitionSpec as P

LANES = 128
COLS = 256
LOW = -4.0
VMEM_LIMIT = 48 * 1024 * 1024
PARAMS = pltpu.CompilerParams(vmem_limit_bytes=VMEM_LIMIT)


def take_lanes(table, index):
    return jnp.take_along_axis(table, index, axis=1, mode="promise_in_bounds")


def pack_kernel(devices, capacity, codes_ref, routes_ref, out_ref):
    subspaces, in_rows = codes_ref.shape
    half_rows = capacity // 2
    targets = routes_ref[...]
    hot = lax.broadcasted_iota(jnp.int32, (devices, in_rows), 0) == targets
    hot32 = jnp.where(hot, 1.0, 0.0)
    earlier = (
        lax.broadcasted_iota(jnp.int32, (in_rows, in_rows), 0)
        < lax.broadcasted_iota(jnp.int32, (in_rows, in_rows), 1)
    )
    running = jnp.dot(
        hot32.astype(jnp.bfloat16),
        jnp.where(earlier, 1.0, 0.0).astype(jnp.bfloat16),
        preferred_element_type=jnp.float32,
    )
    position = jnp.sum(hot32 * running, axis=0, keepdims=True).astype(jnp.int32)
    second = position >= half_rows
    key = targets * half_rows + jnp.where(second, position - half_rows, position)
    out_rows = devices * half_rows
    row_ids = lax.broadcasted_iota(jnp.int32, (out_rows, in_rows), 0)
    values = (codes_ref[...] + 1).astype(jnp.bfloat16)
    halves = []
    for wanted in (jnp.where(second, -1, key), jnp.where(second, key, -1)):
        move = jnp.where(row_ids == wanted, 1.0, 0.0).astype(jnp.bfloat16)
        halves.append(
            lax.dot_general(
                move, values, (((1,), (1,)), ((), ())), preferred_element_type=jnp.float32
            )
        )
    out_ref[...] = jnp.concatenate(halves, axis=1).astype(jnp.bfloat16)


def table_kernel(group_ref, codebook_ref, centroids_ref, table_ref, norms_ref):
    words, width = codebook_ref.shape
    subspaces = norms_ref.shape[0]
    pick = lax.broadcasted_iota(jnp.int32, (centroids_ref.shape[0], 1), 0) == group_ref[0, 0]
    centre = jnp.sum(
        jnp.where(pick, centroids_ref[...].astype(jnp.float32), 0.0), axis=0, keepdims=True
    )
    table = jnp.transpose(codebook_ref[...].astype(jnp.float32) + centre)
    table_ref[...] = table
    norms_ref[...] = jnp.sum((table * table).reshape(subspaces, width // subspaces, words), axis=1)


def owner_block(codes_ref, owner, owners):
    parts = [
        codes_ref[pl.ds(pl.multiple_of((part * owners + owner) * 16, 16), 16), :]
        for part in range(LANES // 16)
    ]
    return jnp.concatenate(parts, axis=0)


def unpack_codes(block, lo_ref, hi_ref, mark_ref, group):
    turned = jnp.transpose(block.astype(jnp.float32)).astype(jnp.int32)
    subspaces = turned.shape[0] // 2
    for half in range(2):
        part = turned[half * subspaces : (half + 1) * subspaces]
        index = jnp.maximum(part - 1, 0)
        lo_ref[2 * group + half] = index & (LANES - 1)
        hi_ref[2 * group + half] = index // LANES
        mark_ref[2 * group + half] = jnp.where(part[0:8] > 0, 1.0, 0.0)


def tile_scale(lo, hi, norms_ref):
    squares = jnp.where(
        hi > 0,
        take_lanes(norms_ref[:, LANES:], lo),
        take_lanes(norms_ref[:, :LANES], lo),
    )
    return lax.rsqrt(jnp.sum(squares, axis=0, keepdims=True) + 1e-06)


def stage_tile(lo_ref, hi_ref, tile, now_ref, half, norms_ref):
    lo, hi = lo_ref[tile], hi_ref[tile]
    now_ref[half, 0] = lo
    now_ref[half, 1] = hi
    return tile_scale(lo, hi, norms_ref)


def decode_tile(lo_ref, hi_ref, tile, now_ref, table_ref, norms_ref, units_ref, start):
    subspaces = norms_ref.shape[0]
    sub_width = table_ref.shape[0] // subspaces
    start = pl.multiple_of(start, LANES)
    scale = stage_tile(lo_ref, hi_ref, tile, now_ref, 0, norms_ref)
    for sub in range(subspaces):
        lo = jnp.broadcast_to(now_ref[0, 0, sub : sub + 1, :], (sub_width, LANES))
        hi = jnp.broadcast_to(now_ref[0, 1, sub : sub + 1, :], (sub_width, LANES)) > 0
        rows = slice(sub * sub_width, (sub + 1) * sub_width)
        word = jnp.where(
            hi,
            take_lanes(table_ref[rows, LANES:], lo),
            take_lanes(table_ref[rows, :LANES], lo),
        )
        units_ref[rows, pl.ds(start, LANES)] = (word * scale).astype(jnp.bfloat16)


def near_kernel(
    place_ref, codes_ref, table_ref, norms_ref, units_ref, mark_ref,
    lo_ref, hi_ref, now_ref,
):
    owners = units_ref.shape[1] // COLS
    for turn in range(owners):
        owner = lax.rem(place_ref[0, 0] + turn, owners)
        unpack_codes(owner_block(codes_ref, owner, owners), lo_ref, hi_ref, mark_ref, turn)

    def one_tile(tile, _):
        decode_tile(lo_ref, hi_ref, tile, now_ref, table_ref, norms_ref, units_ref, tile * LANES)
        return 0

    lax.fori_loop(0, 2 * owners, one_tile, 0)


def last_kernel(sizes, place_ref, *refs):
    capacity, clusters, members = sizes
    more = len(refs) - 12
    codes_refs = refs[:more]
    (
        near_ref, near_mark_ref, table_ref, norms_ref, out_ref,
        left_ref, units_ref, best_ref, lo_ref, hi_ref, mark_ref, now_ref,
    ) = refs[more:]
    slots, width = left_ref.shape
    groups = more + 1
    owners = units_ref.shape[1] // slots
    place = place_ref[0, 0]

    for turn in range(owners):
        owner = lax.rem(place + turn, owners)
        for which in range(more):
            unpack_codes(
                owner_block(codes_refs[which], owner, owners),
                lo_ref, hi_ref, mark_ref, turn * groups + which + 1,
            )
        for half in range(2):
            mark_ref[2 * turn * groups + half] = near_mark_ref[2 * turn + half]
        units_ref[:, turn * slots : turn * slots + COLS] = near_ref[
            :, turn * COLS : (turn + 1) * COLS
        ]

    per_turn = slots // LANES
    for turn in range(owners):

        def one_tile(tile, _):
            tile = tile + turn * per_turn
            decode_tile(
                lo_ref, hi_ref, tile, now_ref, table_ref, norms_ref, units_ref, tile * LANES
            )
            return 0

        lax.fori_loop(2, per_turn, one_tile, 0)

    def turn_left(tile, _):
        start = pl.multiple_of(tile * LANES, LANES)
        left_ref[pl.ds(start, LANES), :] = jnp.transpose(units_ref[:, pl.ds(start, LANES)])
        return 0

    lax.fori_loop(0, per_turn, turn_left, 0)
    best_ref[...] = jnp.full(best_ref.shape, LOW, jnp.float32)

    def score(step, _):
        start = pl.multiple_of(step * COLS, COLS)
        scores = jnp.dot(
            left_ref[...], units_ref[:, pl.ds(start, COLS)], preferred_element_type=jnp.float32
        )
        best = best_ref[...]
        row_ids = lax.broadcasted_iota(jnp.int32, (slots, LANES), 0)
        lane_ids = lax.broadcasted_iota(jnp.int32, (slots, LANES), 1)
        for part in range(COLS // LANES):
            filled = mark_ref[step * (COLS // LANES) + part][0:1, :] > 0
            keep = filled & (row_ids != lane_ids + (start + part * LANES))
            best = jnp.maximum(
                best, jnp.where(keep, scores[:, part * LANES : (part + 1) * LANES], LOW)
            )
        best_ref[...] = best
        return 0

    lax.fori_loop(0, owners * groups, score, 0)

    half_rows = capacity // 2
    tiles = slots // LANES
    lane = lax.broadcasted_iota(jnp.int32, (tiles, LANES), 1)
    slot = lax.broadcasted_iota(jnp.int32, (tiles, LANES), 0) * LANES + lane
    source, within = slot // capacity, slot % capacity
    turn = lax.rem(place - source % members + members, members)
    own_row = (turn * clusters + source // members) * half_rows + within % half_rows
    tile_of = 2 * (own_row // LANES) + within // half_rows
    result = jnp.zeros((tiles, LANES), jnp.float32)
    for tile in range(tiles):
        best = jnp.max(
            jnp.transpose(best_ref[tile * LANES : (tile + 1) * LANES, :]), axis=0, keepdims=True
        )
        mark = mark_ref[tile]
        best = jnp.where(mark[0:1, :] > 0, best, 0.0)
        result = jnp.where(
            tile_of == tile,
            take_lanes(jnp.broadcast_to(best, (tiles, LANES)), own_row % LANES),
            result,
        )
    out_ref[...] = result


def on_device(codes, routes, codebook, centroids):
    clusters = lax.axis_size("cluster")
    members = lax.axis_size("blk")
    devices = clusters * members
    subspaces, in_rows = codes.shape[2:]
    capacity = 2 * in_rows // devices
    half_rows = capacity // 2
    slots = devices * capacity
    tiles = slots // LANES
    groups = slots // COLS
    words, width = codebook.shape
    bf16, f32, i32 = jnp.bfloat16, jnp.float32, jnp.int32
    smem = pl.BlockSpec(memory_space=pltpu.SMEM)
    vmem = pl.BlockSpec(memory_space=pltpu.VMEM)

    packed = pl.pallas_call(
        functools.partial(pack_kernel, devices, capacity),
        out_shape=jax.ShapeDtypeStruct((in_rows, 2 * subspaces), bf16),
        compiler_params=PARAMS,
        name="pack_rows",
    )(codes[0, 0], routes.reshape(1, in_rows))
    here = lax.all_to_all(packed, "cluster", split_axis=0, concat_axis=0, tiled=True)
    there = [
        lax.ppermute(here, "blk", [(i, (i + shift) % members) for i in range(members)])
        for shift in range(1, members)
    ]
    if half_rows == 16 and clusters * half_rows == LANES:
        blocks = [here, *there]
    else:
        every = jnp.stack([here, *there]).reshape(members, clusters, members, half_rows, LANES)
        every = every.transpose(2, 0, 1, 3, 4).reshape(members, groups, LANES // 16, 16, LANES)
        every = every.transpose(1, 2, 0, 3, 4).reshape(groups, members * LANES, LANES)
        blocks = list(every)

    place = lax.axis_index("blk").astype(i32).reshape(1, 1)
    group = lax.axis_index("cluster").astype(i32).reshape(1, 1)
    table, norms = pl.pallas_call(
        table_kernel,
        out_shape=(
            jax.ShapeDtypeStruct((width, words), f32),
            jax.ShapeDtypeStruct((subspaces, words), f32),
        ),
        in_specs=[smem, vmem, vmem],
        compiler_params=PARAMS,
        cost_estimate=pl.CostEstimate(
            flops=4 * words * width, bytes_accessed=6 * words * width, transcendentals=0
        ),
        name="word_table",
    )(group, codebook, centroids)
    near, near_mark = pl.pallas_call(
        near_kernel,
        out_shape=(
            jax.ShapeDtypeStruct((width, members * COLS), bf16),
            jax.ShapeDtypeStruct((2 * members, 8, LANES), f32),
        ),
        in_specs=[smem, vmem, vmem, vmem],
        scratch_shapes=[
            pltpu.VMEM((2 * members, subspaces, LANES), i32),
            pltpu.VMEM((2 * members, subspaces, LANES), i32),
            pltpu.VMEM((1, 2, subspaces, LANES), i32),
        ],
        compiler_params=PARAMS,
        cost_estimate=pl.CostEstimate(
            flops=4 * members * COLS * width,
            bytes_accessed=4 * members * COLS * width,
            transcendentals=0,
        ),
        name="near_rows",
    )(place, blocks[0], table, norms)
    more = groups - 1
    nearest = pl.pallas_call(
        functools.partial(last_kernel, (capacity, clusters, members)),
        out_shape=jax.ShapeDtypeStruct((tiles, LANES), f32),
        in_specs=[smem] + [vmem] * (more + 4),
        scratch_shapes=[
            pltpu.VMEM((slots, width), bf16),
            pltpu.VMEM((width, members * slots), bf16),
            pltpu.VMEM((slots, LANES), f32),
            pltpu.VMEM((2 * members * groups, subspaces, LANES), i32),
            pltpu.VMEM((2 * members * groups, subspaces, LANES), i32),
            pltpu.VMEM((2 * members * groups, 8, LANES), f32),
            pltpu.VMEM((1, 2, subspaces, LANES), i32),
        ],
        compiler_params=PARAMS,
        cost_estimate=pl.CostEstimate(
            flops=2 * slots * members * slots * width,
            bytes_accessed=8 * slots * width,
            transcendentals=0,
        ),
        name="all_rows",
    )(place, *blocks[1:], near, near_mark, table, norms)
    return nearest.reshape(1, 1, slots)


def solution(mesh):
    in_specs = (P("cluster", "blk", None, None), P("cluster", "blk", None, None), P(), P())
    out_specs = P("cluster", "blk", None)
    return jax.shard_map(
        on_device, mesh=mesh, in_specs=in_specs, out_specs=out_specs, check_vma=False
    )
```

time: 58.1 us -> 56.3 us (0.969)
  blocking collectives: 0 us -> 10.5 us
  waiting for transfers between devices: 8.9 us -> 2.7 us
  starting transfers between devices: 9.7 us -> 4.61 us
  Pallas kernels: 35.7 us -> 34.8 us
    all_to_all x0 -> x1, blocking collectives: none -> 10.5 us  [on_device(): lax.all_to_all(packed, 'cluster', split_axis=0, concat_axis=0, tiled=True)]
    all_to_all x1 -> x0, waiting for transfers between devices: 8.4 us -> none  [on_device(): lax.all_to_all(packed, ('cluster', 'blk'), split_axis=0, concat_axis=0, t...]
    all_to_all x1 -> x0, starting transfers between devices: 7.3 us -> none  [on_device(): lax.all_to_all(packed, ('cluster', 'blk'), split_axis=0, concat_axis=0, t...]
    ppermute x3, starting transfers between devices: 2.4 us -> 4.61 us  [on_device(): lax.ppermute(here, 'blk', [(i, (i + shift) % members) for i in range(memb...]
    ppermute x3, waiting for transfers between devices: 0.5 us -> 2.7 us  [on_device(): lax.ppermute(here, 'blk', [(i, (i + shift) % members) for i in range(memb...]
    pallas_call x1, Pallas kernels: 1.35 us -> 0.7 us  [on_device(): pl.pallas_call(functools.partial(pack_kernel, devices, capacity), out_sha...]
    pallas_call x2 -> x3, Pallas kernels: 34.4 us -> 34.1 us  [the longest x1 28.7 us: on_device(): pl.pallas_call(functools.partial(last_kernel, (capacity, clusters, member...]
  transfers between devices with their start and end apart: 4 -> 3, of which waited for: 2 -> 1; matrix products, arithmetic and copies ran while one was open for 0% -> 0% of each run, Pallas kernels for 15% -> 10%
where the time goes in v2:
time: 56.3 us; the launch traced here: 56 us
  Pallas kernels  34.8 us (62%)
  blocking collectives  10.5 us (19%)
  starting transfers between devices  4.61 us (8%)
  local copies, waits for them, and re-layouts  3.34 us (6%)
  waiting for transfers between devices  2.7 us (5%)
    pallas_call x1, Pallas kernels, on_device(): pl.pallas_call(functools.partial(last_kernel, (capacity, clusters, member...  28.7 us
    all_to_all x1, blocking collectives, on_device(): lax.all_to_all(packed, 'cluster', split_axis=0, concat_axis=0, tiled=True)  10.5 us
    pallas_call x1, Pallas kernels, on_device(): pl.pallas_call(near_kernel, out_shape=(jax.ShapeDtypeStruct((width, membe...  5.06 us
    ppermute x3, starting transfers between devices, on_device(): lax.ppermute(here, 'blk', [(i, (i + shift) % members) for i in range(memb...  4.61 us
    unnamed x8, local copies, waits for them, and re-layouts  3.34 us
    ppermute x3, waiting for transfers between devices, on_device(): lax.ppermute(here, 'blk', [(i, (i + shift) % members) for i in range(memb...  2.7 us
  transfers between devices with their start and end apart: 3, of which 1 were waited for; matrix products, arithmetic and copies ran while one was open for 0% of the time, Pallas kernels for 10%

profile of v2, /device:TPU:0, one launch (start us, length us, event | category | flops | bytes accessed | tf_op | source)
XLA Modules:
  0.0 56.0 jit_solution(914523108237208837)
XLA Ops:
  0.0 0.0 copy-start.1
  0.0 0.9 %copy-done.1 = s32[1,1,64,512]{3,2,1,0:T(8,128)S(1)} copy-done((s32[1,1,64,512]{3,2,1,0:T(8,128)S(1)}, s32[1,1,64,512]{3,2,1,0:T(8,128)}, u32[]{:S(2)}) %copy-start.1) | copy-done | bytes 131096
  0.9 0.0 copy-start.3
  0.9 0.7 %copy-done.3 = s32[1,1,512,1]{2,3,1,0:T(1,128)S(1)} copy-done((s32[1,1,512,1]{2,3,1,0:T(1,128)S(1)}, s32[1,1,512,1]{2,3,1,0:T(1,128)}, u32[]{:S(2)}) %copy-start.3) | copy-done | bytes 2072
  1.6 0.7 %pack_rows.1 = bf16[512,128]{1,0:T(8,128)(2,1)S(1)} custom-call(s32[64,512]{1,0:T(8,128)S(1)} %bitcast.12, s32[1,512]{1,0:T(1,128)S(1)} %bitcast.13), custom_call_target="tpu_custom_call" | custom-call | tf_op jit(solution)/shard_map/pack_rows/pallas_call | solution.py:236
  2.3 10.5 %all_to_all.11 = bf16[8,64,128]{2,1,0:T(8,128)(2,1)S(1)} all-to-all(bf16[8,64,128]{2,1,0:T(8,128)(2,1)S(1)} %bitcast.11), channel_id=1, replica_groups=mesh['cluster'=8,'blk'=4] {'cluster'}, dimensions={0} | all-to-all | bytes 262144 | tf_op jit(solution)/shard_map/all_to_all | solution.py:242
  12.8 3.6 %collective-permute-start.2 = (bf16[512,128]{1,0:T(8,128)(2,1)S(1)}, bf16[512,128]{1,0:T(8,128)(2,1)S(1)}, u32[]{:S(2)}, u32[]{:S(2)}) collective-permute-start(bf16[512,128]{1,0:T(8,128)(2,1)S(1)} %bitcast.7), channel_id=1, source_target_pairs={{0,3},{1,0},{2,1},{3,2},{4,7},{5,4},{6,5},{7,6},{8,11},{9,8},{10,9... | collective-permute-start | bytes 393224 | tf_op jit(solution)/shard_map/ppermute | solution.py:244
  16.4 0.0 collective-permute-start.1
  16.4 1.0 %collective-permute-start = (bf16[512,128]{1,0:T(8,128)(2,1)S(1)}, bf16[512,128]{1,0:T(8,128)(2,1)S(1)}, u32[]{:S(2)}, u32[]{:S(2)}) collective-permute-start(bf16[512,128]{1,0:T(8,128)(2,1)S(1)} %bitcast.9), channel_id=1, source_target_pairs={{0,1},{1,2},{2,3},{3,0},{4,5},{5,6},{6,7},{7,4},{8,9},{9,10},{10,1... | collective-permute-start | bytes 393224 | tf_op jit(solution)/shard_map/ppermute | solution.py:244
  17.4 0.0 copy-start
  17.4 1.0 %copy-done = bf16[256,1024]{1,0:T(8,128)(2,1)S(1)} copy-done((bf16[256,1024]{1,0:T(8,128)(2,1)S(1)}, bf16[256,1024]{1,0:T(8,128)(2,1)}, u32[]{:S(2)}) %copy-start) | copy-done | bytes 524312
  18.4 0.0 copy-start.2
  18.5 0.7 %copy-done.2 = bf16[8,1024]{1,0:T(8,128)(2,1)S(1)} copy-done((bf16[8,1024]{1,0:T(8,128)(2,1)S(1)}, bf16[8,1024]{1,0:T(8,128)(2,1)}, u32[]{:S(2)}) %copy-start.2) | copy-done | bytes 16408
  19.2 0.4 word_table.1
  19.5 5.1 %near_rows.1 = (bf16[1024,1024]{1,0:T(8,128)(2,1)S(1)}, f32[8,8,128]{2,1,0:T(8,128)S(1)}) custom-call(s32[1,1]{1,0:T(1,128)} %bitcast.place_ref, bf16[512,128]{1,0:T(8,128)(2,1)S(1)} %bitcast.10, f32[1024,256]{1,0:T(8,128)S(1)} %get-tuple-element.9.table_ref.refs_5_, f32[64,256]{1,0:T(8,128)S(1)} %get-tuple-element.10.norms_ref.refs_6_), custom_call_target="tpu_custom_call" | custom-call | flops 4194304 | bytes 4194304 | tf_op jit(solution)/shard_map/near_rows/pallas_call | solution.py:270
  24.6 0.0 collective-permute-done.2.refs_2_
  24.6 2.7 %collective-permute-done.1.refs_1_ = bf16[512,128]{1,0:T(8,128)(2,1)S(1)} collective-permute-done((bf16[512,128]{1,0:T(8,128)(2,1)S(1)}, bf16[512,128]{1,0:T(8,128)(2,1)S(1)}, u32[]{:S(2)}, u32[]{:S(2)}) %collective-permute-start.1) | collective-permute-done | bytes 131104 | tf_op jit(solution)/shard_map/ppermute | solution.py:244
  27.3 0.0 collective-permute-done.refs_0_
  27.3 28.7 %all_rows.1 = f32[8,128]{1,0:T(8,128)} custom-call(s32[1,1]{1,0:T(1,128)} %bitcast.place_ref, bf16[512,128]{1,0:T(8,128)(2,1)S(1)} %collective-permute-done.refs_0_, bf16[512,128]{1,0:T(8,128)(2,1)S(1)} %collective-permute-done.1.refs_1_, bf16[512,128]{1,0:T(8,128)(2,1)S(1)} %collective-permute-done.2.refs_2_, ...), custom_call_target="tpu_custom_call" | custom-call | flops 8589934592 | bytes 8388608 | tf_op jit(solution)/shard_map/all_rows/pallas_call | solution.py:291
Async XLA Ops:
  0.0 0.9 %copy-start.1 = (s32[1,1,64,512]{3,2,1,0:T(8,128)S(1)}, s32[1,1,64,512]{3,2,1,0:T(8,128)}, u32[]{:S(2)}) copy-start(s32[1,1,64,512]{3,2,1,0:T(8,128)} %param.4) | copy-start | bytes 393220
  0.9 0.7 %copy-start.3 = (s32[1,1,512,1]{2,3,1,0:T(1,128)S(1)}, s32[1,1,512,1]{2,3,1,0:T(1,128)}, u32[]{:S(2)}) copy-start(s32[1,1,512,1]{2,3,1,0:T(1,128)} %param.5) | copy-start | bytes 6148
  12.8 11.8 %collective-permute-start.2 = (bf16[512,128]{1,0:T(8,128)(2,1)S(1)}, bf16[512,128]{1,0:T(8,128)(2,1)S(1)}, u32[]{:S(2)}, u32[]{:S(2)}) collective-permute-start(bf16[512,128]{1,0:T(8,128)(2,1)S(1)} %bitcast.7), channel_id=1, source_target_pairs={{0,3},{1,0},{2,1},{3,2},{4,7},{5,4},{6,5},{7,6},{8,11},{9,8},{10,9... | collective-permute-start | bytes 393224 | tf_op jit(solution)/shard_map/ppermute | solution.py:244
  16.4 10.9 %collective-permute-start.1 = (bf16[512,128]{1,0:T(8,128)(2,1)S(1)}, bf16[512,128]{1,0:T(8,128)(2,1)S(1)}, u32[]{:S(2)}, u32[]{:S(2)}) collective-permute-start(bf16[512,128]{1,0:T(8,128)(2,1)S(1)} %bitcast.8), channel_id=1, source_target_pairs={{0,2},{1,3},{2,0},{3,1},{4,6},{5,7},{6,4},{7,5},{8,10},{9,11},{10,... | collective-permute-start | bytes 393224 | tf_op jit(solution)/shard_map/ppermute | solution.py:244
  16.4 10.9 %collective-permute-start = (bf16[512,128]{1,0:T(8,128)(2,1)S(1)}, bf16[512,128]{1,0:T(8,128)(2,1)S(1)}, u32[]{:S(2)}, u32[]{:S(2)}) collective-permute-start(bf16[512,128]{1,0:T(8,128)(2,1)S(1)} %bitcast.9), channel_id=1, source_target_pairs={{0,1},{1,2},{2,3},{3,0},{4,5},{5,6},{6,7},{7,4},{8,9},{9,10},{10,1... | collective-permute-start | bytes 393224 | tf_op jit(solution)/shard_map/ppermute | solution.py:244
  17.4 1.0 %copy-start = (bf16[256,1024]{1,0:T(8,128)(2,1)S(1)}, bf16[256,1024]{1,0:T(8,128)(2,1)}, u32[]{:S(2)}) copy-start(bf16[256,1024]{1,0:T(8,128)(2,1)} %codebook_ref.1) | copy-start | bytes 1572868
  18.4 0.7 %copy-start.2 = (bf16[8,1024]{1,0:T(8,128)(2,1)S(1)}, bf16[8,1024]{1,0:T(8,128)(2,1)}, u32[]{:S(2)}) copy-start(bf16[8,1024]{1,0:T(8,128)(2,1)} %centroids_ref.1) | copy-start | bytes 49156

commit v3 on v2

--- a/solution.py
+++ b/solution.py
@@ -9,13 +9,26 @@
 
 LANES = 128
 COLS = 256
+STEP = 512
 LOW = -4.0
 VMEM_LIMIT = 48 * 1024 * 1024
 PARAMS = pltpu.CompilerParams(vmem_limit_bytes=VMEM_LIMIT)
 
 
+LANE_LOOKUP = lax.GatherDimensionNumbers(
+    offset_dims=(),
+    collapsed_slice_dims=(1,),
+    start_index_map=(1,),
+    operand_batching_dims=(0,),
+    start_indices_batching_dims=(0,),
+)
+
+
 def take_lanes(table, index):
-    return jnp.take_along_axis(table, index, axis=1, mode="promise_in_bounds")
+    return lax.gather(
+        table, index[:, :, None], LANE_LOOKUP, (1, 1),
+        mode=lax.GatherScatterMode.PROMISE_IN_BOUNDS,
+    )
 
 
 def pack_kernel(devices, capacity, codes_ref, routes_ref, out_ref):
@@ -50,16 +63,23 @@
     out_ref[...] = jnp.concatenate(halves, axis=1).astype(jnp.bfloat16)
 
 
-def table_kernel(group_ref, codebook_ref, centroids_ref, table_ref, norms_ref):
+def table_kernel(group_ref, codebook_ref, centroids_ref, words_ref, centre_ref, norms_ref):
     words, width = codebook_ref.shape
     subspaces = norms_ref.shape[0]
     pick = lax.broadcasted_iota(jnp.int32, (centroids_ref.shape[0], 1), 0) == group_ref[0, 0]
     centre = jnp.sum(
         jnp.where(pick, centroids_ref[...].astype(jnp.float32), 0.0), axis=0, keepdims=True
     )
-    table = jnp.transpose(codebook_ref[...].astype(jnp.float32) + centre)
-    table_ref[...] = table
-    norms_ref[...] = jnp.sum((table * table).reshape(subspaces, width // subspaces, words), axis=1)
+    centre = jnp.transpose(jnp.broadcast_to(centre, (LANES, width)))
+    centre_ref[...] = centre
+    turned = jnp.transpose(codebook_ref[...].astype(jnp.float32))
+    words_ref[...] = turned.astype(jnp.bfloat16)
+    for half in range(words // LANES):
+        lanes = slice(half * LANES, (half + 1) * LANES)
+        table = turned[:, lanes] + centre
+        norms_ref[:, lanes] = jnp.sum(
+            (table * table).reshape(subspaces, width // subspaces, LANES), axis=1
+        )
 
 
 def owner_block(codes_ref, owner, owners):
@@ -97,25 +117,26 @@
     return tile_scale(lo, hi, norms_ref)
 
 
-def decode_tile(lo_ref, hi_ref, tile, now_ref, table_ref, norms_ref, units_ref, start):
+def decode_tile(
+    lo_ref, hi_ref, tile, now_ref, words_ref, centre_ref, norms_ref, units_ref, start
+):
     subspaces = norms_ref.shape[0]
-    sub_width = table_ref.shape[0] // subspaces
+    sub_width = words_ref.shape[0] // subspaces
     start = pl.multiple_of(start, LANES)
     scale = stage_tile(lo_ref, hi_ref, tile, now_ref, 0, norms_ref)
     for sub in range(subspaces):
         lo = jnp.broadcast_to(now_ref[0, 0, sub : sub + 1, :], (sub_width, LANES))
         hi = jnp.broadcast_to(now_ref[0, 1, sub : sub + 1, :], (sub_width, LANES)) > 0
+        lo = lo.astype(jnp.int16)
         rows = slice(sub * sub_width, (sub + 1) * sub_width)
-        word = jnp.where(
-            hi,
-            take_lanes(table_ref[rows, LANES:], lo),
-            take_lanes(table_ref[rows, :LANES], lo),
-        )
-        units_ref[rows, pl.ds(start, LANES)] = (word * scale).astype(jnp.bfloat16)
+        lower = take_lanes(words_ref[rows, :LANES], lo).astype(jnp.float32)
+        upper = take_lanes(words_ref[rows, LANES:], lo).astype(jnp.float32)
+        embed = jnp.where(hi, upper, lower) + centre_ref[rows, :]
+        units_ref[rows, pl.ds(start, LANES)] = (embed * scale).astype(jnp.bfloat16)
 
 
 def near_kernel(
-    place_ref, codes_ref, table_ref, norms_ref, units_ref, mark_ref,
+    place_ref, codes_ref, words_ref, centre_ref, norms_ref, units_ref, mark_ref,
     lo_ref, hi_ref, now_ref,
 ):
     owners = units_ref.shape[1] // COLS
@@ -124,7 +145,10 @@
         unpack_codes(owner_block(codes_ref, owner, owners), lo_ref, hi_ref, mark_ref, turn)
 
     def one_tile(tile, _):
-        decode_tile(lo_ref, hi_ref, tile, now_ref, table_ref, norms_ref, units_ref, tile * LANES)
+        decode_tile(
+            lo_ref, hi_ref, tile, now_ref, words_ref, centre_ref, norms_ref, units_ref,
+            tile * LANES,
+        )
         return 0
 
     lax.fori_loop(0, 2 * owners, one_tile, 0)
@@ -132,10 +156,10 @@
 
 def last_kernel(sizes, place_ref, *refs):
     capacity, clusters, members = sizes
-    more = len(refs) - 12
+    more = len(refs) - 13
     codes_refs = refs[:more]
     (
-        near_ref, near_mark_ref, table_ref, norms_ref, out_ref,
+        near_ref, near_mark_ref, words_ref, centre_ref, norms_ref, out_ref,
         left_ref, units_ref, best_ref, lo_ref, hi_ref, mark_ref, now_ref,
     ) = refs[more:]
     slots, width = left_ref.shape
@@ -162,7 +186,8 @@
         def one_tile(tile, _):
             tile = tile + turn * per_turn
             decode_tile(
-                lo_ref, hi_ref, tile, now_ref, table_ref, norms_ref, units_ref, tile * LANES
+                lo_ref, hi_ref, tile, now_ref, words_ref, centre_ref, norms_ref, units_ref,
+                tile * LANES,
             )
             return 0
 
@@ -176,24 +201,27 @@
     lax.fori_loop(0, per_turn, turn_left, 0)
     best_ref[...] = jnp.full(best_ref.shape, LOW, jnp.float32)
 
-    def score(step, _):
-        start = pl.multiple_of(step * COLS, COLS)
+    def score(step, _, own):
+        start = pl.multiple_of(step * STEP, STEP)
         scores = jnp.dot(
-            left_ref[...], units_ref[:, pl.ds(start, COLS)], preferred_element_type=jnp.float32
+            left_ref[...], units_ref[:, pl.ds(start, STEP)], preferred_element_type=jnp.float32
         )
         best = best_ref[...]
-        row_ids = lax.broadcasted_iota(jnp.int32, (slots, LANES), 0)
-        lane_ids = lax.broadcasted_iota(jnp.int32, (slots, LANES), 1)
-        for part in range(COLS // LANES):
-            filled = mark_ref[step * (COLS // LANES) + part][0:1, :] > 0
-            keep = filled & (row_ids != lane_ids + (start + part * LANES))
+        for part in range(STEP // LANES):
+            keep = mark_ref[step * (STEP // LANES) + part][0:1, :] > 0
+            if own:
+                row_ids = lax.broadcasted_iota(jnp.int32, (slots, LANES), 0)
+                lane_ids = lax.broadcasted_iota(jnp.int32, (slots, LANES), 1)
+                keep = keep & (row_ids != lane_ids + (start + part * LANES))
             best = jnp.maximum(
                 best, jnp.where(keep, scores[:, part * LANES : (part + 1) * LANES], LOW)
             )
         best_ref[...] = best
         return 0
 
-    lax.fori_loop(0, owners * groups, score, 0)
+    own_steps = slots // STEP
+    lax.fori_loop(0, own_steps, functools.partial(score, own=True), 0)
+    lax.fori_loop(own_steps, owners * own_steps, functools.partial(score, own=False), 0)
 
     half_rows = capacity // 2
     tiles = slots // LANES
@@ -254,10 +282,11 @@
 
     place = lax.axis_index("blk").astype(i32).reshape(1, 1)
     group = lax.axis_index("cluster").astype(i32).reshape(1, 1)
-    table, norms = pl.pallas_call(
+    table = pl.pallas_call(
         table_kernel,
         out_shape=(
-            jax.ShapeDtypeStruct((width, words), f32),
+            jax.ShapeDtypeStruct((width, words), bf16),
+            jax.ShapeDtypeStruct((width, LANES), f32),
             jax.ShapeDtypeStruct((subspaces, words), f32),
         ),
         in_specs=[smem, vmem, vmem],
@@ -273,7 +302,7 @@
             jax.ShapeDtypeStruct((width, members * COLS), bf16),
             jax.ShapeDtypeStruct((2 * members, 8, LANES), f32),
         ),
-        in_specs=[smem, vmem, vmem, vmem],
+        in_specs=[smem] + [vmem] * 4,
         scratch_shapes=[
             pltpu.VMEM((2 * members, subspaces, LANES), i32),
             pltpu.VMEM((2 * members, subspaces, LANES), i32),
@@ -286,12 +315,12 @@
             transcendentals=0,
         ),
         name="near_rows",
-    )(place, blocks[0], table, norms)
+    )(place, blocks[0], *table)
     more = groups - 1
     nearest = pl.pallas_call(
         functools.partial(last_kernel, (capacity, clusters, members)),
         out_shape=jax.ShapeDtypeStruct((tiles, LANES), f32),
-        in_specs=[smem] + [vmem] * (more + 4),
+        in_specs=[smem] + [vmem] * (more + 5),
         scratch_shapes=[
             pltpu.VMEM((slots, width), bf16),
             pltpu.VMEM((width, members * slots), bf16),
@@ -308,7 +337,7 @@
             transcendentals=0,
         ),
         name="all_rows",
-    )(place, *blocks[1:], near, near_mark, table, norms)
+    )(place, *blocks[1:], near, near_mark, *table)
     return nearest.reshape(1, 1, slots)
 
 

time: 56.3 us -> 51 us (0.906)
  Pallas kernels: 34.8 us -> 28.4 us
  waiting for transfers between devices: 2.7 us -> 3.82 us
    pallas_call x1, Pallas kernels: 28.7 us -> 23.4 us  [on_device(): pl.pallas_call(functools.partial(last_kernel, (capacity, clusters, member...]
    pallas_call x1, Pallas kernels: 5.06 us -> 3.79 us  [on_device(): pl.pallas_call(near_kernel, out_shape=(jax.ShapeDtypeStruct((width, membe...]
    ppermute x3, waiting for transfers between devices: 2.7 us -> 3.82 us  [on_device(): lax.ppermute(here, 'blk', [(i, (i + shift) % members) for i in range(memb...]
  transfers between devices with their start and end apart: 3 -> 3, of which waited for: 1 -> 1; matrix products, arithmetic and copies ran while one was open for 0% -> 0% of each run, Pallas kernels for 10% -> 8%
where the time goes in v3:
time: 51 us; the launch traced here: 50.7 us
  Pallas kernels  28.4 us (56%)
  blocking collectives  10.5 us (21%)
  starting transfers between devices  4.61 us (9%)
  waiting for transfers between devices  3.82 us (7%)
  local copies, waits for them, and re-layouts  3.34 us (7%)
    pallas_call x1, Pallas kernels, on_device(): pl.pallas_call(functools.partial(last_kernel, (capacity, clusters, member...  23.4 us
    all_to_all x1, blocking collectives, on_device(): lax.all_to_all(packed, 'cluster', split_axis=0, concat_axis=0, tiled=True)  10.5 us
    ppermute x3, starting transfers between devices, on_device(): lax.ppermute(here, 'blk', [(i, (i + shift) % members) for i in range(memb...  4.61 us
    ppermute x3, waiting for transfers between devices, on_device(): lax.ppermute(here, 'blk', [(i, (i + shift) % members) for i in range(memb...  3.82 us
    pallas_call x1, Pallas kernels, on_device(): pl.pallas_call(near_kernel, out_shape=(jax.ShapeDtypeStruct((width, membe...  3.79 us
    unnamed x8, local copies, waits for them, and re-layouts  3.34 us
  transfers between devices with their start and end apart: 3, of which 1 were waited for; matrix products, arithmetic and copies ran while one was open for 0% of the time, Pallas kernels for 8%

profile of v3, /device:TPU:0, one launch (start us, length us, event | category | flops | bytes accessed | tf_op | source)
XLA Modules:
  0.0 50.7 jit_solution(6609991447332645478)
XLA Ops:
  0.0 0.0 copy-start.1
  0.0 0.9 %copy-done.1 = s32[1,1,64,512]{3,2,1,0:T(8,128)S(1)} copy-done((s32[1,1,64,512]{3,2,1,0:T(8,128)S(1)}, s32[1,1,64,512]{3,2,1,0:T(8,128)}, u32[]{:S(2)}) %copy-start.1) | copy-done | bytes 131096
  0.9 0.0 copy-start.3
  0.9 0.7 %copy-done.3 = s32[1,1,512,1]{2,3,1,0:T(1,128)S(1)} copy-done((s32[1,1,512,1]{2,3,1,0:T(1,128)S(1)}, s32[1,1,512,1]{2,3,1,0:T(1,128)}, u32[]{:S(2)}) %copy-start.3) | copy-done | bytes 2072
  1.6 0.7 %pack_rows.1 = bf16[512,128]{1,0:T(8,128)(2,1)S(1)} custom-call(s32[64,512]{1,0:T(8,128)S(1)} %bitcast.12, s32[1,512]{1,0:T(1,128)S(1)} %bitcast.13), custom_call_target="tpu_custom_call" | custom-call | tf_op jit(solution)/shard_map/pack_rows/pallas_call | solution.py:264
  2.3 10.5 %all_to_all.11 = bf16[8,64,128]{2,1,0:T(8,128)(2,1)S(1)} all-to-all(bf16[8,64,128]{2,1,0:T(8,128)(2,1)S(1)} %bitcast.11), channel_id=1, replica_groups=mesh['cluster'=8,'blk'=4] {'cluster'}, dimensions={0} | all-to-all | bytes 262144 | tf_op jit(solution)/shard_map/all_to_all | solution.py:270
  12.8 3.6 %collective-permute-start.2 = (bf16[512,128]{1,0:T(8,128)(2,1)S(1)}, bf16[512,128]{1,0:T(8,128)(2,1)S(1)}, u32[]{:S(2)}, u32[]{:S(2)}) collective-permute-start(bf16[512,128]{1,0:T(8,128)(2,1)S(1)} %bitcast.7), channel_id=1, source_target_pairs={{0,3},{1,0},{2,1},{3,2},{4,7},{5,4},{6,5},{7,6},{8,11},{9,8},{10,9... | collective-permute-start | bytes 393224 | tf_op jit(solution)/shard_map/ppermute | solution.py:272
  16.4 0.0 collective-permute-start.1
  16.4 1.0 %collective-permute-start = (bf16[512,128]{1,0:T(8,128)(2,1)S(1)}, bf16[512,128]{1,0:T(8,128)(2,1)S(1)}, u32[]{:S(2)}, u32[]{:S(2)}) collective-permute-start(bf16[512,128]{1,0:T(8,128)(2,1)S(1)} %bitcast.9), channel_id=1, source_target_pairs={{0,1},{1,2},{2,3},{3,0},{4,5},{5,6},{6,7},{7,4},{8,9},{9,10},{10,1... | collective-permute-start | bytes 393224 | tf_op jit(solution)/shard_map/ppermute | solution.py:272
  17.4 0.0 copy-start
  17.4 1.0 %copy-done = bf16[256,1024]{1,0:T(8,128)(2,1)S(1)} copy-done((bf16[256,1024]{1,0:T(8,128)(2,1)S(1)}, bf16[256,1024]{1,0:T(8,128)(2,1)}, u32[]{:S(2)}) %copy-start) | copy-done | bytes 524312
  18.4 0.0 copy-start.2
  18.5 0.7 %copy-done.2 = bf16[8,1024]{1,0:T(8,128)(2,1)S(1)} copy-done((bf16[8,1024]{1,0:T(8,128)(2,1)S(1)}, bf16[8,1024]{1,0:T(8,128)(2,1)}, u32[]{:S(2)}) %copy-start.2) | copy-done | bytes 16408
  19.2 0.5 word_table.1
  19.7 3.8 %near_rows.1 = (bf16[1024,1024]{1,0:T(8,128)(2,1)S(1)}, f32[8,8,128]{2,1,0:T(8,128)S(1)}) custom-call(s32[1,1]{1,0:T(1,128)} %bitcast.place_ref, bf16[512,128]{1,0:T(8,128)(2,1)S(1)} %bitcast.10, bf16[1024,256]{1,0:T(8,128)(2,1)S(1)} %get-tuple-element.10.words_ref.refs_5_, f32[1024,128]{1,0:T(8,128)S(1)} %get-tuple-element.11.centre_ref.refs_6_, ...), custom_call_target="tpu_custom_call" | custom-call | flops 4194304 | bytes 4194304 | tf_op jit(solution)/shard_map/near_rows/pallas_call | solution.py:299
  23.5 0.0 collective-permute-done.2.refs_2_
  23.5 3.8 %collective-permute-done.1.refs_1_ = bf16[512,128]{1,0:T(8,128)(2,1)S(1)} collective-permute-done((bf16[512,128]{1,0:T(8,128)(2,1)S(1)}, bf16[512,128]{1,0:T(8,128)(2,1)S(1)}, u32[]{:S(2)}, u32[]{:S(2)}) %collective-permute-start.1) | collective-permute-done | bytes 131104 | tf_op jit(solution)/shard_map/ppermute | solution.py:272
  27.3 0.0 collective-permute-done.refs_0_
  27.3 23.4 %all_rows.1 = f32[8,128]{1,0:T(8,128)} custom-call(s32[1,1]{1,0:T(1,128)} %bitcast.place_ref, bf16[512,128]{1,0:T(8,128)(2,1)S(1)} %collective-permute-done.refs_0_, bf16[512,128]{1,0:T(8,128)(2,1)S(1)} %collective-permute-done.1.refs_1_, bf16[512,128]{1,0:T(8,128)(2,1)S(1)} %collective-permute-done.2.refs_2_, ...), custom_call_target="tpu_custom_call" | custom-call | flops 8589934592 | bytes 8388608 | tf_op jit(solution)/shard_map/all_rows/pallas_call | solution.py:320
Async XLA Ops:
  0.0 0.9 %copy-start.1 = (s32[1,1,64,512]{3,2,1,0:T(8,128)S(1)}, s32[1,1,64,512]{3,2,1,0:T(8,128)}, u32[]{:S(2)}) copy-start(s32[1,1,64,512]{3,2,1,0:T(8,128)} %param.4) | copy-start | bytes 393220
  0.9 0.7 %copy-start.3 = (s32[1,1,512,1]{2,3,1,0:T(1,128)S(1)}, s32[1,1,512,1]{2,3,1,0:T(1,128)}, u32[]{:S(2)}) copy-start(s32[1,1,512,1]{2,3,1,0:T(1,128)} %param.5) | copy-start | bytes 6148
  12.8 10.7 %collective-permute-start.2 = (bf16[512,128]{1,0:T(8,128)(2,1)S(1)}, bf16[512,128]{1,0:T(8,128)(2,1)S(1)}, u32[]{:S(2)}, u32[]{:S(2)}) collective-permute-start(bf16[512,128]{1,0:T(8,128)(2,1)S(1)} %bitcast.7), channel_id=1, source_target_pairs={{0,3},{1,0},{2,1},{3,2},{4,7},{5,4},{6,5},{7,6},{8,11},{9,8},{10,9... | collective-permute-start | bytes 393224 | tf_op jit(solution)/shard_map/ppermute | solution.py:272
  16.4 10.9 %collective-permute-start.1 = (bf16[512,128]{1,0:T(8,128)(2,1)S(1)}, bf16[512,128]{1,0:T(8,128)(2,1)S(1)}, u32[]{:S(2)}, u32[]{:S(2)}) collective-permute-start(bf16[512,128]{1,0:T(8,128)(2,1)S(1)} %bitcast.8), channel_id=1, source_target_pairs={{0,2},{1,3},{2,0},{3,1},{4,6},{5,7},{6,4},{7,5},{8,10},{9,11},{10,... | collective-permute-start | bytes 393224 | tf_op jit(solution)/shard_map/ppermute | solution.py:272
  16.4 10.9 %collective-permute-start = (bf16[512,128]{1,0:T(8,128)(2,1)S(1)}, bf16[512,128]{1,0:T(8,128)(2,1)S(1)}, u32[]{:S(2)}, u32[]{:S(2)}) collective-permute-start(bf16[512,128]{1,0:T(8,128)(2,1)S(1)} %bitcast.9), channel_id=1, source_target_pairs={{0,1},{1,2},{2,3},{3,0},{4,5},{5,6},{6,7},{7,4},{8,9},{9,10},{10,1... | collective-permute-start | bytes 393224 | tf_op jit(solution)/shard_map/ppermute | solution.py:272
  17.4 1.0 %copy-start = (bf16[256,1024]{1,0:T(8,128)(2,1)S(1)}, bf16[256,1024]{1,0:T(8,128)(2,1)}, u32[]{:S(2)}) copy-start(bf16[256,1024]{1,0:T(8,128)(2,1)} %codebook_ref.1) | copy-start | bytes 1572868
  18.4 0.7 %copy-start.2 = (bf16[8,1024]{1,0:T(8,128)(2,1)S(1)}, bf16[8,1024]{1,0:T(8,128)(2,1)}, u32[]{:S(2)}) copy-start(bf16[8,1024]{1,0:T(8,128)(2,1)} %centroids_ref.1) | copy-start | bytes 49156

commit v4 on v3

v4 whole, which is shorter than its diff:
```python
import functools

import jax
import jax.numpy as jnp
from jax import lax
from jax.experimental import pallas as pl
from jax.experimental.pallas import tpu as pltpu
from jax.sharding import PartitionSpec as P

LANES = 128
COLS = 256
STEP = 512
LOW = -4.0
VMEM_LIMIT = 40 * 1024 * 1024
PARAMS = pltpu.CompilerParams(vmem_limit_bytes=VMEM_LIMIT)


LANE_LOOKUP = lax.GatherDimensionNumbers(
    offset_dims=(),
    collapsed_slice_dims=(1,),
    start_index_map=(1,),
    operand_batching_dims=(0,),
    start_indices_batching_dims=(0,),
)


def take_lanes(table, index):
    return lax.gather(
        table, index[:, :, None], LANE_LOOKUP, (1, 1),
        mode=lax.GatherScatterMode.PROMISE_IN_BOUNDS,
    )


def pack_kernel(devices, capacity, rows_ref, out_ref):
    subspaces = rows_ref.shape[0] - 1
    in_rows = rows_ref.shape[1]
    half_rows = capacity // 2
    targets = rows_ref[subspaces:, :]
    hot = lax.broadcasted_iota(jnp.int32, (devices, in_rows), 0) == targets
    hot32 = jnp.where(hot, 1.0, 0.0)
    earlier = (
        lax.broadcasted_iota(jnp.int32, (in_rows, in_rows), 0)
        < lax.broadcasted_iota(jnp.int32, (in_rows, in_rows), 1)
    )
    running = jnp.dot(
        hot32.astype(jnp.bfloat16),
        jnp.where(earlier, 1.0, 0.0).astype(jnp.bfloat16),
        preferred_element_type=jnp.float32,
    )
    position = jnp.sum(hot32 * running, axis=0, keepdims=True).astype(jnp.int32)
    second = position >= half_rows
    key = targets * half_rows + jnp.where(second, position - half_rows, position)
    out_rows = devices * half_rows
    row_ids = lax.broadcasted_iota(jnp.int32, (out_rows, in_rows), 0)
    values = (rows_ref[:subspaces, :] + 1).astype(jnp.bfloat16)
    halves = []
    for wanted in (jnp.where(second, -1, key), jnp.where(second, key, -1)):
        move = jnp.where(row_ids == wanted, 1.0, 0.0).astype(jnp.bfloat16)
        halves.append(
            lax.dot_general(
                move, values, (((1,), (1,)), ((), ())), preferred_element_type=jnp.float32
            )
        )
    out_ref[...] = jnp.concatenate(halves, axis=1).astype(jnp.bfloat16)


def table_kernel(group_ref, book_ref, words_ref, centre_ref, norms_ref):
    width, words = words_ref.shape
    subspaces = norms_ref.shape[0]
    centres = book_ref[words:, :].astype(jnp.float32)
    pick = lax.broadcasted_iota(jnp.int32, (centres.shape[0], 1), 0) == group_ref[0, 0]
    centre = jnp.sum(jnp.where(pick, centres, 0.0), axis=0, keepdims=True)
    centre = jnp.transpose(jnp.broadcast_to(centre, (LANES, width)))
    centre_ref[...] = centre
    turned = jnp.transpose(book_ref[:words, :].astype(jnp.float32))
    words_ref[...] = turned.astype(jnp.bfloat16)
    for half in range(words // LANES):
        lanes = slice(half * LANES, (half + 1) * LANES)
        table = turned[:, lanes] + centre
        norms_ref[:, lanes] = jnp.sum(
            (table * table).reshape(subspaces, width // subspaces, LANES), axis=1
        )


def owner_block(codes_ref, owner, owners):
    parts = [
        codes_ref[pl.ds(pl.multiple_of((part * owners + owner) * 16, 16), 16), :]
        for part in range(LANES // 16)
    ]
    return jnp.concatenate(parts, axis=0)


def unpack_codes(block, norms_ref, code_ref, scale_ref, mark_ref, group, place):
    turned = jnp.transpose(block.astype(jnp.float32)).astype(jnp.int32)
    subspaces = turned.shape[0] // 2
    for half in range(2):
        part = turned[half * subspaces : (half + 1) * subspaces]
        code = jnp.maximum(part - 1, 0)
        code_ref[2 * group + half] = code
        mark_ref[2 * place + half] = jnp.where(part[0:8] > 0, 1.0, 0.0)
        low = code & (LANES - 1)
        squares = jnp.where(
            code >= LANES,
            take_lanes(norms_ref[:, LANES:], low),
            take_lanes(norms_ref[:, :LANES], low),
        )
        scale = lax.rsqrt(jnp.sum(squares, axis=0, keepdims=True) + 1e-06)
        scale_ref[2 * group + half] = jnp.broadcast_to(scale, (8, LANES))


def decode_groups(
    place, first, codes_refs, words_ref, centre_ref, norms_ref,
    units_ref, left_ref, mark_ref, code_ref, scale_ref, now_ref,
):
    slots = left_ref.shape[0]
    owners = units_ref.shape[1] // slots
    groups = slots // COLS
    subspaces = norms_ref.shape[0]
    sub_width = words_ref.shape[0] // subspaces
    for which, codes_ref in enumerate(codes_refs):
        for turn in range(owners):
            owner = lax.rem(place + turn, owners)
            unpack_codes(
                owner_block(codes_ref, owner, owners), norms_ref, code_ref, scale_ref, mark_ref,
                which * owners + turn, turn * groups + first + which,
            )

    for which in range(len(codes_refs)):

        def one_group(turn, _):
            start = pl.multiple_of(turn * slots + (first + which) * COLS, COLS)
            scales = []
            for half in range(2):
                tile = 2 * (which * owners + turn) + half
                now_ref[half] = code_ref[tile]
                scales.append(scale_ref[tile])
            for sub in range(subspaces):
                rows = slice(sub * sub_width, (sub + 1) * sub_width)
                for half in range(2):
                    code = jnp.broadcast_to(
                        now_ref[half, sub : sub + 1, :], (sub_width, LANES)
                    ).astype(jnp.int16)
                    low = code & (LANES - 1)
                    word = jnp.where(
                        code > LANES - 1,
                        take_lanes(words_ref[rows, LANES:], low),
                        take_lanes(words_ref[rows, :LANES], low),
                    )
                    embed = word.astype(jnp.float32) + centre_ref[rows, :]
                    unit = embed * jnp.concatenate([scales[half]] * (sub_width // 8), axis=0)
                    units_ref[rows, pl.ds(start + half * LANES, LANES)] = unit.astype(jnp.bfloat16)
            return 0

        lax.fori_loop(0, owners, one_group, 0)
        for half in range(2):
            start = (first + which) * COLS + half * LANES
            left_ref[start : start + LANES, :] = jnp.transpose(units_ref[:, start : start + LANES])


def first_kernel(place_ref, codes_ref, words_ref, centre_ref, norms_ref, *refs):
    decode_groups(place_ref[0, 0], 0, [codes_ref], words_ref, centre_ref, norms_ref, *refs)


def middle_kernel(count, place_ref, *refs):
    codes_refs, refs = refs[:count], refs[count:]
    decode_groups(place_ref[0, 0], 1, codes_refs, *refs[:3], *refs[6:])


def last_kernel(sizes, place_ref, *refs):
    capacity, clusters, members, count = sizes
    place = place_ref[0, 0]
    codes_refs, refs = refs[:count], refs[count:]
    table_refs, refs = refs[:3], refs[6:]
    out_ref, units_ref, left_ref, mark_ref, best_ref, code_ref, scale_ref, now_ref = refs
    slots = left_ref.shape[0]
    owners = units_ref.shape[1] // slots
    decode_groups(
        place, slots // COLS - count, codes_refs, *table_refs,
        units_ref, left_ref, mark_ref, code_ref, scale_ref, now_ref,
    )
    best_ref[...] = jnp.full(best_ref.shape, LOW, jnp.float32)

    def score(step, _, own):
        start = pl.multiple_of(step * STEP, STEP)
        scores = jnp.dot(
            left_ref[...], units_ref[:, pl.ds(start, STEP)], preferred_element_type=jnp.float32
        )
        best = best_ref[...]
        for part in range(STEP // LANES):
            keep = mark_ref[step * (STEP // LANES) + part][0:1, :] > 0
            if own:
                row_ids = lax.broadcasted_iota(jnp.int32, (slots, LANES), 0)
                lane_ids = lax.broadcasted_iota(jnp.int32, (slots, LANES), 1)
                keep = keep & (row_ids != lane_ids + (start + part * LANES))
            best = jnp.maximum(
                best, jnp.where(keep, scores[:, part * LANES : (part + 1) * LANES], LOW)
            )
        best_ref[...] = best
        return 0

    own_steps = slots // STEP
    lax.fori_loop(0, own_steps, functools.partial(score, own=True), 0)
    lax.fori_loop(own_steps, owners * own_steps, functools.partial(score, own=False), 0)

    half_rows = capacity // 2
    tiles = slots // LANES
    lane = lax.broadcasted_iota(jnp.int32, (tiles, LANES), 1)
    slot = lax.broadcasted_iota(jnp.int32, (tiles, LANES), 0) * LANES + lane
    source, within = slot // capacity, slot % capacity
    turn = place ^ (source % members)
    own_row = (turn * clusters + source // members) * half_rows + within % half_rows
    tile_of = 2 * (own_row // LANES) + within // half_rows
    result = jnp.zeros((tiles, LANES), jnp.float32)
    for tile in range(tiles):
        best = jnp.max(
            jnp.transpose(best_ref[tile * LANES : (tile + 1) * LANES, :]), axis=0, keepdims=True
        )
        mark = mark_ref[tile]
        best = jnp.where(mark[0:1, :] > 0, best, 0.0)
        result = jnp.where(
            tile_of == tile,
            take_lanes(jnp.broadcast_to(best, (tiles, LANES)), own_row % LANES),
            result,
        )
    out_ref[...] = result


def on_device(codes, routes, codebook, centroids):
    clusters = lax.axis_size("cluster")
    members = lax.axis_size("blk")
    devices = clusters * members
    subspaces, in_rows = codes.shape[2:]
    capacity = 2 * in_rows // devices
    half_rows = capacity // 2
    slots = devices * capacity
    tiles = slots // LANES
    groups = slots // COLS
    words, width = codebook.shape
    bf16, f32, i32 = jnp.bfloat16, jnp.float32, jnp.int32
    smem = pl.BlockSpec(memory_space=pltpu.SMEM)
    vmem = pl.BlockSpec(memory_space=pltpu.VMEM)

    packed = pl.pallas_call(
        functools.partial(pack_kernel, devices, capacity),
        out_shape=jax.ShapeDtypeStruct((in_rows, 2 * subspaces), bf16),
        compiler_params=PARAMS,
        name="pack_rows",
    )(jnp.concatenate([codes[0, 0], routes.reshape(1, in_rows)], axis=0))
    here = lax.all_to_all(packed, "cluster", split_axis=0, concat_axis=0, tiled=True)
    def from_member(block, mask):
        return lax.ppermute(block, "blk", [(i, i ^ mask) for i in range(members)])

    masks = range(1, members)
    blocks = {0: here}
    for mask in masks:
        if mask & (mask - 1) == 0:
            blocks[mask] = from_member(here, mask)

    place = lax.axis_index("blk").astype(i32).reshape(1, 1)
    group = lax.axis_index("cluster").astype(i32).reshape(1, 1)
    table = pl.pallas_call(
        table_kernel,
        out_shape=(
            jax.ShapeDtypeStruct((width, words), bf16),
            jax.ShapeDtypeStruct((width, LANES), f32),
            jax.ShapeDtypeStruct((subspaces, words), f32),
        ),
        in_specs=[smem, vmem],
        compiler_params=PARAMS,
        cost_estimate=pl.CostEstimate(
            flops=4 * words * width, bytes_accessed=6 * words * width, transcendentals=0
        ),
        name="word_table",
    )(group, jnp.concatenate([codebook, centroids], axis=0))

    state_shape = (
        jax.ShapeDtypeStruct((width, members * slots), bf16),
        jax.ShapeDtypeStruct((slots, width), bf16),
        jax.ShapeDtypeStruct((2 * members * groups, 8, LANES), f32),
    )

    def code_scratch(count):
        return [
            pltpu.VMEM((2 * members * count, subspaces, LANES), i32),
            pltpu.VMEM((2 * members * count, 8, LANES), f32),
            pltpu.VMEM((2, subspaces, LANES), i32),
        ]

    def decode_cost(count):
        return pl.CostEstimate(
            flops=100 * count * members * COLS * width,
            bytes_accessed=4 * count * members * COLS * width,
            transcendentals=0,
        )

    first = pl.pallas_call(
        first_kernel,
        out_shape=state_shape,
        in_specs=[smem] + [vmem] * 4,
        out_specs=(vmem,) * 3,
        scratch_shapes=code_scratch(1),
        compiler_params=PARAMS,
        cost_estimate=decode_cost(1),
        name="first_rows",
    )
    whole_groups = half_rows == 16 and clusters * half_rows == LANES
    if whole_groups:
        units, left, marks = first(place, here, *table)
    for mask in masks:
        if mask not in blocks:
            low = mask & -mask
            block = blocks[mask - low]
            if whole_groups:
                block, marks = lax.optimization_barrier((block, marks))
            blocks[mask] = from_member(block, low)
    blocks = [here] + [blocks[mask] for mask in masks]
    if not whole_groups:
        every = jnp.stack(blocks).reshape(members, clusters, members, half_rows, LANES)
        every = every.transpose(2, 0, 1, 3, 4).reshape(members, groups, LANES // 16, 16, LANES)
        every = every.transpose(1, 2, 0, 3, 4).reshape(groups, members * LANES, LANES)
        blocks = list(every)
        units, left, marks = first(place, blocks[0], *table)
    state = (units, left, marks)
    count = groups - 2
    state = pl.pallas_call(
        functools.partial(middle_kernel, count),
        out_shape=state_shape,
        in_specs=[smem] + [vmem] * (count + 6),
        out_specs=(vmem,) * 3,
        scratch_shapes=code_scratch(count),
        input_output_aliases={count + 4 + which: which for which in range(3)},
        compiler_params=PARAMS,
        cost_estimate=decode_cost(count),
        name="middle_rows",
    )(place, *blocks[1 : 1 + count], *table, *state)
    nearest, *_ = pl.pallas_call(
        functools.partial(last_kernel, (capacity, clusters, members, 1)),
        out_shape=(jax.ShapeDtypeStruct((tiles, LANES), f32), *state_shape),
        in_specs=[smem] + [vmem] * 7,
        out_specs=(vmem,) * 4,
        scratch_shapes=[pltpu.VMEM((slots, LANES), f32)] + code_scratch(1),
        input_output_aliases={5 + which: 1 + which for which in range(3)},
        compiler_params=PARAMS,
        cost_estimate=pl.CostEstimate(
            flops=2 * slots * members * slots * width,
            bytes_accessed=8 * slots * width,
            transcendentals=0,
        ),
        name="last_rows",
    )(place, blocks[groups - 1], *table, *state)
    return nearest.reshape(1, 1, slots)


def solution(mesh):
    in_specs = (P("cluster", "blk", None, None), P("cluster", "blk", None, None), P(), P())
    out_specs = P("cluster", "blk", None)
    return jax.shard_map(
        on_device, mesh=mesh, in_specs=in_specs, out_specs=out_specs, check_vma=False
    )
```

time: 51 us -> 44.6 us (0.87)
  local copies, waits for them, and re-layouts: 3.34 us -> 0 us
  waiting for transfers between devices: 3.82 us -> 0.7 us
  other arithmetic: 0 us -> 2.03 us
  Pallas kernels: 28.4 us -> 26.4 us
    pallas_call x1, Pallas kernels: 23.4 us -> 14.6 us  [on_device(): pl.pallas_call(functools.partial(last_kernel, (capacity, clusters, member...]
    pallas_call x1 -> x2, Pallas kernels: 3.79 us -> 10.6 us  [the longest x1 7.02 us: on_device(): pl.pallas_call(functools.partial(middle_kernel, count), out_shape=state_s...]
    unnamed x8 -> x0, local copies, waits for them, and re-layouts: 3.34 us -> none
    ppermute x3, waiting for transfers between devices: 3.82 us -> 0.7 us  [from_member(): return lax.ppermute(block, 'blk', [(i, i ^ mask) for i in range(members)])]
    concatenate x0 -> x2, other arithmetic: none -> 2.03 us  [the longest x1 1.09 us: on_device(): jnp.concatenate([codebook, centroids], axis=0)]
  transfers between devices with their start and end apart: 3 -> 3, of which waited for: 1 -> 1; matrix products, arithmetic and copies ran while one was open for 0% -> 2% of each run, Pallas kernels for 8% -> 25%
where the time goes in v4:
time: 44.6 us; the launch traced here: 44.3 us
  Pallas kernels  26.4 us (59%)
  blocking collectives  10.5 us (24%)
  starting transfers between devices  4.62 us (10%)
  other arithmetic  2.03 us (5%)
  waiting for transfers between devices  0.7 us (2%)
    pallas_call x1, Pallas kernels, on_device(): pl.pallas_call(functools.partial(last_kernel, (capacity, clusters, member...  14.6 us
    all_to_all x1, blocking collectives, on_device(): lax.all_to_all(packed, 'cluster', split_axis=0, concat_axis=0, tiled=True)  10.5 us
    pallas_call x1, Pallas kernels, on_device(): pl.pallas_call(functools.partial(middle_kernel, count), out_shape=state_s...  7.02 us
    ppermute x3, starting transfers between devices, from_member(): return lax.ppermute(block, 'blk', [(i, i ^ mask) for i in range(members)])  4.62 us
    pallas_call x1, Pallas kernels, on_device(): units, left, marks = first(place, here, *table)  3.61 us
    concatenate x1, other arithmetic, on_device(): jnp.concatenate([codebook, centroids], axis=0)  1.09 us
    concatenate x1, other arithmetic, on_device(): jnp.concatenate([codes[0, 0], routes.reshape(1, in_rows)], axis=0)  0.93 us
  transfers between devices with their start and end apart: 3, of which 1 were waited for; matrix products, arithmetic and copies ran while one was open for 2% of the time, Pallas kernels for 25%

profile of v4, /device:TPU:0, one launch (start us, length us, event | category | flops | bytes accessed | tf_op | source)
XLA Modules:
  0.0 44.3 jit_solution(16089240257386326537)
XLA Ops:
  0.0 0.9 %pad_add_fusion.rows_ref = s32[65,512]{1,0:T(8,128)S(1)} fusion(s32[1,512]{1,0:T(1,128)} %bitcast.12, s32[64,512]{1,0:T(8,128)} %bitcast.11), kind=kLoop, calls=%fused_computation.1 | loop fusion | flops 33280 | bytes 266240 | tf_op jit(solution)/shard_map/concatenate | solution.py:248
  0.9 0.7 %pack_rows.1 = bf16[512,128]{1,0:T(8,128)(2,1)S(1)} custom-call(s32[65,512]{1,0:T(8,128)S(1)} %pad_add_fusion.rows_ref), custom_call_target="tpu_custom_call" | custom-call | tf_op jit(solution)/shard_map/pack_rows/pallas_call | solution.py:243
  1.6 10.5 %all_to_all.11 = bf16[8,64,128]{2,1,0:T(8,128)(2,1)S(1)} all-to-all(bf16[8,64,128]{2,1,0:T(8,128)(2,1)S(1)} %bitcast.10), channel_id=1, replica_groups=mesh['cluster'=8,'blk'=4] {'cluster'}, dimensions={0} | all-to-all | bytes 262144 | tf_op jit(solution)/shard_map/all_to_all | solution.py:249
  12.1 1.6 %collective-permute-start.2 = (bf16[512,128]{1,0:T(8,128)(2,1)S(1)}, bf16[512,128]{1,0:T(8,128)(2,1)S(1)}, u32[]{:S(2)}, u32[]{:S(2)}) collective-permute-start(bf16[512,128]{1,0:T(8,128)(2,1)S(1)} %bitcast.7), channel_id=1, source_target_pairs={{0,1},{1,0},{2,3},{3,2},{4,5},{5,4},{6,7},{7,6},{8,9},{9,8},{10,11... | collective-permute-start | bytes 393224 | tf_op jit(solution)/shard_map/ppermute | solution.py:251
  13.7 2.6 %collective-permute-start = (bf16[512,128]{1,0:T(8,128)(2,1)S(1)}, bf16[512,128]{1,0:T(8,128)(2,1)S(1)}, u32[]{:S(2)}, u32[]{:S(2)}) collective-permute-start(bf16[512,128]{1,0:T(8,128)(2,1)S(1)} %bitcast.8), channel_id=1, source_target_pairs={{0,2},{1,3},{2,0},{3,1},{4,6},{5,7},{6,4},{7,5},{8,10},{9,11},{10,... | collective-permute-start | bytes 393224 | tf_op jit(solution)/shard_map/ppermute | solution.py:251
  16.3 1.1 %pad_maximum_fusion.book_ref = bf16[264,1024]{1,0:T(8,128)(2,1)S(1)} fusion(bf16[8,1024]{1,0:T(8,128)(2,1)} %param.7, bf16[256,1024]{1,0:T(8,128)(2,1)} %param.6), kind=kLoop, calls=%fused_computation | loop fusion | flops 1081344 | bytes 1081344 | tf_op jit(solution)/shard_map/concatenate | solution.py:274
  17.4 0.5 %word_table.1 = (bf16[1024,256]{1,0:T(8,128)(2,1)S(1)}, f32[1024,128]{1,0:T(8,128)S(1)}, f32[64,256]{1,0:T(8,128)S(1)}) custom-call(s32[1,1]{1,0:T(1,128)} %bitcast.5.group_ref, bf16[264,1024]{1,0:T(8,128)(2,1)S(1)} %pad_maximum_fusion.book_ref), custom_call_target="tpu_custom_call" | custom-call | flops 1048576 | bytes 1572864 | tf_op jit(solution)/shard_map/word_table/pallas_call | solution.py:261
  17.9 3.6 %first_rows.1 = (bf16[1024,4096]{1,0:T(8,128)(2,1)S(1)}, bf16[1024,1024]{1,0:T(8,128)(2,1)S(1)}, f32[32,8,128]{2,1,0:T(8,128)S(1)}) custom-call(s32[1,1]{1,0:T(1,128)} %bitcast.place_ref, bf16[512,128]{1,0:T(8,128)(2,1)S(1)} %bitcast.9, bf16[1024,256]{1,0:T(8,128)(2,1)S(1)} %get-tuple-element.17.words_ref.refs_2_.refs_1_, ...), custom_call_target="tpu_custom_call" | custom-call | flops 104857600 | bytes 4194304 | tf_op jit(solution)/shard_map/first_rows/pallas_call | solution.py:308
  21.5 0.7 %collective-permute-done.refs_1_ = bf16[512,128]{1,0:T(8,128)(2,1)S(1)} collective-permute-done((bf16[512,128]{1,0:T(8,128)(2,1)S(1)}, bf16[512,128]{1,0:T(8,128)(2,1)S(1)}, u32[]{:S(2)}, u32[]{:S(2)}) %collective-permute-start) | collective-permute-done | bytes 131104 | tf_op jit(solution)/shard_map/ppermute | solution.py:251
  22.2 0.4 %collective-permute-start.1 = (bf16[512,128]{1,0:T(8,128)(2,1)S(1)}, bf16[512,128]{1,0:T(8,128)(2,1)S(1)}, u32[]{:S(2)}, u32[]{:S(2)}) collective-permute-start(bf16[512,128]{1,0:T(8,128)(2,1)S(1)} %collective-permute-done.refs_1_), channel_id=1, source_target_pairs={{0,1},{1,0},{2,3},{3,2},{4,5},{5,4},{6,7},{7,6},{8,9},{9,8},{10,11... | collective-permute-start | bytes 393224 | tf_op jit(solution)/shard_map/ppermute | solution.py:251
  22.7 0.0 collective-permute-done.2.refs_0_
  22.7 7.0 %middle_rows.1 = (bf16[1024,4096]{1,0:T(8,128)(2,1)S(1)}, bf16[1024,1024]{1,0:T(8,128)(2,1)S(1)}, f32[32,8,128]{2,1,0:T(8,128)S(1)}) custom-call(s32[1,1]{1,0:T(1,128)} %bitcast.place_ref, bf16[512,128]{1,0:T(8,128)(2,1)S(1)} %collective-permute-done.2.refs_0_, ...), custom_call_target="tpu_custom_call", output_to_operand_aliasing={{0}: (6, {}), {1}: (7, {}), {2}: (8, {})} | custom-call | flops 209715200 | bytes 8388608 | tf_op jit(solution)/shard_map/middle_rows/pallas_call | solution.py:325
  29.7 0.0 collective-permute-done.1.refs_0_
  29.7 14.6 %last_rows.1 = (f32[8,128]{1,0:T(8,128)}, bf16[1024,4096]{1,0:T(8,128)(2,1)S(1)}, bf16[1024,1024]{1,0:T(8,128)(2,1)S(1)}, f32[32,8,128]{2,1,0:T(8,128)S(1)}) custom-call(s32[1,1]{1,0:T(1,128)} %bitcast.place_ref, bf16[512,128]{1,0:T(8,128)(2,1)S(1)} %collective-permute-done.1.refs_0_, ...), custom_call_target="tpu_custom_call", output_to_operand_aliasing={{1}: (5, {}), {2}: (6, {}), {3}: (7, {})} | custom-call | flops 8589934592 | bytes 8388608 | tf_op jit(solution)/shard_map/last_rows/pallas_call | solution.py:336
Async XLA Ops:
  12.1 10.5 %collective-permute-start.2 = (bf16[512,128]{1,0:T(8,128)(2,1)S(1)}, bf16[512,128]{1,0:T(8,128)(2,1)S(1)}, u32[]{:S(2)}, u32[]{:S(2)}) collective-permute-start(bf16[512,128]{1,0:T(8,128)(2,1)S(1)} %bitcast.7), channel_id=1, source_target_pairs={{0,1},{1,0},{2,3},{3,2},{4,5},{5,4},{6,7},{7,6},{8,9},{9,8},{10,11... | collective-permute-start | bytes 393224 | tf_op jit(solution)/shard_map/ppermute | solution.py:251
  13.7 8.5 %collective-permute-start = (bf16[512,128]{1,0:T(8,128)(2,1)S(1)}, bf16[512,128]{1,0:T(8,128)(2,1)S(1)}, u32[]{:S(2)}, u32[]{:S(2)}) collective-permute-start(bf16[512,128]{1,0:T(8,128)(2,1)S(1)} %bitcast.8), channel_id=1, source_target_pairs={{0,2},{1,3},{2,0},{3,1},{4,6},{5,7},{6,4},{7,5},{8,10},{9,11},{10,... | collective-permute-start | bytes 393224 | tf_op jit(solution)/shard_map/ppermute | solution.py:251
  22.2 7.5 %collective-permute-start.1 = (bf16[512,128]{1,0:T(8,128)(2,1)S(1)}, bf16[512,128]{1,0:T(8,128)(2,1)S(1)}, u32[]{:S(2)}, u32[]{:S(2)}) collective-permute-start(bf16[512,128]{1,0:T(8,128)(2,1)S(1)} %collective-permute-done.refs_1_), channel_id=1, source_target_pairs={{0,1},{1,0},{2,3},{3,2},{4,5},{5,4},{6,7},{7,6},{8,9},{9,8},{10,11... | collective-permute-start | bytes 393224 | tf_op jit(solution)/shard_map/ppermute | solution.py:251

commit v5 on v4

--- a/solution.py
+++ b/solution.py
@@ -9,7 +9,8 @@
 
 LANES = 128
 COLS = 256
-STEP = 512
+STEP = 1024
+ROWS = 16
 LOW = -4.0
 VMEM_LIMIT = 40 * 1024 * 1024
 PARAMS = pltpu.CompilerParams(vmem_limit_bytes=VMEM_LIMIT)
@@ -67,18 +68,24 @@
 def table_kernel(group_ref, book_ref, words_ref, centre_ref, norms_ref):
     width, words = words_ref.shape
     subspaces = norms_ref.shape[0]
-    centres = book_ref[words:, :].astype(jnp.float32)
-    pick = lax.broadcasted_iota(jnp.int32, (centres.shape[0], 1), 0) == group_ref[0, 0]
-    centre = jnp.sum(jnp.where(pick, centres, 0.0), axis=0, keepdims=True)
-    centre = jnp.transpose(jnp.broadcast_to(centre, (LANES, width)))
-    centre_ref[...] = centre
-    turned = jnp.transpose(book_ref[:words, :].astype(jnp.float32))
-    words_ref[...] = turned.astype(jnp.bfloat16)
-    for half in range(words // LANES):
-        lanes = slice(half * LANES, (half + 1) * LANES)
-        table = turned[:, lanes] + centre
-        norms_ref[:, lanes] = jnp.sum(
-            (table * table).reshape(subspaces, width // subspaces, LANES), axis=1
+    sub_width = width // subspaces
+    block = ROWS * sub_width
+    new = lax.broadcasted_iota(jnp.int32, (block, block), 0)
+    old = lax.broadcasted_iota(jnp.int32, (block, block), 1)
+    order = jnp.where(old == (new % ROWS) * sub_width + new // ROWS, 1.0, 0.0).astype(jnp.bfloat16)
+    clusters = book_ref.shape[0] - words
+    pick = lax.broadcasted_iota(jnp.int32, (1, clusters), 1) == group_ref[0, 0]
+    for part in range(width // block):
+        rows = slice(part * block, (part + 1) * block)
+        turned = lax.dot_general(
+            order, book_ref[:, rows], (((1,), (1,)), ((), ())), preferred_element_type=jnp.float32
+        )
+        centre = jnp.sum(jnp.where(pick, turned[:, words:], 0.0), axis=1, keepdims=True)
+        words_ref[rows, :] = turned[:, :words].astype(jnp.bfloat16)
+        centre_ref[rows, :] = jnp.broadcast_to(centre, (block, LANES))
+        table = turned[:, :words] + centre
+        norms_ref[part * ROWS : (part + 1) * ROWS, :] = jnp.sum(
+            (table * table).reshape(sub_width, ROWS, words), axis=0
         )
 
 
@@ -110,7 +117,7 @@
 
 def decode_groups(
     place, first, codes_refs, words_ref, centre_ref, norms_ref,
-    units_ref, left_ref, mark_ref, code_ref, scale_ref, now_ref,
+    units_ref, left_ref, mark_ref, code_ref, scale_ref,
 ):
     slots = left_ref.shape[0]
     owners = units_ref.shape[1] // slots
@@ -129,26 +136,26 @@
 
         def one_group(turn, _):
             start = pl.multiple_of(turn * slots + (first + which) * COLS, COLS)
-            scales = []
             for half in range(2):
                 tile = 2 * (which * owners + turn) + half
-                now_ref[half] = code_ref[tile]
-                scales.append(scale_ref[tile])
-            for sub in range(subspaces):
-                rows = slice(sub * sub_width, (sub + 1) * sub_width)
-                for half in range(2):
-                    code = jnp.broadcast_to(
-                        now_ref[half, sub : sub + 1, :], (sub_width, LANES)
-                    ).astype(jnp.int16)
+                codes = code_ref[tile].astype(jnp.int16)
+                scale = jnp.concatenate([scale_ref[tile]] * (ROWS // 8), axis=0)
+                for part in range(subspaces // ROWS):
+                    code = codes[part * ROWS : (part + 1) * ROWS]
                     low = code & (LANES - 1)
-                    word = jnp.where(
-                        code > LANES - 1,
-                        take_lanes(words_ref[rows, LANES:], low),
-                        take_lanes(words_ref[rows, :LANES], low),
-                    )
-                    embed = word.astype(jnp.float32) + centre_ref[rows, :]
-                    unit = embed * jnp.concatenate([scales[half]] * (sub_width // 8), axis=0)
-                    units_ref[rows, pl.ds(start + half * LANES, LANES)] = unit.astype(jnp.bfloat16)
+                    high = code > LANES - 1
+                    for entry in range(sub_width):
+                        row = (part * sub_width + entry) * ROWS
+                        rows = slice(row, row + ROWS)
+                        word = jnp.where(
+                            high,
+                            take_lanes(words_ref[rows, LANES:], low),
+                            take_lanes(words_ref[rows, :LANES], low),
+                        )
+                        unit = (word.astype(jnp.float32) + centre_ref[rows, :]) * scale
+                        units_ref[rows, pl.ds(start + half * LANES, LANES)] = unit.astype(
+                            jnp.bfloat16
+                        )
             return 0
 
         lax.fori_loop(0, owners, one_group, 0)
@@ -171,12 +178,12 @@
     place = place_ref[0, 0]
     codes_refs, refs = refs[:count], refs[count:]
     table_refs, refs = refs[:3], refs[6:]
-    out_ref, units_ref, left_ref, mark_ref, best_ref, code_ref, scale_ref, now_ref = refs
+    out_ref, units_ref, left_ref, mark_ref, best_ref, code_ref, scale_ref = refs
     slots = left_ref.shape[0]
     owners = units_ref.shape[1] // slots
     decode_groups(
         place, slots // COLS - count, codes_refs, *table_refs,
-        units_ref, left_ref, mark_ref, code_ref, scale_ref, now_ref,
+        units_ref, left_ref, mark_ref, code_ref, scale_ref,
     )
     best_ref[...] = jnp.full(best_ref.shape, LOW, jnp.float32)
 
@@ -283,7 +290,6 @@
         return [
             pltpu.VMEM((2 * members * count, subspaces, LANES), i32),
             pltpu.VMEM((2 * members * count, 8, LANES), f32),
-            pltpu.VMEM((2, subspaces, LANES), i32),
         ]
 
     def decode_cost(count):

time: 44.6 us -> 39.7 us (0.89)
  Pallas kernels: 26.4 us -> 19.9 us
  waiting for transfers between devices: 0.7 us -> 2.33 us
    pallas_call x1, Pallas kernels: 7.02 us -> 4.26 us  [on_device(): pl.pallas_call(functools.partial(middle_kernel, count), out_shape=state_s...]
    pallas_call x1, Pallas kernels: 14.6 us -> 12.2 us  [on_device(): pl.pallas_call(functools.partial(last_kernel, (capacity, clusters, member...]
    ppermute x3, waiting for transfers between devices: 0.7 us -> 2.33 us  [from_member(): return lax.ppermute(block, 'blk', [(i, i ^ mask) for i in range(members)])]
    pallas_call x1, Pallas kernels: 3.61 us -> 2.22 us  [on_device(): units, left, marks = first(place, here, *table)]
  transfers between devices with their start and end apart: 3 -> 3, of which waited for: 1 -> 2; matrix products, arithmetic and copies ran while one was open for 2% -> 3% of each run, Pallas kernels for 25% -> 18%
where the time goes in v5:
time: 39.7 us; the launch traced here: 39.4 us
  Pallas kernels  19.9 us (50%)
  blocking collectives  10.5 us (26%)
  starting transfers between devices  4.61 us (12%)
  waiting for transfers between devices  2.33 us (6%)
  other arithmetic  2.03 us (5%)
    pallas_call x1, Pallas kernels, on_device(): pl.pallas_call(functools.partial(last_kernel, (capacity, clusters, member...  12.2 us
    all_to_all x1, blocking collectives, on_device(): lax.all_to_all(packed, 'cluster', split_axis=0, concat_axis=0, tiled=True)  10.5 us
    ppermute x3, starting transfers between devices, from_member(): return lax.ppermute(block, 'blk', [(i, i ^ mask) for i in range(members)])  4.61 us
    pallas_call x1, Pallas kernels, on_device(): pl.pallas_call(functools.partial(middle_kernel, count), out_shape=state_s...  4.26 us
    ppermute x3, waiting for transfers between devices, from_member(): return lax.ppermute(block, 'blk', [(i, i ^ mask) for i in range(members)])  2.33 us
    pallas_call x1, Pallas kernels, on_device(): units, left, marks = first(place, here, *table)  2.22 us
    concatenate x1, other arithmetic, on_device(): jnp.concatenate([codebook, centroids], axis=0)  1.09 us
    concatenate x1, other arithmetic, on_device(): jnp.concatenate([codes[0, 0], routes.reshape(1, in_rows)], axis=0)  0.93 us
  transfers between devices with their start and end apart: 3, of which 2 were waited for; matrix products, arithmetic and copies ran while one was open for 3% of the time, Pallas kernels for 18%

profile of v5, /device:TPU:0, one launch (start us, length us, event | category | flops | bytes accessed | tf_op | source)
XLA Modules:
  0.0 39.4 jit_solution(5984297803856767792)
XLA Ops:
  0.0 0.9 %pad_add_fusion.rows_ref = s32[65,512]{1,0:T(8,128)S(1)} fusion(s32[1,512]{1,0:T(1,128)} %bitcast.12, s32[64,512]{1,0:T(8,128)} %bitcast.11), kind=kLoop, calls=%fused_computation.1 | loop fusion | flops 33280 | bytes 266240 | tf_op jit(solution)/shard_map/concatenate | solution.py:255
  0.9 0.7 %pack_rows.1 = bf16[512,128]{1,0:T(8,128)(2,1)S(1)} custom-call(s32[65,512]{1,0:T(8,128)S(1)} %pad_add_fusion.rows_ref), custom_call_target="tpu_custom_call" | custom-call | tf_op jit(solution)/shard_map/pack_rows/pallas_call | solution.py:250
  1.6 10.5 %all_to_all.11 = bf16[8,64,128]{2,1,0:T(8,128)(2,1)S(1)} all-to-all(bf16[8,64,128]{2,1,0:T(8,128)(2,1)S(1)} %bitcast.10), channel_id=1, replica_groups=mesh['cluster'=8,'blk'=4] {'cluster'}, dimensions={0} | all-to-all | bytes 262144 | tf_op jit(solution)/shard_map/all_to_all | solution.py:256
  12.1 1.6 %collective-permute-start.2 = (bf16[512,128]{1,0:T(8,128)(2,1)S(1)}, bf16[512,128]{1,0:T(8,128)(2,1)S(1)}, u32[]{:S(2)}, u32[]{:S(2)}) collective-permute-start(bf16[512,128]{1,0:T(8,128)(2,1)S(1)} %bitcast.7), channel_id=1, source_target_pairs={{0,1},{1,0},{2,3},{3,2},{4,5},{5,4},{6,7},{7,6},{8,9},{9,8},{10,11... | collective-permute-start | bytes 393224 | tf_op jit(solution)/shard_map/ppermute | solution.py:258
  13.7 2.6 %collective-permute-start = (bf16[512,128]{1,0:T(8,128)(2,1)S(1)}, bf16[512,128]{1,0:T(8,128)(2,1)S(1)}, u32[]{:S(2)}, u32[]{:S(2)}) collective-permute-start(bf16[512,128]{1,0:T(8,128)(2,1)S(1)} %bitcast.8), channel_id=1, source_target_pairs={{0,2},{1,3},{2,0},{3,1},{4,6},{5,7},{6,4},{7,5},{8,10},{9,11},{10,... | collective-permute-start | bytes 393224 | tf_op jit(solution)/shard_map/ppermute | solution.py:258
  16.3 1.1 %pad_maximum_fusion.book_ref = bf16[264,1024]{1,0:T(8,128)(2,1)S(1)} fusion(bf16[8,1024]{1,0:T(8,128)(2,1)} %param.7, bf16[256,1024]{1,0:T(8,128)(2,1)} %param.6), kind=kLoop, calls=%fused_computation | loop fusion | flops 1081344 | bytes 1081344 | tf_op jit(solution)/shard_map/concatenate | solution.py:281
  17.4 0.5 %word_table.1 = (bf16[1024,256]{1,0:T(8,128)(2,1)S(1)}, f32[1024,128]{1,0:T(8,128)S(1)}, f32[64,256]{1,0:T(8,128)S(1)}) custom-call(s32[1,1]{1,0:T(1,128)} %bitcast.5.group_ref, bf16[264,1024]{1,0:T(8,128)(2,1)S(1)} %pad_maximum_fusion.book_ref), custom_call_target="tpu_custom_call" | custom-call | flops 1048576 | bytes 1572864 | tf_op jit(solution)/shard_map/word_table/pallas_call | solution.py:268
  17.9 2.2 %first_rows.1 = (bf16[1024,4096]{1,0:T(8,128)(2,1)S(1)}, bf16[1024,1024]{1,0:T(8,128)(2,1)S(1)}, f32[32,8,128]{2,1,0:T(8,128)S(1)}) custom-call(s32[1,1]{1,0:T(1,128)} %bitcast.place_ref, bf16[512,128]{1,0:T(8,128)(2,1)S(1)} %bitcast.9, bf16[1024,256]{1,0:T(8,128)(2,1)S(1)} %get-tuple-element.17.words_ref.refs_2_.refs_1_, ...), custom_call_target="tpu_custom_call" | custom-call | flops 104857600 | bytes 4194304 | tf_op jit(solution)/shard_map/first_rows/pallas_call | solution.py:314
  20.2 2.1 %collective-permute-done.refs_1_ = bf16[512,128]{1,0:T(8,128)(2,1)S(1)} collective-permute-done((bf16[512,128]{1,0:T(8,128)(2,1)S(1)}, bf16[512,128]{1,0:T(8,128)(2,1)S(1)}, u32[]{:S(2)}, u32[]{:S(2)}) %collective-permute-start) | collective-permute-done | bytes 131104 | tf_op jit(solution)/shard_map/ppermute | solution.py:258
  22.2 0.4 %collective-permute-start.1 = (bf16[512,128]{1,0:T(8,128)(2,1)S(1)}, bf16[512,128]{1,0:T(8,128)(2,1)S(1)}, u32[]{:S(2)}, u32[]{:S(2)}) collective-permute-start(bf16[512,128]{1,0:T(8,128)(2,1)S(1)} %collective-permute-done.refs_1_), channel_id=1, source_target_pairs={{0,1},{1,0},{2,3},{3,2},{4,5},{5,4},{6,7},{7,6},{8,9},{9,8},{10,11... | collective-permute-start | bytes 393224 | tf_op jit(solution)/shard_map/ppermute | solution.py:258
  22.7 0.0 collective-permute-done.2.refs_0_
  22.7 4.3 %middle_rows.1 = (bf16[1024,4096]{1,0:T(8,128)(2,1)S(1)}, bf16[1024,1024]{1,0:T(8,128)(2,1)S(1)}, f32[32,8,128]{2,1,0:T(8,128)S(1)}) custom-call(s32[1,1]{1,0:T(1,128)} %bitcast.place_ref, bf16[512,128]{1,0:T(8,128)(2,1)S(1)} %collective-permute-done.2.refs_0_, ...), custom_call_target="tpu_custom_call", output_to_operand_aliasing={{0}: (6, {}), {1}: (7, {}), {2}: (8, {})} | custom-call | flops 209715200 | bytes 8388608 | tf_op jit(solution)/shard_map/middle_rows/pallas_call | solution.py:331
  26.9 0.3 collective-permute-done.1.refs_0_
  27.2 12.2 %last_rows.1 = (f32[8,128]{1,0:T(8,128)}, bf16[1024,4096]{1,0:T(8,128)(2,1)S(1)}, bf16[1024,1024]{1,0:T(8,128)(2,1)S(1)}, f32[32,8,128]{2,1,0:T(8,128)S(1)}) custom-call(s32[1,1]{1,0:T(1,128)} %bitcast.place_ref, bf16[512,128]{1,0:T(8,128)(2,1)S(1)} %collective-permute-done.1.refs_0_, ...), custom_call_target="tpu_custom_call", output_to_operand_aliasing={{1}: (5, {}), {2}: (6, {}), {3}: (7, {})} | custom-call | flops 8589934592 | bytes 8388608 | tf_op jit(solution)/shard_map/last_rows/pallas_call | solution.py:342
Async XLA Ops:
  12.1 10.5 %collective-permute-start.2 = (bf16[512,128]{1,0:T(8,128)(2,1)S(1)}, bf16[512,128]{1,0:T(8,128)(2,1)S(1)}, u32[]{:S(2)}, u32[]{:S(2)}) collective-permute-start(bf16[512,128]{1,0:T(8,128)(2,1)S(1)} %bitcast.7), channel_id=1, source_target_pairs={{0,1},{1,0},{2,3},{3,2},{4,5},{5,4},{6,7},{7,6},{8,9},{9,8},{10,11... | collective-permute-start | bytes 393224 | tf_op jit(solution)/shard_map/ppermute | solution.py:258
  13.7 8.5 %collective-permute-start = (bf16[512,128]{1,0:T(8,128)(2,1)S(1)}, bf16[512,128]{1,0:T(8,128)(2,1)S(1)}, u32[]{:S(2)}, u32[]{:S(2)}) collective-permute-start(bf16[512,128]{1,0:T(8,128)(2,1)S(1)} %bitcast.8), channel_id=1, source_target_pairs={{0,2},{1,3},{2,0},{3,1},{4,6},{5,7},{6,4},{7,5},{8,10},{9,11},{10,... | collective-permute-start | bytes 393224 | tf_op jit(solution)/shard_map/ppermute | solution.py:258
  22.2 5.0 %collective-permute-start.1 = (bf16[512,128]{1,0:T(8,128)(2,1)S(1)}, bf16[512,128]{1,0:T(8,128)(2,1)S(1)}, u32[]{:S(2)}, u32[]{:S(2)}) collective-permute-start(bf16[512,128]{1,0:T(8,128)(2,1)S(1)} %collective-permute-done.refs_1_), channel_id=1, source_target_pairs={{0,1},{1,0},{2,3},{3,2},{4,5},{5,4},{6,7},{7,6},{8,9},{9,8},{10,11... | collective-permute-start | bytes 393224 | tf_op jit(solution)/shard_map/ppermute | solution.py:258

commit v6 on v5

--- a/solution.py
+++ b/solution.py
@@ -9,7 +9,6 @@
 
 LANES = 128
 COLS = 256
-STEP = 1024
 ROWS = 16
 LOW = -4.0
 VMEM_LIMIT = 40 * 1024 * 1024
@@ -115,99 +114,193 @@
         scale_ref[2 * group + half] = jnp.broadcast_to(scale, (8, LANES))
 
 
-def decode_groups(
-    place, first, codes_refs, words_ref, centre_ref, norms_ref,
+def unpack_block(
+    place, first, which, codes_ref, norms_ref, code_ref, scale_ref, mark_ref, owners, groups
+):
+    for turn in range(owners):
+        owner = lax.rem(place + turn, owners)
+        unpack_codes(
+            owner_block(codes_ref, owner, owners), norms_ref, code_ref, scale_ref, mark_ref,
+            which * owners + turn, turn * groups + first + which,
+        )
+
+
+def decode_half(code_ref, scale_ref, tile, words_ref, centre_ref, units_ref, start):
+    subspaces = code_ref.shape[1]
+    sub_width = words_ref.shape[0] // subspaces
+    codes = code_ref[tile].astype(jnp.int16)
+    scale = jnp.concatenate([scale_ref[tile]] * (ROWS // 8), axis=0)
+    for part in range(subspaces // ROWS):
+        code = codes[part * ROWS : (part + 1) * ROWS]
+        low = code & (LANES - 1)
+        high = code > LANES - 1
+        for entry in range(sub_width):
+            row = (part * sub_width + entry) * ROWS
+            rows = slice(row, row + ROWS)
+            word = jnp.where(
+                high,
+                take_lanes(words_ref[rows, LANES:], low),
+                take_lanes(words_ref[rows, :LANES], low),
+            )
+            unit = (word.astype(jnp.float32) + centre_ref[rows, :]) * scale
+            units_ref[rows, pl.ds(start, LANES)] = unit.astype(jnp.bfloat16)
+
+
+def turn_own(units_ref, left_ref, block):
+    for half in range(2):
+        start = block * COLS + half * LANES
+        left_ref[start : start + LANES, :] = jnp.transpose(
+            units_ref[:, half * LANES : (half + 1) * LANES]
+        )
+
+
+def score(left_ref, rows, units_ref, start, marks, best_ref):
+    scores = jnp.dot(
+        left_ref[rows, :], units_ref[:, pl.ds(start, COLS)], preferred_element_type=jnp.float32
+    )
+    best = best_ref[rows, :]
+    for part in range(COLS // LANES):
+        best = jnp.maximum(
+            best, jnp.where(marks[part], scores[:, part * LANES : (part + 1) * LANES], LOW)
+        )
+    best_ref[rows, :] = best
+
+
+def own_score(left_ref, units_ref, mark_ref, block, best_ref, mirror_ref):
+    above, count = block * COLS, (block + 1) * COLS
+    scores = jnp.dot(
+        left_ref[:count, :], units_ref[:, :COLS], preferred_element_type=jnp.float32
+    )
+    row_ids = lax.broadcasted_iota(jnp.int32, (COLS, LANES), 0)
+    lane_ids = lax.broadcasted_iota(jnp.int32, (COLS, LANES), 1)
+    for part in range(COLS // LANES):
+        tile = block * (COLS // LANES) + part
+        lanes = slice(part * LANES, (part + 1) * LANES)
+        filled = mark_ref[tile][0:1, :] > 0
+        keep = filled & (row_ids != lane_ids + part * LANES)
+        best_ref[above:count, :] = jnp.maximum(
+            best_ref[above:count, :], jnp.where(keep, scores[above:count, lanes], LOW)
+        )
+        mirror = jnp.full((1, LANES), LOW, jnp.float32)
+        for other in range(above // LANES):
+            rows = slice(other * LANES, (other + 1) * LANES)
+            piece = scores[rows, lanes]
+            best_ref[rows, :] = jnp.maximum(best_ref[rows, :], jnp.where(filled, piece, LOW))
+            row_filled = jnp.transpose(
+                jnp.broadcast_to(mark_ref[other][0:1, :], (LANES, LANES))
+            )
+            mirror = jnp.maximum(
+                mirror,
+                jnp.max(jnp.where(row_filled > 0, piece, LOW), axis=0, keepdims=True),
+            )
+        mirror_ref[tile] = jnp.broadcast_to(mirror, (8, LANES))
+
+
+def marks_of(mark_ref, group):
+    return [mark_ref[2 * group + part][0:1, :] > 0 for part in range(COLS // LANES)]
+
+
+def first_kernel(
+    place_ref, codes_ref, words_ref, centre_ref, norms_ref,
     units_ref, left_ref, mark_ref, code_ref, scale_ref,
 ):
-    slots = left_ref.shape[0]
-    owners = units_ref.shape[1] // slots
-    groups = slots // COLS
-    subspaces = norms_ref.shape[0]
-    sub_width = words_ref.shape[0] // subspaces
+    owners = units_ref.shape[1] // COLS
+    groups = left_ref.shape[0] // COLS
+    unpack_block(
+        place_ref[0, 0], 0, 0, codes_ref, norms_ref, code_ref, scale_ref, mark_ref, owners, groups
+    )
+
+    def one_group(turn, _):
+        for half in range(2):
+            start = pl.multiple_of(turn * COLS + half * LANES, LANES)
+            decode_half(
+                code_ref, scale_ref, 2 * turn + half, words_ref, centre_ref, units_ref, start
+            )
+        return 0
+
+    lax.fori_loop(0, owners, one_group, 0)
+    turn_own(units_ref, left_ref, 0)
+
+
+def blocks_kernel(first, done_rows, place, codes_refs, table_refs, units_refs, state):
+    left_ref, mark_ref, best_ref, mirror_ref, code_ref, scale_ref = state
+    words_ref, centre_ref, norms_ref = table_refs
+    owners = units_refs[0].shape[1] // COLS
+    groups = left_ref.shape[0] // COLS
     for which, codes_ref in enumerate(codes_refs):
-        for turn in range(owners):
-            owner = lax.rem(place + turn, owners)
-            unpack_codes(
-                owner_block(codes_ref, owner, owners), norms_ref, code_ref, scale_ref, mark_ref,
-                which * owners + turn, turn * groups + first + which,
-            )
-
+        unpack_block(
+            place, first, which, codes_ref, norms_ref, code_ref, scale_ref, mark_ref,
+            owners, groups,
+        )
+        for half in range(2):
+            decode_half(
+                code_ref, scale_ref, 2 * which * owners + half, words_ref, centre_ref,
+                units_refs[which + 1], half * LANES,
+            )
+        turn_own(units_refs[which + 1], left_ref, first + which)
     for which in range(len(codes_refs)):
-
-        def one_group(turn, _):
-            start = pl.multiple_of(turn * slots + (first + which) * COLS, COLS)
+        own_score(left_ref, units_refs[which + 1], mark_ref, first + which, best_ref, mirror_ref)
+
+    halves = [slice(0, done_rows // 2), slice(done_rows // 2, done_rows)]
+    for which in range(len(codes_refs)):
+
+        def both(turn, _):
+            column = pl.multiple_of(turn * COLS, LANES)
+            marks = marks_of(mark_ref, turn * groups + first + which - 1)
             for half in range(2):
-                tile = 2 * (which * owners + turn) + half
-                codes = code_ref[tile].astype(jnp.int16)
-                scale = jnp.concatenate([scale_ref[tile]] * (ROWS // 8), axis=0)
-                for part in range(subspaces // ROWS):
-                    code = codes[part * ROWS : (part + 1) * ROWS]
-                    low = code & (LANES - 1)
-                    high = code > LANES - 1
-                    for entry in range(sub_width):
-                        row = (part * sub_width + entry) * ROWS
-                        rows = slice(row, row + ROWS)
-                        word = jnp.where(
-                            high,
-                            take_lanes(words_ref[rows, LANES:], low),
-                            take_lanes(words_ref[rows, :LANES], low),
-                        )
-                        unit = (word.astype(jnp.float32) + centre_ref[rows, :]) * scale
-                        units_ref[rows, pl.ds(start + half * LANES, LANES)] = unit.astype(
-                            jnp.bfloat16
-                        )
+                score(left_ref, halves[half], units_refs[which], column, marks, best_ref)
+                decode_half(
+                    code_ref, scale_ref, 2 * (which * owners + turn) + half,
+                    words_ref, centre_ref, units_refs[which + 1],
+                    pl.multiple_of(turn * COLS + half * LANES, LANES),
+                )
             return 0
 
-        lax.fori_loop(0, owners, one_group, 0)
-        for half in range(2):
-            start = (first + which) * COLS + half * LANES
-            left_ref[start : start + LANES, :] = jnp.transpose(units_ref[:, start : start + LANES])
-
-
-def first_kernel(place_ref, codes_ref, words_ref, centre_ref, norms_ref, *refs):
-    decode_groups(place_ref[0, 0], 0, [codes_ref], words_ref, centre_ref, norms_ref, *refs)
+        lax.fori_loop(1, owners, both, 0)
 
 
 def middle_kernel(count, place_ref, *refs):
     codes_refs, refs = refs[:count], refs[count:]
-    decode_groups(place_ref[0, 0], 1, codes_refs, *refs[:3], *refs[6:])
-
-
-def last_kernel(sizes, place_ref, *refs):
-    capacity, clusters, members, count = sizes
+    table_refs, refs = refs[:3], refs[3:]
+    near_ref, refs = refs[0], refs[3:]
+    units_refs, refs = refs[:count], refs[count:]
+    left_ref, mark_ref, best_ref, mirror_ref, code_ref, scale_ref = refs
+    best_ref[...] = jnp.full(best_ref.shape, LOW, jnp.float32)
+    own_score(left_ref, near_ref, mark_ref, 0, best_ref, mirror_ref)
+    blocks_kernel(
+        1, (count + 1) * COLS, place_ref[0, 0], codes_refs, table_refs,
+        [near_ref, *units_refs], refs,
+    )
+
+
+def last_kernel(sizes, place_ref, codes_ref, *refs):
+    capacity, clusters, members = sizes
     place = place_ref[0, 0]
-    codes_refs, refs = refs[:count], refs[count:]
-    table_refs, refs = refs[:3], refs[6:]
-    out_ref, units_ref, left_ref, mark_ref, best_ref, code_ref, scale_ref = refs
+    table_refs, refs = refs[:3], refs[3:]
+    units_refs, refs = refs[:-12], refs[-8:]
+    out_ref, left_ref, mark_ref, best_ref, mirror_ref, units_ref, code_ref, scale_ref = refs
     slots = left_ref.shape[0]
-    owners = units_ref.shape[1] // slots
-    decode_groups(
-        place, slots // COLS - count, codes_refs, *table_refs,
-        units_ref, left_ref, mark_ref, code_ref, scale_ref,
-    )
-    best_ref[...] = jnp.full(best_ref.shape, LOW, jnp.float32)
-
-    def score(step, _, own):
-        start = pl.multiple_of(step * STEP, STEP)
-        scores = jnp.dot(
-            left_ref[...], units_ref[:, pl.ds(start, STEP)], preferred_element_type=jnp.float32
-        )
-        best = best_ref[...]
-        for part in range(STEP // LANES):
-            keep = mark_ref[step * (STEP // LANES) + part][0:1, :] > 0
-            if own:
-                row_ids = lax.broadcasted_iota(jnp.int32, (slots, LANES), 0)
-                lane_ids = lax.broadcasted_iota(jnp.int32, (slots, LANES), 1)
-                keep = keep & (row_ids != lane_ids + (start + part * LANES))
-            best = jnp.maximum(
-                best, jnp.where(keep, scores[:, part * LANES : (part + 1) * LANES], LOW)
-            )
-        best_ref[...] = best
+    groups = slots // COLS
+    owners = units_ref.shape[1] // COLS
+    blocks_kernel(
+        groups - 1, slots, place, [codes_ref], table_refs, [units_refs[-1], units_ref],
+        (left_ref, mark_ref, best_ref, mirror_ref, code_ref, scale_ref),
+    )
+
+    def rest(turn, _):
+        column = pl.multiple_of(turn * COLS, LANES)
+        score(
+            left_ref, slice(0, slots), units_ref, column,
+            marks_of(mark_ref, turn * groups + groups - 1), best_ref,
+        )
+        for which in range(groups - 2):
+            score(
+                left_ref, slice(slots - COLS, slots), units_refs[which], column,
+                marks_of(mark_ref, turn * groups + which), best_ref,
+            )
         return 0
 
-    own_steps = slots // STEP
-    lax.fori_loop(0, own_steps, functools.partial(score, own=True), 0)
-    lax.fori_loop(own_steps, owners * own_steps, functools.partial(score, own=False), 0)
+    lax.fori_loop(1, owners, rest, 0)
 
     half_rows = capacity // 2
     tiles = slots // LANES
@@ -222,6 +315,7 @@
         best = jnp.max(
             jnp.transpose(best_ref[tile * LANES : (tile + 1) * LANES, :]), axis=0, keepdims=True
         )
+        best = jnp.maximum(best, mirror_ref[tile][0:1, :])
         mark = mark_ref[tile]
         best = jnp.where(mark[0:1, :] > 0, best, 0.0)
         result = jnp.where(
@@ -280,10 +374,12 @@
         name="word_table",
     )(group, jnp.concatenate([codebook, centroids], axis=0))
 
+    units_shape = jax.ShapeDtypeStruct((width, members * COLS), bf16)
     state_shape = (
-        jax.ShapeDtypeStruct((width, members * slots), bf16),
         jax.ShapeDtypeStruct((slots, width), bf16),
         jax.ShapeDtypeStruct((2 * members * groups, 8, LANES), f32),
+        jax.ShapeDtypeStruct((slots, LANES), f32),
+        jax.ShapeDtypeStruct((tiles, 8, LANES), f32),
     )
 
     def code_scratch(count):
@@ -292,21 +388,20 @@
             pltpu.VMEM((2 * members * count, 8, LANES), f32),
         ]
 
-    def decode_cost(count):
+    def cost(flops):
         return pl.CostEstimate(
-            flops=100 * count * members * COLS * width,
-            bytes_accessed=4 * count * members * COLS * width,
-            transcendentals=0,
-        )
-
+            flops=flops, bytes_accessed=16 * slots * width, transcendentals=0
+        )
+
+    scores_flops = 2 * slots * members * slots * width
     first = pl.pallas_call(
         first_kernel,
-        out_shape=state_shape,
+        out_shape=(units_shape, *state_shape[:2]),
         in_specs=[smem] + [vmem] * 4,
         out_specs=(vmem,) * 3,
         scratch_shapes=code_scratch(1),
         compiler_params=PARAMS,
-        cost_estimate=decode_cost(1),
+        cost_estimate=cost(scores_flops // 4),
         name="first_rows",
     )
     whole_groups = half_rows == 16 and clusters * half_rows == LANES
@@ -326,34 +421,29 @@
         every = every.transpose(1, 2, 0, 3, 4).reshape(groups, members * LANES, LANES)
         blocks = list(every)
         units, left, marks = first(place, blocks[0], *table)
-    state = (units, left, marks)
     count = groups - 2
-    state = pl.pallas_call(
+    *more, left, marks, best, mirror = pl.pallas_call(
         functools.partial(middle_kernel, count),
-        out_shape=state_shape,
+        out_shape=(*[units_shape] * count, *state_shape),
         in_specs=[smem] + [vmem] * (count + 6),
-        out_specs=(vmem,) * 3,
+        out_specs=(vmem,) * (count + 4),
         scratch_shapes=code_scratch(count),
-        input_output_aliases={count + 4 + which: which for which in range(3)},
+        input_output_aliases={count + 5 + which: count + which for which in range(2)},
         compiler_params=PARAMS,
-        cost_estimate=decode_cost(count),
+        cost_estimate=cost(scores_flops // 2),
         name="middle_rows",
-    )(place, *blocks[1 : 1 + count], *table, *state)
+    )(place, *blocks[1 : 1 + count], *table, units, left, marks)
     nearest, *_ = pl.pallas_call(
-        functools.partial(last_kernel, (capacity, clusters, members, 1)),
+        functools.partial(last_kernel, (capacity, clusters, members)),
         out_shape=(jax.ShapeDtypeStruct((tiles, LANES), f32), *state_shape),
-        in_specs=[smem] + [vmem] * 7,
-        out_specs=(vmem,) * 4,
-        scratch_shapes=[pltpu.VMEM((slots, LANES), f32)] + code_scratch(1),
-        input_output_aliases={5 + which: 1 + which for which in range(3)},
+        in_specs=[smem] + [vmem] * (groups + 7),
+        out_specs=(vmem,) * 5,
+        scratch_shapes=[pltpu.VMEM((width, members * COLS), bf16)] + code_scratch(1),
+        input_output_aliases={groups + 4 + which: 1 + which for which in range(4)},
         compiler_params=PARAMS,
-        cost_estimate=pl.CostEstimate(
-            flops=2 * slots * members * slots * width,
-            bytes_accessed=8 * slots * width,
-            transcendentals=0,
-        ),
+        cost_estimate=cost(scores_flops),
         name="last_rows",
-    )(place, blocks[groups - 1], *table, *state)
+    )(place, blocks[groups - 1], *table, units, *more, left, marks, best, mirror)
     return nearest.reshape(1, 1, slots)
 
 

time: 39.7 us -> 38.1 us (0.960)
  blocking collectives: 10.5 us -> 0 us
  waiting for transfers between devices: 2.33 us -> 7.63 us
  starting transfers between devices: 4.61 us -> 9.78 us
  Pallas kernels: 19.9 us -> 18.3 us
    all_to_all x1 -> x0, blocking collectives: 10.5 us -> none  [on_device(): lax.all_to_all(packed, 'cluster', split_axis=0, concat_axis=0, tiled=True)]
    all_to_all x0 -> x1, starting transfers between devices: none -> 5.17 us  [on_device(): lax.all_to_all(packed, 'cluster', split_axis=0, concat_axis=0, tiled=True)]
    pallas_call x1, Pallas kernels: 12.2 us -> 7.88 us  [on_device(): pl.pallas_call(functools.partial(last_kernel, (capacity, clusters, member...]
    all_to_all x0 -> x1, waiting for transfers between devices: none -> 3.91 us  [on_device(): lax.all_to_all(packed, 'cluster', split_axis=0, concat_axis=0, tiled=True)]
    pallas_call x1, Pallas kernels: 4.26 us -> 6.31 us  [on_device(): pl.pallas_call(functools.partial(middle_kernel, count), out_shape=(*[unit...]
    ppermute x3, waiting for transfers between devices: 2.33 us -> 3.72 us  [from_member(): return lax.ppermute(block, 'blk', [(i, i ^ mask) for i in range(members)])]
    pallas_call x1, Pallas kernels: 0.7 us -> 1.35 us  [on_device(): pl.pallas_call(functools.partial(pack_kernel, devices, capacity), out_sha...]
  transfers between devices with their start and end apart: 3 -> 4, of which waited for: 2 -> 2; matrix products, arithmetic and copies ran while one was open for 3% -> 3% of each run, Pallas kernels for 18% -> 24%
where the time goes in v6:
time: 38.1 us; the launch traced here: 37.7 us
  Pallas kernels  18.3 us (48%)
  starting transfers between devices  9.78 us (26%)
  waiting for transfers between devices  7.63 us (20%)
  other arithmetic  2.03 us (5%)
    pallas_call x1, Pallas kernels, on_device(): pl.pallas_call(functools.partial(last_kernel, (capacity, clusters, member...  7.88 us
    pallas_call x1, Pallas kernels, on_device(): pl.pallas_call(functools.partial(middle_kernel, count), out_shape=(*[unit...  6.31 us
    all_to_all x1, starting transfers between devices, on_device(): lax.all_to_all(packed, 'cluster', split_axis=0, concat_axis=0, tiled=True)  5.17 us
    ppermute x3, starting transfers between devices, from_member(): return lax.ppermute(block, 'blk', [(i, i ^ mask) for i in range(members)])  4.61 us
    all_to_all x1, waiting for transfers between devices, on_device(): lax.all_to_all(packed, 'cluster', split_axis=0, concat_axis=0, tiled=True)  3.91 us
    ppermute x3, waiting for transfers between devices, from_member(): return lax.ppermute(block, 'blk', [(i, i ^ mask) for i in range(members)])  3.72 us
    pallas_call x1, Pallas kernels, on_device(): units, left, marks = first(place, here, *table)  2.2 us
    pallas_call x1, Pallas kernels, on_device(): pl.pallas_call(functools.partial(pack_kernel, devices, capacity), out_sha...  1.35 us
  transfers between devices with their start and end apart: 4, of which 2 were waited for; matrix products, arithmetic and copies ran while one was open for 3% of the time, Pallas kernels for 24%

profile of v6, /device:TPU:0, one launch (start us, length us, event | category | flops | bytes accessed | tf_op | source)
XLA Modules:
  0.0 37.7 jit_solution(17978771031999988678)
XLA Ops:
  0.0 0.9 %pad_add_fusion.rows_ref = s32[65,512]{1,0:T(8,128)S(1)} fusion(s32[1,512]{1,0:T(1,128)} %bitcast.11, s32[64,512]{1,0:T(8,128)} %bitcast.10), kind=kLoop, calls=%fused_computation.1 | loop fusion | flops 33280 | bytes 266240 | tf_op jit(solution)/shard_map/concatenate | solution.py:349
  0.9 1.4 %pack_rows.1 = bf16[512,128]{1,0:T(8,128)(2,1)} custom-call(s32[65,512]{1,0:T(8,128)S(1)} %pad_add_fusion.rows_ref), custom_call_target="tpu_custom_call" | custom-call | tf_op jit(solution)/shard_map/pack_rows/pallas_call | solution.py:344
  2.3 5.2 %all-to-all-start = ((bf16[8,64,128]{2,1,0:T(8,128)(2,1)}), bf16[8,64,128]{2,1,0:T(8,128)(2,1)S(1)}, u32[]{:S(2)}, u32[]{:S(2)}) async-start(bf16[8,64,128]{2,1,0:T(8,128)(2,1)} %bitcast.3), calls=%async_computation | async-start | bytes 262144 | tf_op jit(solution)/shard_map/all_to_all | solution.py:350
  7.5 1.1 %pad_maximum_fusion.book_ref = bf16[264,1024]{1,0:T(8,128)(2,1)S(1)} fusion(bf16[8,1024]{1,0:T(8,128)(2,1)} %param.7, bf16[256,1024]{1,0:T(8,128)(2,1)} %param.6), kind=kLoop, calls=%fused_computation | loop fusion | flops 1081344 | bytes 1081344 | tf_op jit(solution)/shard_map/concatenate | solution.py:375
  8.6 0.5 %word_table.1 = (bf16[1024,256]{1,0:T(8,128)(2,1)S(1)}, f32[1024,128]{1,0:T(8,128)S(1)}, f32[64,256]{1,0:T(8,128)S(1)}) custom-call(s32[1,1]{1,0:T(1,128)} %bitcast.5.group_ref, bf16[264,1024]{1,0:T(8,128)(2,1)S(1)} %pad_maximum_fusion.book_ref), custom_call_target="tpu_custom_call" | custom-call | flops 1048576 | bytes 1572864 | tf_op jit(solution)/shard_map/word_table/pallas_call | solution.py:362
  9.1 3.9 %all-to-all-done = bf16[8,64,128]{2,1,0:T(8,128)(2,1)S(1)} async-done(((bf16[8,64,128]{2,1,0:T(8,128)(2,1)}), bf16[8,64,128]{2,1,0:T(8,128)(2,1)S(1)}, u32[]{:S(2)}, u32[]{:S(2)}) %all-to-all-start) | async-done | bytes 131104 | tf_op jit(solution)/shard_map/all_to_all | solution.py:350
  13.0 1.6 %collective-permute-start.2 = (bf16[512,128]{1,0:T(8,128)(2,1)S(1)}, bf16[512,128]{1,0:T(8,128)(2,1)S(1)}, u32[]{:S(2)}, u32[]{:S(2)}) collective-permute-start(bf16[512,128]{1,0:T(8,128)(2,1)S(1)} %bitcast.7), channel_id=1, source_target_pairs={{0,1},{1,0},{2,3},{3,2},{4,5},{5,4},{6,7},{7,6},{8,9},{9,8},{10,11... | collective-permute-start | bytes 393224 | tf_op jit(solution)/shard_map/ppermute | solution.py:352
  14.6 2.6 %collective-permute-start = (bf16[512,128]{1,0:T(8,128)(2,1)S(1)}, bf16[512,128]{1,0:T(8,128)(2,1)S(1)}, u32[]{:S(2)}, u32[]{:S(2)}) collective-permute-start(bf16[512,128]{1,0:T(8,128)(2,1)S(1)} %bitcast.8), channel_id=1, source_target_pairs={{0,2},{1,3},{2,0},{3,1},{4,6},{5,7},{6,4},{7,5},{8,10},{9,11},{10,... | collective-permute-start | bytes 393224 | tf_op jit(solution)/shard_map/ppermute | solution.py:352
  17.2 2.2 %first_rows.1 = (bf16[1024,1024]{1,0:T(8,128)(2,1)S(1)}, bf16[1024,1024]{1,0:T(8,128)(2,1)S(1)}, f32[32,8,128]{2,1,0:T(8,128)S(1)}) custom-call(s32[1,1]{1,0:T(1,128)} %bitcast.place_ref, bf16[512,128]{1,0:T(8,128)(2,1)S(1)} %bitcast.9, bf16[1024,256]{1,0:T(8,128)(2,1)S(1)} %get-tuple-element.20.words_ref.refs_2_.refs_0_, ...), custom_call_target="tpu_custom_call" | custom-call | flops 2147483648 | bytes 16777216 | tf_op jit(solution)/shard_map/first_rows/pallas_call | solution.py:409
  19.4 3.7 %collective-permute-done.refs_1_ = bf16[512,128]{1,0:T(8,128)(2,1)S(1)} collective-permute-done((bf16[512,128]{1,0:T(8,128)(2,1)S(1)}, bf16[512,128]{1,0:T(8,128)(2,1)S(1)}, u32[]{:S(2)}, u32[]{:S(2)}) %collective-permute-start) | collective-permute-done | bytes 131104 | tf_op jit(solution)/shard_map/ppermute | solution.py:352
  23.1 0.4 %collective-permute-start.1 = (bf16[512,128]{1,0:T(8,128)(2,1)S(1)}, bf16[512,128]{1,0:T(8,128)(2,1)S(1)}, u32[]{:S(2)}, u32[]{:S(2)}) collective-permute-start(bf16[512,128]{1,0:T(8,128)(2,1)S(1)} %collective-permute-done.refs_1_), channel_id=1, source_target_pairs={{0,1},{1,0},{2,3},{3,2},{4,5},{5,4},{6,7},{7,6},{8,9},{9,8},{10,11... | collective-permute-start | bytes 393224 | tf_op jit(solution)/shard_map/ppermute | solution.py:352
  23.5 0.0 collective-permute-done.2.refs_0_
  23.5 6.3 %middle_rows.1 = (bf16[1024,1024]{1,0:T(8,128)(2,1)S(1)}, bf16[1024,1024]{1,0:T(8,128)(2,1)S(1)}, bf16[1024,1024]{1,0:T(8,128)(2,1)S(1)}, f32[32,8,128]{2,1,0:T(...) custom-call(s32[1,1]{1,0:T(1,128)} %bitcast.place_ref, ...), custom_call_target="tpu_custom_call", output_to_operand_aliasing={{2}: (7, {}), {3}: (8, {})} | custom-call | flops 4294967296 | bytes 16777216 | tf_op jit(solution)/shard_map/middle_rows/pallas_call | solution.py:425
  29.9 0.0 collective-permute-done.1.codes_ref
  29.9 7.9 %last_rows.1 = (f32[8,128]{1,0:T(8,128)}, bf16[1024,1024]{1,0:T(8,128)(2,1)S(1)}, f32[32,8,128]{2,1,0:T(8,128)S(1)}, f32[1024,128]{1,0:T(8,128)S(1)}, f32[8,8,128]{2,1,0:T(8,128)S(1)}) custom-call(s32[1,1]{1,0:T(1,128)} %bitcast.place_ref, ...), custom_call_target="tpu_custom_call", output_to_operand_aliasing={{1}: (8, {}), {2}: (9, {}), {3}: (10, {}), {4}: (11, {})} | custom-call | flops 8589934592 | bytes 16777216 | tf_op jit(solution)/shard_map/last_rows/pallas_call | solution.py:436
Async XLA Ops:
  2.3 10.7 %all-to-all-start = ((bf16[8,64,128]{2,1,0:T(8,128)(2,1)}), bf16[8,64,128]{2,1,0:T(8,128)(2,1)S(1)}, u32[]{:S(2)}, u32[]{:S(2)}) async-start(bf16[8,64,128]{2,1,0:T(8,128)(2,1)} %bitcast.3), calls=%async_computation | async-start | bytes 262144 | tf_op jit(solution)/shard_map/all_to_all | solution.py:350
  13.0 10.5 %collective-permute-start.2 = (bf16[512,128]{1,0:T(8,128)(2,1)S(1)}, bf16[512,128]{1,0:T(8,128)(2,1)S(1)}, u32[]{:S(2)}, u32[]{:S(2)}) collective-permute-start(bf16[512,128]{1,0:T(8,128)(2,1)S(1)} %bitcast.7), channel_id=1, source_target_pairs={{0,1},{1,0},{2,3},{3,2},{4,5},{5,4},{6,7},{7,6},{8,9},{9,8},{10,11... | collective-permute-start | bytes 393224 | tf_op jit(solution)/shard_map/ppermute | solution.py:352
  14.6 8.5 %collective-permute-start = (bf16[512,128]{1,0:T(8,128)(2,1)S(1)}, bf16[512,128]{1,0:T(8,128)(2,1)S(1)}, u32[]{:S(2)}, u32[]{:S(2)}) collective-permute-start(bf16[512,128]{1,0:T(8,128)(2,1)S(1)} %bitcast.8), channel_id=1, source_target_pairs={{0,2},{1,3},{2,0},{3,1},{4,6},{5,7},{6,4},{7,5},{8,10},{9,11},{10,... | collective-permute-start | bytes 393224 | tf_op jit(solution)/shard_map/ppermute | solution.py:352
  23.1 6.8 %collective-permute-start.1 = (bf16[512,128]{1,0:T(8,128)(2,1)S(1)}, bf16[512,128]{1,0:T(8,128)(2,1)S(1)}, u32[]{:S(2)}, u32[]{:S(2)}) collective-permute-start(bf16[512,128]{1,0:T(8,128)(2,1)S(1)} %collective-permute-done.refs_1_), channel_id=1, source_target_pairs={{0,1},{1,0},{2,3},{3,2},{4,5},{5,4},{6,7},{7,6},{8,9},{9,8},{10,11... | collective-permute-start | bytes 393224 | tf_op jit(solution)/shard_map/ppermute | solution.py:352

commit v7 on v6

--- a/solution.py
+++ b/solution.py
@@ -125,13 +125,13 @@
         )
 
 
-def decode_half(code_ref, scale_ref, tile, words_ref, centre_ref, units_ref, start):
+def decode_steps(code_ref, scale_ref, tile, words_ref, centre_ref, units_ref, start):
     subspaces = code_ref.shape[1]
     sub_width = words_ref.shape[0] // subspaces
-    codes = code_ref[tile].astype(jnp.int16)
-    scale = jnp.concatenate([scale_ref[tile]] * (ROWS // 8), axis=0)
-    for part in range(subspaces // ROWS):
-        code = codes[part * ROWS : (part + 1) * ROWS]
+
+    def step(part):
+        code = code_ref[tile, part * ROWS : (part + 1) * ROWS, :].astype(jnp.int16)
+        scale = jnp.concatenate([scale_ref[tile]] * (ROWS // 8), axis=0)
         low = code & (LANES - 1)
         high = code > LANES - 1
         for entry in range(sub_width):
@@ -145,6 +145,22 @@
             unit = (word.astype(jnp.float32) + centre_ref[rows, :]) * scale
             units_ref[rows, pl.ds(start, LANES)] = unit.astype(jnp.bfloat16)
 
+    return [functools.partial(step, part) for part in range(subspaces // ROWS)]
+
+
+def run(steps):
+    for step in steps:
+        step()
+
+
+def mix(some, others):
+    done = 0
+    for place, step in enumerate(some):
+        step()
+        upto = (place + 1) * len(others) // len(some)
+        run(others[done:upto])
+        done = upto
+
 
 def turn_own(units_ref, left_ref, block):
     for half in range(2):
@@ -213,8 +229,10 @@
     def one_group(turn, _):
         for half in range(2):
             start = pl.multiple_of(turn * COLS + half * LANES, LANES)
-            decode_half(
-                code_ref, scale_ref, 2 * turn + half, words_ref, centre_ref, units_ref, start
+            run(
+                decode_steps(
+                    code_ref, scale_ref, 2 * turn + half, words_ref, centre_ref, units_ref, start
+                )
             )
         return 0
 
@@ -222,54 +240,58 @@
     turn_own(units_ref, left_ref, 0)
 
 
-def blocks_kernel(first, done_rows, place, codes_refs, table_refs, units_refs, state):
+def block_kernel(block, place, codes_ref, table_refs, units_refs, state):
     left_ref, mark_ref, best_ref, mirror_ref, code_ref, scale_ref = state
     words_ref, centre_ref, norms_ref = table_refs
-    owners = units_refs[0].shape[1] // COLS
+    units_ref = units_refs[block]
+    owners = units_ref.shape[1] // COLS
     groups = left_ref.shape[0] // COLS
-    for which, codes_ref in enumerate(codes_refs):
-        unpack_block(
-            place, first, which, codes_ref, norms_ref, code_ref, scale_ref, mark_ref,
-            owners, groups,
-        )
+    unpack_block(
+        place, block, 0, codes_ref, norms_ref, code_ref, scale_ref, mark_ref, owners, groups
+    )
+
+    def decoding(turn):
+        steps = []
         for half in range(2):
-            decode_half(
-                code_ref, scale_ref, 2 * which * owners + half, words_ref, centre_ref,
-                units_refs[which + 1], half * LANES,
-            )
-        turn_own(units_refs[which + 1], left_ref, first + which)
-    for which in range(len(codes_refs)):
-        own_score(left_ref, units_refs[which + 1], mark_ref, first + which, best_ref, mirror_ref)
-
-    halves = [slice(0, done_rows // 2), slice(done_rows // 2, done_rows)]
-    for which in range(len(codes_refs)):
-
-        def both(turn, _):
-            column = pl.multiple_of(turn * COLS, LANES)
-            marks = marks_of(mark_ref, turn * groups + first + which - 1)
-            for half in range(2):
-                score(left_ref, halves[half], units_refs[which], column, marks, best_ref)
-                decode_half(
-                    code_ref, scale_ref, 2 * (which * owners + turn) + half,
-                    words_ref, centre_ref, units_refs[which + 1],
-                    pl.multiple_of(turn * COLS + half * LANES, LANES),
-                )
-            return 0
-
-        lax.fori_loop(1, owners, both, 0)
-
-
-def middle_kernel(count, place_ref, *refs):
-    codes_refs, refs = refs[:count], refs[count:]
+            start = turn * COLS + half * LANES
+            if not isinstance(turn, int):
+                start = pl.multiple_of(start, LANES)
+            steps += decode_steps(
+                code_ref, scale_ref, 2 * turn + half, words_ref, centre_ref, units_ref, start
+            )
+        return steps
+
+    run(decoding(0))
+    turn_own(units_ref, left_ref, block)
+    own_score(left_ref, units_ref, mark_ref, block, best_ref, mirror_ref)
+
+    def both(turn, _):
+        column = pl.multiple_of(turn * COLS, LANES)
+        pairs = [(block - 1, chunk) for chunk in range(block + 1)]
+        pairs += [(earlier, block) for earlier in range(block - 1)]
+        scoring = [
+            functools.partial(
+                score, left_ref, slice(chunk * COLS, (chunk + 1) * COLS), units_refs[which],
+                column, marks_of(mark_ref, turn * groups + which), best_ref,
+            )
+            for which, chunk in pairs
+        ]
+        mix(scoring, decoding(turn))
+        return 0
+
+    lax.fori_loop(1, owners, both, 0)
+
+
+def next_kernel(block, place_ref, codes_ref, *refs):
     table_refs, refs = refs[:3], refs[3:]
-    near_ref, refs = refs[0], refs[3:]
-    units_refs, refs = refs[:count], refs[count:]
-    left_ref, mark_ref, best_ref, mirror_ref, code_ref, scale_ref = refs
-    best_ref[...] = jnp.full(best_ref.shape, LOW, jnp.float32)
-    own_score(left_ref, near_ref, mark_ref, 0, best_ref, mirror_ref)
-    blocks_kernel(
-        1, (count + 1) * COLS, place_ref[0, 0], codes_refs, table_refs,
-        [near_ref, *units_refs], refs,
+    units_refs, refs = refs[:block], refs[block:]
+    units_ref, left_ref, mark_ref, best_ref, mirror_ref, code_ref, scale_ref = refs[-7:]
+    if block == 1:
+        best_ref[...] = jnp.full(best_ref.shape, LOW, jnp.float32)
+        own_score(left_ref, units_refs[0], mark_ref, 0, best_ref, mirror_ref)
+    block_kernel(
+        block, place_ref[0, 0], codes_ref, table_refs, [*units_refs, units_ref],
+        (left_ref, mark_ref, best_ref, mirror_ref, code_ref, scale_ref),
     )
 
 
@@ -282,8 +304,8 @@
     slots = left_ref.shape[0]
     groups = slots // COLS
     owners = units_ref.shape[1] // COLS
-    blocks_kernel(
-        groups - 1, slots, place, [codes_ref], table_refs, [units_refs[-1], units_ref],
+    block_kernel(
+        groups - 1, place, codes_ref, table_refs, [*units_refs, units_ref],
         (left_ref, mark_ref, best_ref, mirror_ref, code_ref, scale_ref),
     )
 
@@ -293,11 +315,6 @@
             left_ref, slice(0, slots), units_ref, column,
             marks_of(mark_ref, turn * groups + groups - 1), best_ref,
         )
-        for which in range(groups - 2):
-            score(
-                left_ref, slice(slots - COLS, slots), units_refs[which], column,
-                marks_of(mark_ref, turn * groups + which), best_ref,
-            )
         return 0
 
     lax.fori_loop(1, owners, rest, 0)
@@ -404,15 +421,33 @@
         cost_estimate=cost(scores_flops // 4),
         name="first_rows",
     )
+    def take_in(block, codes_in, units, state):
+        kept = len(state)
+        outs = pl.pallas_call(
+            functools.partial(next_kernel, block),
+            out_shape=(units_shape, *state_shape),
+            in_specs=[smem] + [vmem] * (4 + block + kept),
+            out_specs=(vmem,) * 5,
+            scratch_shapes=code_scratch(1),
+            input_output_aliases={5 + block + which: 1 + which for which in range(kept)},
+            compiler_params=PARAMS,
+            cost_estimate=cost(scores_flops // 4),
+            name="next_rows",
+        )(place, codes_in, *table, *units, *state)
+        return [*units, outs[0]], outs[1:]
+
     whole_groups = half_rows == 16 and clusters * half_rows == LANES
     if whole_groups:
-        units, left, marks = first(place, here, *table)
+        near, *state = first(place, here, *table)
+        units, state = take_in(1, blocks[1], [near], state)
     for mask in masks:
         if mask not in blocks:
             low = mask & -mask
             block = blocks[mask - low]
             if whole_groups:
+                left, marks, best, mirror = state
                 block, marks = lax.optimization_barrier((block, marks))
+                state = (left, marks, best, mirror)
             blocks[mask] = from_member(block, low)
     blocks = [here] + [blocks[mask] for mask in masks]
     if not whole_groups:
@@ -420,19 +455,10 @@
         every = every.transpose(2, 0, 1, 3, 4).reshape(members, groups, LANES // 16, 16, LANES)
         every = every.transpose(1, 2, 0, 3, 4).reshape(groups, members * LANES, LANES)
         blocks = list(every)
-        units, left, marks = first(place, blocks[0], *table)
-    count = groups - 2
-    *more, left, marks, best, mirror = pl.pallas_call(
-        functools.partial(middle_kernel, count),
-        out_shape=(*[units_shape] * count, *state_shape),
-        in_specs=[smem] + [vmem] * (count + 6),
-        out_specs=(vmem,) * (count + 4),
-        scratch_shapes=code_scratch(count),
-        input_output_aliases={count + 5 + which: count + which for which in range(2)},
-        compiler_params=PARAMS,
-        cost_estimate=cost(scores_flops // 2),
-        name="middle_rows",
-    )(place, *blocks[1 : 1 + count], *table, units, left, marks)
+        near, *state = first(place, blocks[0], *table)
+        units, state = take_in(1, blocks[1], [near], state)
+    for block in range(2, groups - 1):
+        units, state = take_in(block, blocks[block], units, state)
     nearest, *_ = pl.pallas_call(
         functools.partial(last_kernel, (capacity, clusters, members)),
         out_shape=(jax.ShapeDtypeStruct((tiles, LANES), f32), *state_shape),
@@ -443,7 +469,7 @@
         compiler_params=PARAMS,
         cost_estimate=cost(scores_flops),
         name="last_rows",
-    )(place, blocks[groups - 1], *table, units, *more, left, marks, best, mirror)
+    )(place, blocks[groups - 1], *table, *units, *state)
     return nearest.reshape(1, 1, slots)
 
 

time: 38.1 us -> 36.4 us (0.955)
  waiting for transfers between devices: 7.63 us -> 5.19 us
  Pallas kernels: 18.3 us -> 19 us
    ppermute x3, waiting for transfers between devices: 3.72 us -> 1.28 us  [from_member(): return lax.ppermute(block, 'blk', [(i, i ^ mask) for i in range(members)])]
    pallas_call x2 -> x3, Pallas kernels: 8.52 us -> 9.14 us  [the longest x2 6.94 us: take_in(): pl.pallas_call(functools.partial(next_kernel, block), out_shape=(units_sh...]
  transfers between devices with their start and end apart: 4 -> 4, of which waited for: 2 -> 4; matrix products, arithmetic and copies ran while one was open for 3% -> 3% of each run, Pallas kernels for 24% -> 27%
where the time goes in v7:
time: 36.4 us; the launch traced here: 36 us
  Pallas kernels  19 us (52%)
  starting transfers between devices  9.79 us (27%)
  waiting for transfers between devices  5.19 us (14%)
  other arithmetic  2.03 us (6%)
    pallas_call x1, Pallas kernels, on_device(): pl.pallas_call(functools.partial(last_kernel, (capacity, clusters, member...  7.97 us
    pallas_call x2, Pallas kernels, take_in(): pl.pallas_call(functools.partial(next_kernel, block), out_shape=(units_sh...  6.94 us
    all_to_all x1, starting transfers between devices, on_device(): lax.all_to_all(packed, 'cluster', split_axis=0, concat_axis=0, tiled=True)  5.17 us
    ppermute x3, starting transfers between devices, from_member(): return lax.ppermute(block, 'blk', [(i, i ^ mask) for i in range(members)])  4.62 us
    all_to_all x1, waiting for transfers between devices, on_device(): lax.all_to_all(packed, 'cluster', split_axis=0, concat_axis=0, tiled=True)  3.91 us
    pallas_call x1, Pallas kernels, on_device(): near, *state = first(place, here, *table)  2.21 us
    pallas_call x1, Pallas kernels, on_device(): pl.pallas_call(functools.partial(pack_kernel, devices, capacity), out_sha...  1.35 us
    ppermute x3, waiting for transfers between devices, from_member(): return lax.ppermute(block, 'blk', [(i, i ^ mask) for i in range(members)])  1.28 us
  transfers between devices with their start and end apart: 4, of which 4 were waited for; matrix products, arithmetic and copies ran while one was open for 3% of the time, Pallas kernels for 27%

profile of v7, /device:TPU:0, one launch (start us, length us, event | category | flops | bytes accessed | tf_op | source)
XLA Modules:
  0.0 36.0 jit_solution(12244164890280713060)
XLA Ops:
  0.0 0.9 %pad_add_fusion.rows_ref = s32[65,512]{1,0:T(8,128)S(1)} fusion(s32[1,512]{1,0:T(1,128)} %bitcast.11, s32[64,512]{1,0:T(8,128)} %bitcast.10), kind=kLoop, calls=%fused_computation.1 | loop fusion | flops 33280 | bytes 266240 | tf_op jit(solution)/shard_map/concatenate | solution.py:366
  0.9 1.4 %pack_rows.1 = bf16[512,128]{1,0:T(8,128)(2,1)} custom-call(s32[65,512]{1,0:T(8,128)S(1)} %pad_add_fusion.rows_ref), custom_call_target="tpu_custom_call" | custom-call | tf_op jit(solution)/shard_map/pack_rows/pallas_call | solution.py:361
  2.3 5.2 %all-to-all-start = ((bf16[8,64,128]{2,1,0:T(8,128)(2,1)}), bf16[8,64,128]{2,1,0:T(8,128)(2,1)S(1)}, u32[]{:S(2)}, u32[]{:S(2)}) async-start(bf16[8,64,128]{2,1,0:T(8,128)(2,1)} %bitcast.3), calls=%async_computation | async-start | bytes 262144 | tf_op jit(solution)/shard_map/all_to_all | solution.py:367
  7.5 1.1 %pad_maximum_fusion.book_ref = bf16[264,1024]{1,0:T(8,128)(2,1)S(1)} fusion(bf16[8,1024]{1,0:T(8,128)(2,1)} %param.7, bf16[256,1024]{1,0:T(8,128)(2,1)} %param.6), kind=kLoop, calls=%fused_computation | loop fusion | flops 1081344 | bytes 1081344 | tf_op jit(solution)/shard_map/concatenate | solution.py:392
  8.6 0.5 %word_table.1 = (bf16[1024,256]{1,0:T(8,128)(2,1)S(1)}, f32[1024,128]{1,0:T(8,128)S(1)}, f32[64,256]{1,0:T(8,128)S(1)}) custom-call(s32[1,1]{1,0:T(1,128)} %bitcast.5.group_ref, bf16[264,1024]{1,0:T(8,128)(2,1)S(1)} %pad_maximum_fusion.book_ref), custom_call_target="tpu_custom_call" | custom-call | flops 1048576 | bytes 1572864 | tf_op jit(solution)/shard_map/word_table/pallas_call | solution.py:379
  9.1 3.9 %all-to-all-done = bf16[8,64,128]{2,1,0:T(8,128)(2,1)S(1)} async-done(((bf16[8,64,128]{2,1,0:T(8,128)(2,1)}), bf16[8,64,128]{2,1,0:T(8,128)(2,1)S(1)}, u32[]{:S(2)}, u32[]{:S(2)}) %all-to-all-start) | async-done | bytes 131104 | tf_op jit(solution)/shard_map/all_to_all | solution.py:367
  13.0 1.6 %collective-permute-start.1 = (bf16[512,128]{1,0:T(8,128)(2,1)S(1)}, bf16[512,128]{1,0:T(8,128)(2,1)S(1)}, u32[]{:S(2)}, u32[]{:S(2)}) collective-permute-start(bf16[512,128]{1,0:T(8,128)(2,1)S(1)} %bitcast.7), channel_id=1, source_target_pairs={{0,1},{1,0},{2,3},{3,2},{4,5},{5,4},{6,7},{7,6},{8,9},{9,8},{10,11... | collective-permute-start | bytes 393224 | tf_op jit(solution)/shard_map/ppermute | solution.py:369
  14.6 2.6 %collective-permute-start = (bf16[512,128]{1,0:T(8,128)(2,1)S(1)}, bf16[512,128]{1,0:T(8,128)(2,1)S(1)}, u32[]{:S(2)}, u32[]{:S(2)}) collective-permute-start(bf16[512,128]{1,0:T(8,128)(2,1)S(1)} %bitcast.8), channel_id=1, source_target_pairs={{0,2},{1,3},{2,0},{3,1},{4,6},{5,7},{6,4},{7,5},{8,10},{9,11},{10,... | collective-permute-start | bytes 393224 | tf_op jit(solution)/shard_map/ppermute | solution.py:369
  17.2 2.2 %first_rows.1 = (bf16[1024,1024]{1,0:T(8,128)(2,1)S(1)}, bf16[1024,1024]{1,0:T(8,128)(2,1)S(1)}, f32[32,8,128]{2,1,0:T(8,128)S(1)}) custom-call(s32[1,1]{1,0:T(1,128)} %bitcast.place_ref, bf16[512,128]{1,0:T(8,128)(2,1)S(1)} %bitcast.9, bf16[1024,256]{1,0:T(8,128)(2,1)S(1)} %get-tuple-element.24.words_ref.refs_0_, ...), custom_call_target="tpu_custom_call" | custom-call | flops 2147483648 | bytes 16777216 | tf_op jit(solution)/shard_map/first_rows/pallas_call | solution.py:441
  19.4 0.4 %collective-permute-done.1.codes_ref = bf16[512,128]{1,0:T(8,128)(2,1)S(1)} collective-permute-done((bf16[512,128]{1,0:T(8,128)(2,1)S(1)}, bf16[512,128]{1,0:T(8,128)(2,1)S(1)}, u32[]{:S(2)}, u32[]{:S(2)}) %collective-permute-start.1) | collective-permute-done | bytes 131104 | tf_op jit(solution)/shard_map/ppermute | solution.py:369
  19.8 3.0 %next_rows.2 = (bf16[1024,1024]{1,0:T(8,128)(2,1)S(1)}, bf16[1024,1024]{1,0:T(8,128)(2,1)S(1)}, f32[32,8,128]{2,1,0:T(8,128)S(1)}, f32[1024,128]{1,0:T(8,128)S(1)}, f32[8,8,128]{2,1,0:T(8,128)S(1)}) custom-call(s32[1,1]{1,0:T(1,128)} %bitcast.place_ref, ...), custom_call_target="tpu_custom_call", output_to_operand_aliasing={{1}: (6, {}), {2}: (7, {})} | custom-call | flops 2147483648 | bytes 16777216 | tf_op jit(solution)/shard_map/next_rows/pallas_call | solution.py:426
  22.8 0.2 collective-permute-done.codes_ref
  23.1 0.4 %collective-permute-start.2 = (bf16[512,128]{1,0:T(8,128)(2,1)S(1)}, bf16[512,128]{1,0:T(8,128)(2,1)S(1)}, u32[]{:S(2)}, u32[]{:S(2)}) collective-permute-start(bf16[512,128]{1,0:T(8,128)(2,1)S(1)} %collective-permute-done.codes_ref), channel_id=1, source_target_pairs={{0,1},{1,0},{2,3},{3,2},{4,5},{5,4},{6,7},{7,6},{8,9},{9,8},{10,11... | collective-permute-start | bytes 393224 | tf_op jit(solution)/shard_map/ppermute | solution.py:369
  23.5 3.9 %next_rows.3 = (bf16[1024,1024]{1,0:T(8,128)(2,1)S(1)}, bf16[1024,1024]{1,0:T(8,128)(2,1)S(1)}, f32[32,8,128]{2,1,0:T(8,128)S(1)}, f32[1024,128]{1,0:T(8,128)S(1)}, f32[8,8,128]{2,1,0:T(8,128)S(1)}) custom-call(s32[1,1]{1,0:T(1,128)} %bitcast.place_ref, ...), custom_call_target="tpu_custom_call", output_to_operand_aliasing={{1}: (7, {}), {2}: (8, {}), {3}: (9, {}), {4}: (10, {})} | custom-call | flops 2147483648 | bytes 16777216 | tf_op jit(solution)/shard_map/next_rows/pallas_call | solution.py:426
  27.5 0.6 %collective-permute-done.2.codes_ref = bf16[512,128]{1,0:T(8,128)(2,1)S(1)} collective-permute-done((bf16[512,128]{1,0:T(8,128)(2,1)S(1)}, bf16[512,128]{1,0:T(8,128)(2,1)S(1)}, u32[]{:S(2)}, u32[]{:S(2)}) %collective-permute-start.2) | collective-permute-done | bytes 131104 | tf_op jit(solution)/shard_map/ppermute | solution.py:369
  28.0 8.0 %last_rows.1 = (f32[8,128]{1,0:T(8,128)}, bf16[1024,1024]{1,0:T(8,128)(2,1)S(1)}, f32[32,8,128]{2,1,0:T(8,128)S(1)}, f32[1024,128]{1,0:T(8,128)S(1)}, f32[8,8,128]{2,1,0:T(8,128)S(1)}) custom-call(s32[1,1]{1,0:T(1,128)} %bitcast.place_ref, ...), custom_call_target="tpu_custom_call", output_to_operand_aliasing={{1}: (8, {}), {2}: (9, {}), {3}: (10, {}), {4}: (11, {})} | custom-call | flops 8589934592 | bytes 16777216 | tf_op jit(solution)/shard_map/last_rows/pallas_call | solution.py:462
Async XLA Ops:
  2.3 10.7 %all-to-all-start = ((bf16[8,64,128]{2,1,0:T(8,128)(2,1)}), bf16[8,64,128]{2,1,0:T(8,128)(2,1)S(1)}, u32[]{:S(2)}, u32[]{:S(2)}) async-start(bf16[8,64,128]{2,1,0:T(8,128)(2,1)} %bitcast.3), calls=%async_computation | async-start | bytes 262144 | tf_op jit(solution)/shard_map/all_to_all | solution.py:367
  13.0 6.8 %collective-permute-start.1 = (bf16[512,128]{1,0:T(8,128)(2,1)S(1)}, bf16[512,128]{1,0:T(8,128)(2,1)S(1)}, u32[]{:S(2)}, u32[]{:S(2)}) collective-permute-start(bf16[512,128]{1,0:T(8,128)(2,1)S(1)} %bitcast.7), channel_id=1, source_target_pairs={{0,1},{1,0},{2,3},{3,2},{4,5},{5,4},{6,7},{7,6},{8,9},{9,8},{10,11... | collective-permute-start | bytes 393224 | tf_op jit(solution)/shard_map/ppermute | solution.py:369
  14.6 8.5 %collective-permute-start = (bf16[512,128]{1,0:T(8,128)(2,1)S(1)}, bf16[512,128]{1,0:T(8,128)(2,1)S(1)}, u32[]{:S(2)}, u32[]{:S(2)}) collective-permute-start(bf16[512,128]{1,0:T(8,128)(2,1)S(1)} %bitcast.8), channel_id=1, source_target_pairs={{0,2},{1,3},{2,0},{3,1},{4,6},{5,7},{6,4},{7,5},{8,10},{9,11},{10,... | collective-permute-start | bytes 393224 | tf_op jit(solution)/shard_map/ppermute | solution.py:369
  23.1 5.0 %collective-permute-start.2 = (bf16[512,128]{1,0:T(8,128)(2,1)S(1)}, bf16[512,128]{1,0:T(8,128)(2,1)S(1)}, u32[]{:S(2)}, u32[]{:S(2)}) collective-permute-start(bf16[512,128]{1,0:T(8,128)(2,1)S(1)} %collective-permute-done.codes_ref), channel_id=1, source_target_pairs={{0,1},{1,0},{2,3},{3,2},{4,5},{5,4},{6,7},{7,6},{8,9},{9,8},{10,11... | collective-permute-start | bytes 393224 | tf_op jit(solution)/shard_map/ppermute | solution.py:369

commit v8 on v7

--- a/solution.py
+++ b/solution.py
@@ -10,6 +10,7 @@
 LANES = 128
 COLS = 256
 ROWS = 16
+HELD = 3
 LOW = -4.0
 VMEM_LIMIT = 40 * 1024 * 1024
 PARAMS = pltpu.CompilerParams(vmem_limit_bytes=VMEM_LIMIT)
@@ -134,6 +135,7 @@
         scale = jnp.concatenate([scale_ref[tile]] * (ROWS // 8), axis=0)
         low = code & (LANES - 1)
         high = code > LANES - 1
+        values = []
         for entry in range(sub_width):
             row = (part * sub_width + entry) * ROWS
             rows = slice(row, row + ROWS)
@@ -143,22 +145,31 @@
                 take_lanes(words_ref[rows, :LANES], low),
             )
             unit = (word.astype(jnp.float32) + centre_ref[rows, :]) * scale
-            units_ref[rows, pl.ds(start, LANES)] = unit.astype(jnp.bfloat16)
-
-    return [functools.partial(step, part) for part in range(subspaces // ROWS)]
-
-
-def run(steps):
-    for step in steps:
-        step()
-
-
-def mix(some, others):
+            values.append((rows, unit.astype(jnp.bfloat16)))
+        return values
+
+    def put(values):
+        for rows, value in values:
+            units_ref[rows, pl.ds(start, LANES)] = value
+
+    return [(functools.partial(step, part), put) for part in range(subspaces // ROWS)]
+
+
+def run(decoding):
+    for step, put in decoding:
+        put(step())
+
+
+def mix(scoring, decoding):
     done = 0
-    for place, step in enumerate(some):
-        step()
-        upto = (place + 1) * len(others) // len(some)
-        run(others[done:upto])
+    for place, score_chunk in enumerate(scoring):
+        upto = (place + 1) * len(decoding) // len(scoring)
+        beside = decoding[done : min(upto, done + HELD)]
+        held = [(step(), put) for step, put in beside]
+        score_chunk()
+        for values, put in held:
+            put(values)
+        run(decoding[done + len(beside) : upto])
         done = upto
 
 
@@ -182,62 +193,40 @@
     best_ref[rows, :] = best
 
 
-def own_score(left_ref, units_ref, mark_ref, block, best_ref, mirror_ref):
-    above, count = block * COLS, (block + 1) * COLS
+def own_score(left_ref, chunk, units_ref, block, mark_ref, best_ref, mirror_ref):
+    start = chunk * COLS
     scores = jnp.dot(
-        left_ref[:count, :], units_ref[:, :COLS], preferred_element_type=jnp.float32
+        left_ref[start : start + COLS, :], units_ref[:, :COLS],
+        preferred_element_type=jnp.float32,
     )
     row_ids = lax.broadcasted_iota(jnp.int32, (COLS, LANES), 0)
     lane_ids = lax.broadcasted_iota(jnp.int32, (COLS, LANES), 1)
+    best = best_ref[start : start + COLS, :]
     for part in range(COLS // LANES):
         tile = block * (COLS // LANES) + part
-        lanes = slice(part * LANES, (part + 1) * LANES)
-        filled = mark_ref[tile][0:1, :] > 0
-        keep = filled & (row_ids != lane_ids + part * LANES)
-        best_ref[above:count, :] = jnp.maximum(
-            best_ref[above:count, :], jnp.where(keep, scores[above:count, lanes], LOW)
-        )
-        mirror = jnp.full((1, LANES), LOW, jnp.float32)
-        for other in range(above // LANES):
-            rows = slice(other * LANES, (other + 1) * LANES)
-            piece = scores[rows, lanes]
-            best_ref[rows, :] = jnp.maximum(best_ref[rows, :], jnp.where(filled, piece, LOW))
-            row_filled = jnp.transpose(
-                jnp.broadcast_to(mark_ref[other][0:1, :], (LANES, LANES))
-            )
-            mirror = jnp.maximum(
-                mirror,
-                jnp.max(jnp.where(row_filled > 0, piece, LOW), axis=0, keepdims=True),
-            )
-        mirror_ref[tile] = jnp.broadcast_to(mirror, (8, LANES))
+        piece = scores[:, part * LANES : (part + 1) * LANES]
+        keep = mark_ref[tile][0:1, :] > 0
+        if chunk == block:
+            keep = keep & (row_ids != lane_ids + part * LANES)
+        best = jnp.maximum(best, jnp.where(keep, piece, LOW))
+        if chunk == 0:
+            mirror = jnp.full((8, LANES), LOW, jnp.float32)
+        else:
+            mirror = mirror_ref[tile]
+        if chunk < block:
+            for other in range(COLS // LANES):
+                row_marks = mark_ref[chunk * (COLS // LANES) + other][0:1, :]
+                row_filled = jnp.transpose(jnp.broadcast_to(row_marks, (LANES, LANES))) > 0
+                across = jnp.where(
+                    row_filled, piece[other * LANES : (other + 1) * LANES], LOW
+                )
+                mirror = jnp.maximum(mirror, jnp.max(across, axis=0, keepdims=True))
+        mirror_ref[tile] = mirror
+    best_ref[start : start + COLS, :] = best
 
 
 def marks_of(mark_ref, group):
     return [mark_ref[2 * group + part][0:1, :] > 0 for part in range(COLS // LANES)]
-
-
-def first_kernel(
-    place_ref, codes_ref, words_ref, centre_ref, norms_ref,
-    units_ref, left_ref, mark_ref, code_ref, scale_ref,
-):
-    owners = units_ref.shape[1] // COLS
-    groups = left_ref.shape[0] // COLS
-    unpack_block(
-        place_ref[0, 0], 0, 0, codes_ref, norms_ref, code_ref, scale_ref, mark_ref, owners, groups
-    )
-
-    def one_group(turn, _):
-        for half in range(2):
-            start = pl.multiple_of(turn * COLS + half * LANES, LANES)
-            run(
-                decode_steps(
-                    code_ref, scale_ref, 2 * turn + half, words_ref, centre_ref, units_ref, start
-                )
-            )
-        return 0
-
-    lax.fori_loop(0, owners, one_group, 0)
-    turn_own(units_ref, left_ref, 0)
 
 
 def block_kernel(block, place, codes_ref, table_refs, units_refs, state):
@@ -250,45 +239,59 @@
         place, block, 0, codes_ref, norms_ref, code_ref, scale_ref, mark_ref, owners, groups
     )
 
+    def column_of(turn, offset=0):
+        column = turn * COLS + offset
+        return column if isinstance(turn, int) else pl.multiple_of(column, LANES)
+
     def decoding(turn):
         steps = []
         for half in range(2):
-            start = turn * COLS + half * LANES
-            if not isinstance(turn, int):
-                start = pl.multiple_of(start, LANES)
             steps += decode_steps(
-                code_ref, scale_ref, 2 * turn + half, words_ref, centre_ref, units_ref, start
+                code_ref, scale_ref, 2 * turn + half, words_ref, centre_ref, units_ref,
+                column_of(turn, half * LANES),
             )
         return steps
 
-    run(decoding(0))
-    turn_own(units_ref, left_ref, block)
-    own_score(left_ref, units_ref, mark_ref, block, best_ref, mirror_ref)
-
-    def both(turn, _):
-        column = pl.multiple_of(turn * COLS, LANES)
-        pairs = [(block - 1, chunk) for chunk in range(block + 1)]
-        pairs += [(earlier, block) for earlier in range(block - 1)]
-        scoring = [
+    def scoring(which, turn, chunks):
+        return [
             functools.partial(
                 score, left_ref, slice(chunk * COLS, (chunk + 1) * COLS), units_refs[which],
-                column, marks_of(mark_ref, turn * groups + which), best_ref,
+                column_of(turn), marks_of(mark_ref, turn * groups + which), best_ref,
             )
-            for which, chunk in pairs
+            for chunk in chunks
         ]
-        mix(scoring, decoding(turn))
+
+    if block == 0:
+        best_ref[...] = jnp.full(best_ref.shape, LOW, jnp.float32)
+        run(decoding(0))
+    else:
+        mix(scoring(block - 1, owners - 1, range(block)), decoding(0))
+    turn_own(units_ref, left_ref, block)
+
+    steps = [
+        functools.partial(
+            own_score, left_ref, chunk, units_ref, block, mark_ref, best_ref, mirror_ref
+        )
+        for chunk in range(block + 1)
+    ]
+    for which in range(block):
+        steps += scoring(which, 1, [block])
+    mix(steps, decoding(1))
+
+    def both(turn, _):
+        steps = scoring(block, turn - 1, range(block + 1))
+        for which in range(block):
+            steps += scoring(which, turn, [block])
+        mix(steps, decoding(turn))
         return 0
 
-    lax.fori_loop(1, owners, both, 0)
+    lax.fori_loop(2, owners, both, 0)
 
 
 def next_kernel(block, place_ref, codes_ref, *refs):
     table_refs, refs = refs[:3], refs[3:]
     units_refs, refs = refs[:block], refs[block:]
     units_ref, left_ref, mark_ref, best_ref, mirror_ref, code_ref, scale_ref = refs[-7:]
-    if block == 1:
-        best_ref[...] = jnp.full(best_ref.shape, LOW, jnp.float32)
-        own_score(left_ref, units_refs[0], mark_ref, 0, best_ref, mirror_ref)
     block_kernel(
         block, place_ref[0, 0], codes_ref, table_refs, [*units_refs, units_ref],
         (left_ref, mark_ref, best_ref, mirror_ref, code_ref, scale_ref),
@@ -309,15 +312,11 @@
         (left_ref, mark_ref, best_ref, mirror_ref, code_ref, scale_ref),
     )
 
-    def rest(turn, _):
-        column = pl.multiple_of(turn * COLS, LANES)
-        score(
-            left_ref, slice(0, slots), units_ref, column,
-            marks_of(mark_ref, turn * groups + groups - 1), best_ref,
-        )
-        return 0
-
-    lax.fori_loop(1, owners, rest, 0)
+    final = (owners - 1) * groups + groups - 1
+    score(
+        left_ref, slice(0, slots), units_ref, (owners - 1) * COLS, marks_of(mark_ref, final),
+        best_ref,
+    )
 
     half_rows = capacity // 2
     tiles = slots // LANES
@@ -411,16 +410,6 @@
         )
 
     scores_flops = 2 * slots * members * slots * width
-    first = pl.pallas_call(
-        first_kernel,
-        out_shape=(units_shape, *state_shape[:2]),
-        in_specs=[smem] + [vmem] * 4,
-        out_specs=(vmem,) * 3,
-        scratch_shapes=code_scratch(1),
-        compiler_params=PARAMS,
-        cost_estimate=cost(scores_flops // 4),
-        name="first_rows",
-    )
     def take_in(block, codes_in, units, state):
         kept = len(state)
         outs = pl.pallas_call(
@@ -432,14 +421,14 @@
             input_output_aliases={5 + block + which: 1 + which for which in range(kept)},
             compiler_params=PARAMS,
             cost_estimate=cost(scores_flops // 4),
-            name="next_rows",
+            name=f"rows_{block}",
         )(place, codes_in, *table, *units, *state)
         return [*units, outs[0]], outs[1:]
 
     whole_groups = half_rows == 16 and clusters * half_rows == LANES
     if whole_groups:
-        near, *state = first(place, here, *table)
-        units, state = take_in(1, blocks[1], [near], state)
+        units, state = take_in(0, here, [], ())
+        units, state = take_in(1, blocks[1], units, state)
     for mask in masks:
         if mask not in blocks:
             low = mask & -mask
@@ -455,8 +444,8 @@
         every = every.transpose(2, 0, 1, 3, 4).reshape(members, groups, LANES // 16, 16, LANES)
         every = every.transpose(1, 2, 0, 3, 4).reshape(groups, members * LANES, LANES)
         blocks = list(every)
-        near, *state = first(place, blocks[0], *table)
-        units, state = take_in(1, blocks[1], [near], state)
+        units, state = take_in(0, blocks[0], [], ())
+        units, state = take_in(1, blocks[1], units, state)
     for block in range(2, groups - 1):
         units, state = take_in(block, blocks[block], units, state)
     nearest, *_ = pl.pallas_call(

time: 36.4 us -> 34.9 us (0.959)
  Pallas kernels: 19 us -> 17.7 us
    pallas_call x2 -> x3, Pallas kernels: 6.94 us -> 9.3 us  [take_in(): pl.pallas_call(functools.partial(next_kernel, block), out_shape=(units_sh...]
    pallas_call x1 -> x0, Pallas kernels: 2.21 us -> none  [on_device(): near, *state = first(place, here, *table)]
    pallas_call x1, Pallas kernels: 7.97 us -> 6.5 us  [on_device(): pl.pallas_call(functools.partial(last_kernel, (capacity, clusters, member...]
  transfers between devices with their start and end apart: 4 -> 4, of which waited for: 4 -> 4; matrix products, arithmetic and copies ran while one was open for 3% -> 3% of each run, Pallas kernels for 27% -> 28%
where the time goes in v8:
time: 34.9 us; the launch traced here: 34.5 us
  Pallas kernels  17.7 us (51%)
  starting transfers between devices  9.79 us (28%)
  waiting for transfers between devices  5.03 us (14%)
  other arithmetic  2.03 us (6%)
    pallas_call x3, Pallas kernels, take_in(): pl.pallas_call(functools.partial(next_kernel, block), out_shape=(units_sh...  9.3 us
    pallas_call x1, Pallas kernels, on_device(): pl.pallas_call(functools.partial(last_kernel, (capacity, clusters, member...  6.5 us
    all_to_all x1, starting transfers between devices, on_device(): lax.all_to_all(packed, 'cluster', split_axis=0, concat_axis=0, tiled=True)  5.17 us
    ppermute x3, starting transfers between devices, from_member(): return lax.ppermute(block, 'blk', [(i, i ^ mask) for i in range(members)])  4.62 us
    all_to_all x1, waiting for transfers between devices, on_device(): lax.all_to_all(packed, 'cluster', split_axis=0, concat_axis=0, tiled=True)  3.91 us
    pallas_call x1, Pallas kernels, on_device(): pl.pallas_call(functools.partial(pack_kernel, devices, capacity), out_sha...  1.35 us
    ppermute x3, waiting for transfers between devices, from_member(): return lax.ppermute(block, 'blk', [(i, i ^ mask) for i in range(members)])  1.12 us
    concatenate x1, other arithmetic, on_device(): jnp.concatenate([codebook, centroids], axis=0)  1.09 us
  transfers between devices with their start and end apart: 4, of which 4 were waited for; matrix products, arithmetic and copies ran while one was open for 3% of the time, Pallas kernels for 28%

profile of v8, /device:TPU:0, one launch (start us, length us, event | category | flops | bytes accessed | tf_op | source)
XLA Modules:
  0.0 34.5 jit_solution(722350988679969341)
XLA Ops:
  0.0 0.9 %pad_add_fusion.rows_ref = s32[65,512]{1,0:T(8,128)S(1)} fusion(s32[1,512]{1,0:T(1,128)} %bitcast.11, s32[64,512]{1,0:T(8,128)} %bitcast.10), kind=kLoop, calls=%fused_computation.1 | loop fusion | flops 33280 | bytes 266240 | tf_op jit(solution)/shard_map/concatenate | solution.py:365
  0.9 1.4 %pack_rows.1 = bf16[512,128]{1,0:T(8,128)(2,1)} custom-call(s32[65,512]{1,0:T(8,128)S(1)} %pad_add_fusion.rows_ref), custom_call_target="tpu_custom_call" | custom-call | tf_op jit(solution)/shard_map/pack_rows/pallas_call | solution.py:360
  2.3 5.2 %all-to-all-start = ((bf16[8,64,128]{2,1,0:T(8,128)(2,1)}), bf16[8,64,128]{2,1,0:T(8,128)(2,1)S(1)}, u32[]{:S(2)}, u32[]{:S(2)}) async-start(bf16[8,64,128]{2,1,0:T(8,128)(2,1)} %bitcast.3), calls=%async_computation | async-start | bytes 262144 | tf_op jit(solution)/shard_map/all_to_all | solution.py:366
  7.5 1.1 %pad_maximum_fusion.book_ref = bf16[264,1024]{1,0:T(8,128)(2,1)S(1)} fusion(bf16[8,1024]{1,0:T(8,128)(2,1)} %param.7, bf16[256,1024]{1,0:T(8,128)(2,1)} %param.6), kind=kLoop, calls=%fused_computation | loop fusion | flops 1081344 | bytes 1081344 | tf_op jit(solution)/shard_map/concatenate | solution.py:391
  8.6 0.5 %word_table.1 = (bf16[1024,256]{1,0:T(8,128)(2,1)S(1)}, f32[1024,128]{1,0:T(8,128)S(1)}, f32[64,256]{1,0:T(8,128)S(1)}) custom-call(s32[1,1]{1,0:T(1,128)} %bitcast.5.group_ref, bf16[264,1024]{1,0:T(8,128)(2,1)S(1)} %pad_maximum_fusion.book_ref), custom_call_target="tpu_custom_call" | custom-call | flops 1048576 | bytes 1572864 | tf_op jit(solution)/shard_map/word_table/pallas_call | solution.py:378
  9.1 3.9 %all-to-all-done = bf16[8,64,128]{2,1,0:T(8,128)(2,1)S(1)} async-done(((bf16[8,64,128]{2,1,0:T(8,128)(2,1)}), bf16[8,64,128]{2,1,0:T(8,128)(2,1)S(1)}, u32[]{:S(2)}, u32[]{:S(2)}) %all-to-all-start) | async-done | bytes 131104 | tf_op jit(solution)/shard_map/all_to_all | solution.py:366
  13.0 1.6 %collective-permute-start.1 = (bf16[512,128]{1,0:T(8,128)(2,1)S(1)}, bf16[512,128]{1,0:T(8,128)(2,1)S(1)}, u32[]{:S(2)}, u32[]{:S(2)}) collective-permute-start(bf16[512,128]{1,0:T(8,128)(2,1)S(1)} %bitcast.7), channel_id=1, source_target_pairs={{0,1},{1,0},{2,3},{3,2},{4,5},{5,4},{6,7},{7,6},{8,9},{9,8},{10,11... | collective-permute-start | bytes 393224 | tf_op jit(solution)/shard_map/ppermute | solution.py:368
  14.6 2.6 %collective-permute-start = (bf16[512,128]{1,0:T(8,128)(2,1)S(1)}, bf16[512,128]{1,0:T(8,128)(2,1)S(1)}, u32[]{:S(2)}, u32[]{:S(2)}) collective-permute-start(bf16[512,128]{1,0:T(8,128)(2,1)S(1)} %bitcast.8), channel_id=1, source_target_pairs={{0,2},{1,3},{2,0},{3,1},{4,6},{5,7},{6,4},{7,5},{8,10},{9,11},{10,... | collective-permute-start | bytes 393224 | tf_op jit(solution)/shard_map/ppermute | solution.py:368
  17.2 2.3 %rows_0.1 = (bf16[1024,1024]{1,0:T(8,128)(2,1)S(1)}, bf16[1024,1024]{1,0:T(8,128)(2,1)S(1)}, f32[32,8,128]{2,1,0:T(8,128)S(1)}, f32[1024,128]{1,0:T(8,128)S(1)}, f32[8,8,128]{2,1,0:T(8,128)S(1)}) custom-call(s32[1,1]{1,0:T(1,128)} %bitcast.place_ref, bf16[512,128]{1,0:T(8,128)(2,1)S(1)} %bitcast.9, bf16[1024,256]{1,0:T(8,128)(2,1)S(1)} %get-tuple-element.26.refs_0_, ...), custom_call_target="tpu_custom_call" | custom-call | flops 2147483648 | bytes 16777216 | tf_op jit(solution)/shard_map/rows_0/pallas_call | solution.py:415
  19.5 0.4 %collective-permute-done.1.codes_ref = bf16[512,128]{1,0:T(8,128)(2,1)S(1)} collective-permute-done((bf16[512,128]{1,0:T(8,128)(2,1)S(1)}, bf16[512,128]{1,0:T(8,128)(2,1)S(1)}, u32[]{:S(2)}, u32[]{:S(2)}) %collective-permute-start.1) | collective-permute-done | bytes 131104 | tf_op jit(solution)/shard_map/ppermute | solution.py:368
  19.8 2.9 %rows_1.1 = (bf16[1024,1024]{1,0:T(8,128)(2,1)S(1)}, bf16[1024,1024]{1,0:T(8,128)(2,1)S(1)}, f32[32,8,128]{2,1,0:T(8,128)S(1)}, f32[1024,128]{1,0:T(8,128)S(1)}, f32[8,8,128]{2,1,0:T(8,128)S(1)}) custom-call(s32[1,1]{1,0:T(1,128)} %bitcast.place_ref, ...), custom_call_target="tpu_custom_call", output_to_operand_aliasing={{1}: (6, {}), {2}: (7, {}), {3}: (8, {}), {4}: (9, {})} | custom-call | flops 2147483648 | bytes 16777216 | tf_op jit(solution)/shard_map/rows_1/pallas_call | solution.py:415
  22.7 0.3 collective-permute-done.codes_ref
  23.1 0.4 %collective-permute-start.2 = (bf16[512,128]{1,0:T(8,128)(2,1)S(1)}, bf16[512,128]{1,0:T(8,128)(2,1)S(1)}, u32[]{:S(2)}, u32[]{:S(2)}) collective-permute-start(bf16[512,128]{1,0:T(8,128)(2,1)S(1)} %collective-permute-done.codes_ref), channel_id=1, source_target_pairs={{0,1},{1,0},{2,3},{3,2},{4,5},{5,4},{6,7},{7,6},{8,9},{9,8},{10,11... | collective-permute-start | bytes 393224 | tf_op jit(solution)/shard_map/ppermute | solution.py:368
  23.5 4.1 %rows_2.1 = (bf16[1024,1024]{1,0:T(8,128)(2,1)S(1)}, bf16[1024,1024]{1,0:T(8,128)(2,1)S(1)}, f32[32,8,128]{2,1,0:T(8,128)S(1)}, f32[1024,128]{1,0:T(8,128)S(1)}, f32[8,8,128]{2,1,0:T(8,128)S(1)}) custom-call(s32[1,1]{1,0:T(1,128)} %bitcast.place_ref, ...), custom_call_target="tpu_custom_call", output_to_operand_aliasing={{1}: (7, {}), {2}: (8, {}), {3}: (9, {}), {4}: (10, {})} | custom-call | flops 2147483648 | bytes 16777216 | tf_op jit(solution)/shard_map/rows_2/pallas_call | solution.py:415
  27.6 0.4 %collective-permute-done.2.codes_ref = bf16[512,128]{1,0:T(8,128)(2,1)S(1)} collective-permute-done((bf16[512,128]{1,0:T(8,128)(2,1)S(1)}, bf16[512,128]{1,0:T(8,128)(2,1)S(1)}, u32[]{:S(2)}, u32[]{:S(2)}) %collective-permute-start.2) | collective-permute-done | bytes 131104 | tf_op jit(solution)/shard_map/ppermute | solution.py:368
  28.0 6.5 %last_rows.1 = (f32[8,128]{1,0:T(8,128)}, bf16[1024,1024]{1,0:T(8,128)(2,1)S(1)}, f32[32,8,128]{2,1,0:T(8,128)S(1)}, f32[1024,128]{1,0:T(8,128)S(1)}, f32[8,8,128]{2,1,0:T(8,128)S(1)}) custom-call(s32[1,1]{1,0:T(1,128)} %bitcast.place_ref, ...), custom_call_target="tpu_custom_call", output_to_operand_aliasing={{1}: (8, {}), {2}: (9, {}), {3}: (10, {}), {4}: (11, {})} | custom-call | flops 8589934592 | bytes 16777216 | tf_op jit(solution)/shard_map/last_rows/pallas_call | solution.py:451
Async XLA Ops:
  2.3 10.7 %all-to-all-start = ((bf16[8,64,128]{2,1,0:T(8,128)(2,1)}), bf16[8,64,128]{2,1,0:T(8,128)(2,1)S(1)}, u32[]{:S(2)}, u32[]{:S(2)}) async-start(bf16[8,64,128]{2,1,0:T(8,128)(2,1)} %bitcast.3), calls=%async_computation | async-start | bytes 262144 | tf_op jit(solution)/shard_map/all_to_all | solution.py:366
  13.0 6.8 %collective-permute-start.1 = (bf16[512,128]{1,0:T(8,128)(2,1)S(1)}, bf16[512,128]{1,0:T(8,128)(2,1)S(1)}, u32[]{:S(2)}, u32[]{:S(2)}) collective-permute-start(bf16[512,128]{1,0:T(8,128)(2,1)S(1)} %bitcast.7), channel_id=1, source_target_pairs={{0,1},{1,0},{2,3},{3,2},{4,5},{5,4},{6,7},{7,6},{8,9},{9,8},{10,11... | collective-permute-start | bytes 393224 | tf_op jit(solution)/shard_map/ppermute | solution.py:368
  14.6 8.5 %collective-permute-start = (bf16[512,128]{1,0:T(8,128)(2,1)S(1)}, bf16[512,128]{1,0:T(8,128)(2,1)S(1)}, u32[]{:S(2)}, u32[]{:S(2)}) collective-permute-start(bf16[512,128]{1,0:T(8,128)(2,1)S(1)} %bitcast.8), channel_id=1, source_target_pairs={{0,2},{1,3},{2,0},{3,1},{4,6},{5,7},{6,4},{7,5},{8,10},{9,11},{10,... | collective-permute-start | bytes 393224 | tf_op jit(solution)/shard_map/ppermute | solution.py:368
  23.1 5.0 %collective-permute-start.2 = (bf16[512,128]{1,0:T(8,128)(2,1)S(1)}, bf16[512,128]{1,0:T(8,128)(2,1)S(1)}, u32[]{:S(2)}, u32[]{:S(2)}) collective-permute-start(bf16[512,128]{1,0:T(8,128)(2,1)S(1)} %collective-permute-done.codes_ref), channel_id=1, source_target_pairs={{0,1},{1,0},{2,3},{3,2},{4,5},{5,4},{6,7},{7,6},{8,9},{9,8},{10,11... | collective-permute-start | bytes 393224 | tf_op jit(solution)/shard_map/ppermute | solution.py:368

commit v9 on v8

--- a/solution.py
+++ b/solution.py
@@ -11,6 +11,7 @@
 COLS = 256
 ROWS = 16
 HELD = 3
+DEPTH = 256
 LOW = -4.0
 VMEM_LIMIT = 40 * 1024 * 1024
 PARAMS = pltpu.CompilerParams(vmem_limit_bytes=VMEM_LIMIT)
@@ -181,10 +182,19 @@
         )
 
 
+def products(left_ref, rows, units_ref, columns):
+    total = None
+    for start in range(0, left_ref.shape[1], DEPTH):
+        depth = slice(start, start + DEPTH)
+        piece = jnp.dot(
+            left_ref[rows, depth], units_ref[depth, columns], preferred_element_type=jnp.float32
+        )
+        total = piece if total is None else total + piece
+    return total
+
+
 def score(left_ref, rows, units_ref, start, marks, best_ref):
-    scores = jnp.dot(
-        left_ref[rows, :], units_ref[:, pl.ds(start, COLS)], preferred_element_type=jnp.float32
-    )
+    scores = products(left_ref, rows, units_ref, pl.ds(start, COLS))
     best = best_ref[rows, :]
     for part in range(COLS // LANES):
         best = jnp.maximum(
@@ -195,10 +205,7 @@
 
 def own_score(left_ref, chunk, units_ref, block, mark_ref, best_ref, mirror_ref):
     start = chunk * COLS
-    scores = jnp.dot(
-        left_ref[start : start + COLS, :], units_ref[:, :COLS],
-        preferred_element_type=jnp.float32,
-    )
+    scores = products(left_ref, slice(start, start + COLS), units_ref, slice(0, COLS))
     row_ids = lax.broadcasted_iota(jnp.int32, (COLS, LANES), 0)
     lane_ids = lax.broadcasted_iota(jnp.int32, (COLS, LANES), 1)
     best = best_ref[start : start + COLS, :]

time: 34.9 us -> 34.9 us (level)
  transfers between devices with their start and end apart: 4 -> 4, of which waited for: 4 -> 4; matrix products, arithmetic and copies ran while one was open for 3% -> 3% of each run, Pallas kernels for 28% -> 29%
where the time goes in v9:
time: 34.9 us; the launch traced here: 34.5 us
  Pallas kernels  17.8 us (51%)
  starting transfers between devices  9.79 us (28%)
  waiting for transfers between devices  4.9 us (14%)
  other arithmetic  2.03 us (6%)
    pallas_call x3, Pallas kernels, take_in(): pl.pallas_call(functools.partial(next_kernel, block), out_shape=(units_sh...  9.43 us
    pallas_call x1, Pallas kernels, on_device(): pl.pallas_call(functools.partial(last_kernel, (capacity, clusters, member...  6.49 us
    all_to_all x1, starting transfers between devices, on_device(): lax.all_to_all(packed, 'cluster', split_axis=0, concat_axis=0, tiled=True)  5.17 us
    ppermute x3, starting transfers between devices, from_member(): return lax.ppermute(block, 'blk', [(i, i ^ mask) for i in range(members)])  4.62 us
    all_to_all x1, waiting for transfers between devices, on_device(): lax.all_to_all(packed, 'cluster', split_axis=0, concat_axis=0, tiled=True)  3.91 us
    pallas_call x1, Pallas kernels, on_device(): pl.pallas_call(functools.partial(pack_kernel, devices, capacity), out_sha...  1.35 us
    concatenate x1, other arithmetic, on_device(): jnp.concatenate([codebook, centroids], axis=0)  1.09 us
    ppermute x3, waiting for transfers between devices, from_member(): return lax.ppermute(block, 'blk', [(i, i ^ mask) for i in range(members)])  0.99 us
  transfers between devices with their start and end apart: 4, of which 4 were waited for; matrix products, arithmetic and copies ran while one was open for 3% of the time, Pallas kernels for 29%

profile of v9, /device:TPU:0, one launch (start us, length us, event | category | flops | bytes accessed | tf_op | source)
XLA Modules:
  0.0 34.5 jit_solution(15821989527900171026)
XLA Ops:
  0.0 0.9 %pad_add_fusion.rows_ref = s32[65,512]{1,0:T(8,128)S(1)} fusion(s32[1,512]{1,0:T(1,128)} %bitcast.11, s32[64,512]{1,0:T(8,128)} %bitcast.10), kind=kLoop, calls=%fused_computation.1 | loop fusion | flops 33280 | bytes 266240 | tf_op jit(solution)/shard_map/concatenate | solution.py:372
  0.9 1.4 %pack_rows.1 = bf16[512,128]{1,0:T(8,128)(2,1)} custom-call(s32[65,512]{1,0:T(8,128)S(1)} %pad_add_fusion.rows_ref), custom_call_target="tpu_custom_call" | custom-call | tf_op jit(solution)/shard_map/pack_rows/pallas_call | solution.py:367
  2.3 5.2 %all-to-all-start = ((bf16[8,64,128]{2,1,0:T(8,128)(2,1)}), bf16[8,64,128]{2,1,0:T(8,128)(2,1)S(1)}, u32[]{:S(2)}, u32[]{:S(2)}) async-start(bf16[8,64,128]{2,1,0:T(8,128)(2,1)} %bitcast.3), calls=%async_computation | async-start | bytes 262144 | tf_op jit(solution)/shard_map/all_to_all | solution.py:373
  7.5 1.1 %pad_maximum_fusion.book_ref = bf16[264,1024]{1,0:T(8,128)(2,1)S(1)} fusion(bf16[8,1024]{1,0:T(8,128)(2,1)} %param.7, bf16[256,1024]{1,0:T(8,128)(2,1)} %param.6), kind=kLoop, calls=%fused_computation | loop fusion | flops 1081344 | bytes 1081344 | tf_op jit(solution)/shard_map/concatenate | solution.py:398
  8.6 0.5 %word_table.1 = (bf16[1024,256]{1,0:T(8,128)(2,1)S(1)}, f32[1024,128]{1,0:T(8,128)S(1)}, f32[64,256]{1,0:T(8,128)S(1)}) custom-call(s32[1,1]{1,0:T(1,128)} %bitcast.5.group_ref, bf16[264,1024]{1,0:T(8,128)(2,1)S(1)} %pad_maximum_fusion.book_ref), custom_call_target="tpu_custom_call" | custom-call | flops 1048576 | bytes 1572864 | tf_op jit(solution)/shard_map/word_table/pallas_call | solution.py:385
  9.1 3.9 %all-to-all-done = bf16[8,64,128]{2,1,0:T(8,128)(2,1)S(1)} async-done(((bf16[8,64,128]{2,1,0:T(8,128)(2,1)}), bf16[8,64,128]{2,1,0:T(8,128)(2,1)S(1)}, u32[]{:S(2)}, u32[]{:S(2)}) %all-to-all-start) | async-done | bytes 131104 | tf_op jit(solution)/shard_map/all_to_all | solution.py:373
  13.0 1.6 %collective-permute-start.1 = (bf16[512,128]{1,0:T(8,128)(2,1)S(1)}, bf16[512,128]{1,0:T(8,128)(2,1)S(1)}, u32[]{:S(2)}, u32[]{:S(2)}) collective-permute-start(bf16[512,128]{1,0:T(8,128)(2,1)S(1)} %bitcast.7), channel_id=1, source_target_pairs={{0,1},{1,0},{2,3},{3,2},{4,5},{5,4},{6,7},{7,6},{8,9},{9,8},{10,11... | collective-permute-start | bytes 393224 | tf_op jit(solution)/shard_map/ppermute | solution.py:375
  14.6 2.6 %collective-permute-start = (bf16[512,128]{1,0:T(8,128)(2,1)S(1)}, bf16[512,128]{1,0:T(8,128)(2,1)S(1)}, u32[]{:S(2)}, u32[]{:S(2)}) collective-permute-start(bf16[512,128]{1,0:T(8,128)(2,1)S(1)} %bitcast.8), channel_id=1, source_target_pairs={{0,2},{1,3},{2,0},{3,1},{4,6},{5,7},{6,4},{7,5},{8,10},{9,11},{10,... | collective-permute-start | bytes 393224 | tf_op jit(solution)/shard_map/ppermute | solution.py:375
  17.2 2.3 %rows_0.1 = (bf16[1024,1024]{1,0:T(8,128)(2,1)S(1)}, bf16[1024,1024]{1,0:T(8,128)(2,1)S(1)}, f32[32,8,128]{2,1,0:T(8,128)S(1)}, f32[1024,128]{1,0:T(8,128)S(1)}, f32[8,8,128]{2,1,0:T(8,128)S(1)}) custom-call(s32[1,1]{1,0:T(1,128)} %bitcast.place_ref, bf16[512,128]{1,0:T(8,128)(2,1)S(1)} %bitcast.9, bf16[1024,256]{1,0:T(8,128)(2,1)S(1)} %get-tuple-element.26.refs_0_, ...), custom_call_target="tpu_custom_call" | custom-call | flops 2147483648 | bytes 16777216 | tf_op jit(solution)/shard_map/rows_0/pallas_call | solution.py:422
  19.4 0.4 %collective-permute-done.1.codes_ref = bf16[512,128]{1,0:T(8,128)(2,1)S(1)} collective-permute-done((bf16[512,128]{1,0:T(8,128)(2,1)S(1)}, bf16[512,128]{1,0:T(8,128)(2,1)S(1)}, u32[]{:S(2)}, u32[]{:S(2)}) %collective-permute-start.1) | collective-permute-done | bytes 131104 | tf_op jit(solution)/shard_map/ppermute | solution.py:375
  19.8 3.0 %rows_1.1 = (bf16[1024,1024]{1,0:T(8,128)(2,1)S(1)}, bf16[1024,1024]{1,0:T(8,128)(2,1)S(1)}, f32[32,8,128]{2,1,0:T(8,128)S(1)}, f32[1024,128]{1,0:T(8,128)S(1)}, f32[8,8,128]{2,1,0:T(8,128)S(1)}) custom-call(s32[1,1]{1,0:T(1,128)} %bitcast.place_ref, ...), custom_call_target="tpu_custom_call", output_to_operand_aliasing={{1}: (6, {}), {2}: (7, {}), {3}: (8, {}), {4}: (9, {})} | custom-call | flops 2147483648 | bytes 16777216 | tf_op jit(solution)/shard_map/rows_1/pallas_call | solution.py:422
  22.8 0.3 collective-permute-done.codes_ref
  23.1 0.4 %collective-permute-start.2 = (bf16[512,128]{1,0:T(8,128)(2,1)S(1)}, bf16[512,128]{1,0:T(8,128)(2,1)S(1)}, u32[]{:S(2)}, u32[]{:S(2)}) collective-permute-start(bf16[512,128]{1,0:T(8,128)(2,1)S(1)} %collective-permute-done.codes_ref), channel_id=1, source_target_pairs={{0,1},{1,0},{2,3},{3,2},{4,5},{5,4},{6,7},{7,6},{8,9},{9,8},{10,11... | collective-permute-start | bytes 393224 | tf_op jit(solution)/shard_map/ppermute | solution.py:375
  23.5 4.2 %rows_2.1 = (bf16[1024,1024]{1,0:T(8,128)(2,1)S(1)}, bf16[1024,1024]{1,0:T(8,128)(2,1)S(1)}, f32[32,8,128]{2,1,0:T(8,128)S(1)}, f32[1024,128]{1,0:T(8,128)S(1)}, f32[8,8,128]{2,1,0:T(8,128)S(1)}) custom-call(s32[1,1]{1,0:T(1,128)} %bitcast.place_ref, ...), custom_call_target="tpu_custom_call", output_to_operand_aliasing={{1}: (7, {}), {2}: (8, {}), {3}: (9, {}), {4}: (10, {})} | custom-call | flops 2147483648 | bytes 16777216 | tf_op jit(solution)/shard_map/rows_2/pallas_call | solution.py:422
  27.7 0.3 collective-permute-done.2.codes_ref
  28.0 6.5 %last_rows.1 = (f32[8,128]{1,0:T(8,128)}, bf16[1024,1024]{1,0:T(8,128)(2,1)S(1)}, f32[32,8,128]{2,1,0:T(8,128)S(1)}, f32[1024,128]{1,0:T(8,128)S(1)}, f32[8,8,128]{2,1,0:T(8,128)S(1)}) custom-call(s32[1,1]{1,0:T(1,128)} %bitcast.place_ref, ...), custom_call_target="tpu_custom_call", output_to_operand_aliasing={{1}: (8, {}), {2}: (9, {}), {3}: (10, {}), {4}: (11, {})} | custom-call | flops 8589934592 | bytes 16777216 | tf_op jit(solution)/shard_map/last_rows/pallas_call | solution.py:458
Async XLA Ops:
  2.3 10.7 %all-to-all-start = ((bf16[8,64,128]{2,1,0:T(8,128)(2,1)}), bf16[8,64,128]{2,1,0:T(8,128)(2,1)S(1)}, u32[]{:S(2)}, u32[]{:S(2)}) async-start(bf16[8,64,128]{2,1,0:T(8,128)(2,1)} %bitcast.3), calls=%async_computation | async-start | bytes 262144 | tf_op jit(solution)/shard_map/all_to_all | solution.py:373
  13.0 6.8 %collective-permute-start.1 = (bf16[512,128]{1,0:T(8,128)(2,1)S(1)}, bf16[512,128]{1,0:T(8,128)(2,1)S(1)}, u32[]{:S(2)}, u32[]{:S(2)}) collective-permute-start(bf16[512,128]{1,0:T(8,128)(2,1)S(1)} %bitcast.7), channel_id=1, source_target_pairs={{0,1},{1,0},{2,3},{3,2},{4,5},{5,4},{6,7},{7,6},{8,9},{9,8},{10,11... | collective-permute-start | bytes 393224 | tf_op jit(solution)/shard_map/ppermute | solution.py:375
  14.6 8.5 %collective-permute-start = (bf16[512,128]{1,0:T(8,128)(2,1)S(1)}, bf16[512,128]{1,0:T(8,128)(2,1)S(1)}, u32[]{:S(2)}, u32[]{:S(2)}) collective-permute-start(bf16[512,128]{1,0:T(8,128)(2,1)S(1)} %bitcast.8), channel_id=1, source_target_pairs={{0,2},{1,3},{2,0},{3,1},{4,6},{5,7},{6,4},{7,5},{8,10},{9,11},{10,... | collective-permute-start | bytes 393224 | tf_op jit(solution)/shard_map/ppermute | solution.py:375
  23.1 5.0 %collective-permute-start.2 = (bf16[512,128]{1,0:T(8,128)(2,1)S(1)}, bf16[512,128]{1,0:T(8,128)(2,1)S(1)}, u32[]{:S(2)}, u32[]{:S(2)}) collective-permute-start(bf16[512,128]{1,0:T(8,128)(2,1)S(1)} %collective-permute-done.codes_ref), channel_id=1, source_target_pairs={{0,1},{1,0},{2,3},{3,2},{4,5},{5,4},{6,7},{7,6},{8,9},{9,8},{10,11... | collective-permute-start | bytes 393224 | tf_op jit(solution)/shard_map/ppermute | solution.py:375

commit v10 on v8

--- a/solution.py
+++ b/solution.py
@@ -11,9 +11,11 @@
 COLS = 256
 ROWS = 16
 HELD = 3
+CHUNK = 128
 LOW = -4.0
 VMEM_LIMIT = 40 * 1024 * 1024
 PARAMS = pltpu.CompilerParams(vmem_limit_bytes=VMEM_LIMIT)
+PACK_PARAMS = pltpu.CompilerParams(vmem_limit_bytes=60 * 1024 * 1024)
 
 
 LANE_LOOKUP = lax.GatherDimensionNumbers(
@@ -32,37 +34,52 @@
     )
 
 
-def pack_kernel(devices, capacity, rows_ref, out_ref):
-    subspaces = rows_ref.shape[0] - 1
-    in_rows = rows_ref.shape[1]
+def pack_kernel(
+    devices, capacity, codes_any, routes_any, out_any, codes_ref, routes_ref, out_ref, semaphores
+):
+    routes_in = pltpu.make_async_copy(routes_any, routes_ref, semaphores.at[0])
+    codes_in = pltpu.make_async_copy(codes_any, codes_ref, semaphores.at[1])
+    routes_in.start()
+    codes_in.start()
+    in_rows = codes_ref.shape[1]
     half_rows = capacity // 2
-    targets = rows_ref[subspaces:, :]
-    hot = lax.broadcasted_iota(jnp.int32, (devices, in_rows), 0) == targets
-    hot32 = jnp.where(hot, 1.0, 0.0)
     earlier = (
         lax.broadcasted_iota(jnp.int32, (in_rows, in_rows), 0)
         < lax.broadcasted_iota(jnp.int32, (in_rows, in_rows), 1)
     )
+    earlier = jnp.where(earlier, 1.0, 0.0).astype(jnp.bfloat16)
+    routes_in.wait()
+    targets = routes_ref[...]
+    hot = lax.broadcasted_iota(jnp.int32, (devices, in_rows), 0) == targets
+    hot32 = jnp.where(hot, 1.0, 0.0)
     running = jnp.dot(
-        hot32.astype(jnp.bfloat16),
-        jnp.where(earlier, 1.0, 0.0).astype(jnp.bfloat16),
-        preferred_element_type=jnp.float32,
+        hot32.astype(jnp.bfloat16), earlier, preferred_element_type=jnp.float32
     )
     position = jnp.sum(hot32 * running, axis=0, keepdims=True).astype(jnp.int32)
     second = position >= half_rows
     key = targets * half_rows + jnp.where(second, position - half_rows, position)
-    out_rows = devices * half_rows
-    row_ids = lax.broadcasted_iota(jnp.int32, (out_rows, in_rows), 0)
-    values = (rows_ref[:subspaces, :] + 1).astype(jnp.bfloat16)
-    halves = []
-    for wanted in (jnp.where(second, -1, key), jnp.where(second, key, -1)):
-        move = jnp.where(row_ids == wanted, 1.0, 0.0).astype(jnp.bfloat16)
-        halves.append(
-            lax.dot_general(
-                move, values, (((1,), (1,)), ((), ())), preferred_element_type=jnp.float32
+    codes_in.wait()
+    values = (codes_ref[...] + 1).astype(jnp.bfloat16)
+    out_rows = out_ref.shape[0] // 2
+    copies = []
+    for part in range(2):
+        rows = slice(part * out_rows, (part + 1) * out_rows)
+        row_ids = lax.broadcasted_iota(jnp.int32, (out_rows, in_rows), 0) + part * out_rows
+        halves = []
+        for wanted in (jnp.where(second, -1, key), jnp.where(second, key, -1)):
+            move = jnp.where(row_ids == wanted, 1.0, 0.0).astype(jnp.bfloat16)
+            halves.append(
+                lax.dot_general(
+                    move, values, (((1,), (1,)), ((), ())), preferred_element_type=jnp.float32
+                )
             )
-        )
-    out_ref[...] = jnp.concatenate(halves, axis=1).astype(jnp.bfloat16)
+        out_ref[rows, :] = jnp.concatenate(halves, axis=1).astype(jnp.bfloat16)
+        copies.append(
+            pltpu.make_async_copy(out_ref.at[rows], out_any.at[rows], semaphores.at[2 + part])
+        )
+        copies[part].start()
+    for copy in copies:
+        copy.wait()
 
 
 def table_kernel(group_ref, book_ref, words_ref, centre_ref, norms_ref):
@@ -255,10 +272,11 @@
     def scoring(which, turn, chunks):
         return [
             functools.partial(
-                score, left_ref, slice(chunk * COLS, (chunk + 1) * COLS), units_refs[which],
+                score, left_ref, slice(start, start + CHUNK), units_refs[which],
                 column_of(turn), marks_of(mark_ref, turn * groups + which), best_ref,
             )
             for chunk in chunks
+            for start in range(chunk * COLS, (chunk + 1) * COLS, CHUNK)
         ]
 
     if block == 0:
@@ -357,12 +375,21 @@
     smem = pl.BlockSpec(memory_space=pltpu.SMEM)
     vmem = pl.BlockSpec(memory_space=pltpu.VMEM)
 
+    anywhere = pl.BlockSpec(memory_space=pl.ANY)
     packed = pl.pallas_call(
         functools.partial(pack_kernel, devices, capacity),
         out_shape=jax.ShapeDtypeStruct((in_rows, 2 * subspaces), bf16),
-        compiler_params=PARAMS,
+        in_specs=[anywhere] * 2,
+        out_specs=anywhere,
+        scratch_shapes=[
+            pltpu.VMEM((subspaces, in_rows), i32),
+            pltpu.VMEM((1, in_rows), i32),
+            pltpu.VMEM((in_rows, 2 * subspaces), bf16),
+            pltpu.SemaphoreType.DMA((4,)),
+        ],
+        compiler_params=PACK_PARAMS,
         name="pack_rows",
-    )(jnp.concatenate([codes[0, 0], routes.reshape(1, in_rows)], axis=0))
+    )(codes[0, 0], routes.reshape(1, in_rows))
     here = lax.all_to_all(packed, "cluster", split_axis=0, concat_axis=0, tiled=True)
     def from_member(block, mask):
         return lax.ppermute(block, "blk", [(i, i ^ mask) for i in range(members)])

time: 34.9 us -> 35.2 us (level)
  Pallas kernels: 17.7 us -> 19.6 us
  other arithmetic: 2.03 us -> 1.09 us
  waiting for transfers between devices: 5.03 us -> 4.28 us
    pallas_call x3, Pallas kernels: 9.3 us -> 10.3 us  [take_in(): pl.pallas_call(functools.partial(next_kernel, block), out_shape=(units_sh...]
    concatenate x1 -> x0, other arithmetic: 0.93 us -> none  [on_device(): jnp.concatenate([codes[0, 0], routes.reshape(1, in_rows)], axis=0)]
    ppermute x3, waiting for transfers between devices: 1.12 us -> 0.38 us  [from_member(): return lax.ppermute(block, 'blk', [(i, i ^ mask) for i in range(members)])]
    pallas_call x1, Pallas kernels: 1.35 us -> 2.08 us  [on_device(): pl.pallas_call(functools.partial(pack_kernel, devices, capacity), out_sha...]
  transfers between devices with their start and end apart: 4 -> 4, of which waited for: 4 -> 3; matrix products, arithmetic and copies ran while one was open for 3% -> 3% of each run, Pallas kernels for 28% -> 31%
where the time goes in v10:
time: 35.2 us; the launch traced here: 34.8 us
  Pallas kernels  19.6 us (56%)
  starting transfers between devices  9.82 us (28%)
  waiting for transfers between devices  4.28 us (12%)
  other arithmetic  1.09 us (3%)
    pallas_call x3, Pallas kernels, take_in(): pl.pallas_call(functools.partial(next_kernel, block), out_shape=(units_sh...  10.3 us
    pallas_call x1, Pallas kernels, on_device(): pl.pallas_call(functools.partial(last_kernel, (capacity, clusters, member...  6.66 us
    all_to_all x1, starting transfers between devices, on_device(): lax.all_to_all(packed, 'cluster', split_axis=0, concat_axis=0, tiled=True)  5.19 us
    ppermute x3, starting transfers between devices, from_member(): return lax.ppermute(block, 'blk', [(i, i ^ mask) for i in range(members)])  4.63 us
    all_to_all x1, waiting for transfers between devices, on_device(): lax.all_to_all(packed, 'cluster', split_axis=0, concat_axis=0, tiled=True)  3.91 us
    pallas_call x1, Pallas kernels, on_device(): pl.pallas_call(functools.partial(pack_kernel, devices, capacity), out_sha...  2.08 us
    concatenate x1, other arithmetic, on_device(): jnp.concatenate([codebook, centroids], axis=0)  1.09 us
  transfers between devices with their start and end apart: 4, of which 3 were waited for; matrix products, arithmetic and copies ran while one was open for 3% of the time, Pallas kernels for 31%

profile of v10, /device:TPU:0, one launch (start us, length us, event | category | flops | bytes accessed | tf_op | source)
XLA Modules:
  0.0 34.8 jit_solution(15228508994246458950)
XLA Ops:
  0.0 2.1 %pack_rows.1 = bf16[512,128]{1,0:T(8,128)(2,1)} custom-call(s32[64,512]{1,0:T(8,128)} %bitcast.11, s32[1,512]{1,0:T(1,128)} %bitcast.12), custom_call_target="tpu_custom_call" | custom-call | tf_op jit(solution)/shard_map/pack_rows/pallas_call | solution.py:379
  2.1 5.2 %all-to-all-start = ((bf16[8,64,128]{2,1,0:T(8,128)(2,1)}), bf16[8,64,128]{2,1,0:T(8,128)(2,1)S(1)}, u32[]{:S(2)}, u32[]{:S(2)}) async-start(bf16[8,64,128]{2,1,0:T(8,128)(2,1)} %bitcast.10), calls=%async_computation | async-start | bytes 262144 | tf_op jit(solution)/shard_map/all_to_all | solution.py:393
  7.3 1.1 %pad_maximum_fusion.book_ref = bf16[264,1024]{1,0:T(8,128)(2,1)S(1)} fusion(bf16[8,1024]{1,0:T(8,128)(2,1)} %param.7, bf16[256,1024]{1,0:T(8,128)(2,1)} %param.6), kind=kLoop, calls=%fused_computation | loop fusion | flops 1081344 | bytes 1081344 | tf_op jit(solution)/shard_map/concatenate | solution.py:418
  8.4 0.5 %word_table.1 = (bf16[1024,256]{1,0:T(8,128)(2,1)S(1)}, f32[1024,128]{1,0:T(8,128)S(1)}, f32[64,256]{1,0:T(8,128)S(1)}) custom-call(s32[1,1]{1,0:T(1,128)} %bitcast.5.group_ref, bf16[264,1024]{1,0:T(8,128)(2,1)S(1)} %pad_maximum_fusion.book_ref), custom_call_target="tpu_custom_call" | custom-call | flops 1048576 | bytes 1572864 | tf_op jit(solution)/shard_map/word_table/pallas_call | solution.py:405
  8.9 3.9 %all-to-all-done = bf16[8,64,128]{2,1,0:T(8,128)(2,1)S(1)} async-done(((bf16[8,64,128]{2,1,0:T(8,128)(2,1)}), bf16[8,64,128]{2,1,0:T(8,128)(2,1)S(1)}, u32[]{:S(2)}, u32[]{:S(2)}) %all-to-all-start) | async-done | bytes 131104 | tf_op jit(solution)/shard_map/all_to_all | solution.py:393
  12.8 1.6 %collective-permute-start.1 = (bf16[512,128]{1,0:T(8,128)(2,1)S(1)}, bf16[512,128]{1,0:T(8,128)(2,1)S(1)}, u32[]{:S(2)}, u32[]{:S(2)}) collective-permute-start(bf16[512,128]{1,0:T(8,128)(2,1)S(1)} %bitcast.7), channel_id=1, source_target_pairs={{0,1},{1,0},{2,3},{3,2},{4,5},{5,4},{6,7},{7,6},{8,9},{9,8},{10,11... | collective-permute-start | bytes 393224 | tf_op jit(solution)/shard_map/ppermute | solution.py:395
  14.4 2.6 %collective-permute-start = (bf16[512,128]{1,0:T(8,128)(2,1)S(1)}, bf16[512,128]{1,0:T(8,128)(2,1)S(1)}, u32[]{:S(2)}, u32[]{:S(2)}) collective-permute-start(bf16[512,128]{1,0:T(8,128)(2,1)S(1)} %bitcast.8), channel_id=1, source_target_pairs={{0,2},{1,3},{2,0},{3,1},{4,6},{5,7},{6,4},{7,5},{8,10},{9,11},{10,... | collective-permute-start | bytes 393224 | tf_op jit(solution)/shard_map/ppermute | solution.py:395
  17.0 2.6 %rows_0.1 = (bf16[1024,1024]{1,0:T(8,128)(2,1)S(1)}, bf16[1024,1024]{1,0:T(8,128)(2,1)S(1)}, f32[32,8,128]{2,1,0:T(8,128)S(1)}, f32[1024,128]{1,0:T(8,128)S(1)}, f32[8,8,128]{2,1,0:T(8,128)S(1)}) custom-call(s32[1,1]{1,0:T(1,128)} %bitcast.place_ref, bf16[512,128]{1,0:T(8,128)(2,1)S(1)} %bitcast.9, bf16[1024,256]{1,0:T(8,128)(2,1)S(1)} %get-tuple-element.26.refs_0_, ...), custom_call_target="tpu_custom_call" | custom-call | flops 2147483648 | bytes 16777216 | tf_op jit(solution)/shard_map/rows_0/pallas_call | solution.py:442
  19.6 0.1 collective-permute-done.1.codes_ref
  19.6 3.5 %rows_1.1 = (bf16[1024,1024]{1,0:T(8,128)(2,1)S(1)}, bf16[1024,1024]{1,0:T(8,128)(2,1)S(1)}, f32[32,8,128]{2,1,0:T(8,128)S(1)}, f32[1024,128]{1,0:T(8,128)S(1)}, f32[8,8,128]{2,1,0:T(8,128)S(1)}) custom-call(s32[1,1]{1,0:T(1,128)} %bitcast.place_ref, ...), custom_call_target="tpu_custom_call", output_to_operand_aliasing={{1}: (6, {}), {2}: (7, {}), {3}: (8, {}), {4}: (9, {})} | custom-call | flops 2147483648 | bytes 16777216 | tf_op jit(solution)/shard_map/rows_1/pallas_call | solution.py:442
  23.1 0.0 collective-permute-done.codes_ref
  23.1 0.5 %collective-permute-start.2 = (bf16[512,128]{1,0:T(8,128)(2,1)S(1)}, bf16[512,128]{1,0:T(8,128)(2,1)S(1)}, u32[]{:S(2)}, u32[]{:S(2)}) collective-permute-start(bf16[512,128]{1,0:T(8,128)(2,1)S(1)} %collective-permute-done.codes_ref), channel_id=1, source_target_pairs={{0,1},{1,0},{2,3},{3,2},{4,5},{5,4},{6,7},{7,6},{8,9},{9,8},{10,11... | collective-permute-start | bytes 393224 | tf_op jit(solution)/shard_map/ppermute | solution.py:395
  23.6 4.3 %rows_2.1 = (bf16[1024,1024]{1,0:T(8,128)(2,1)S(1)}, bf16[1024,1024]{1,0:T(8,128)(2,1)S(1)}, f32[32,8,128]{2,1,0:T(8,128)S(1)}, f32[1024,128]{1,0:T(8,128)S(1)}, f32[8,8,128]{2,1,0:T(8,128)S(1)}) custom-call(s32[1,1]{1,0:T(1,128)} %bitcast.place_ref, ...), custom_call_target="tpu_custom_call", output_to_operand_aliasing={{1}: (7, {}), {2}: (8, {}), {3}: (9, {}), {4}: (10, {})} | custom-call | flops 2147483648 | bytes 16777216 | tf_op jit(solution)/shard_map/rows_2/pallas_call | solution.py:442
  27.9 0.3 collective-permute-done.2.codes_ref
  28.2 6.7 %last_rows.1 = (f32[8,128]{1,0:T(8,128)}, bf16[1024,1024]{1,0:T(8,128)(2,1)S(1)}, f32[32,8,128]{2,1,0:T(8,128)S(1)}, f32[1024,128]{1,0:T(8,128)S(1)}, f32[8,8,128]{2,1,0:T(8,128)S(1)}) custom-call(s32[1,1]{1,0:T(1,128)} %bitcast.place_ref, ...), custom_call_target="tpu_custom_call", output_to_operand_aliasing={{1}: (8, {}), {2}: (9, {}), {3}: (10, {}), {4}: (11, {})} | custom-call | flops 8589934592 | bytes 16777216 | tf_op jit(solution)/shard_map/last_rows/pallas_call | solution.py:478
Async XLA Ops:
  2.1 10.7 %all-to-all-start = ((bf16[8,64,128]{2,1,0:T(8,128)(2,1)}), bf16[8,64,128]{2,1,0:T(8,128)(2,1)S(1)}, u32[]{:S(2)}, u32[]{:S(2)}) async-start(bf16[8,64,128]{2,1,0:T(8,128)(2,1)} %bitcast.10), calls=%async_computation | async-start | bytes 262144 | tf_op jit(solution)/shard_map/all_to_all | solution.py:393
  12.8 6.8 %collective-permute-start.1 = (bf16[512,128]{1,0:T(8,128)(2,1)S(1)}, bf16[512,128]{1,0:T(8,128)(2,1)S(1)}, u32[]{:S(2)}, u32[]{:S(2)}) collective-permute-start(bf16[512,128]{1,0:T(8,128)(2,1)S(1)} %bitcast.7), channel_id=1, source_target_pairs={{0,1},{1,0},{2,3},{3,2},{4,5},{5,4},{6,7},{7,6},{8,9},{9,8},{10,11... | collective-permute-start | bytes 393224 | tf_op jit(solution)/shard_map/ppermute | solution.py:395
  14.4 8.7 %collective-permute-start = (bf16[512,128]{1,0:T(8,128)(2,1)S(1)}, bf16[512,128]{1,0:T(8,128)(2,1)S(1)}, u32[]{:S(2)}, u32[]{:S(2)}) collective-permute-start(bf16[512,128]{1,0:T(8,128)(2,1)S(1)} %bitcast.8), channel_id=1, source_target_pairs={{0,2},{1,3},{2,0},{3,1},{4,6},{5,7},{6,4},{7,5},{8,10},{9,11},{10,... | collective-permute-start | bytes 393224 | tf_op jit(solution)/shard_map/ppermute | solution.py:395
  23.1 5.0 %collective-permute-start.2 = (bf16[512,128]{1,0:T(8,128)(2,1)S(1)}, bf16[512,128]{1,0:T(8,128)(2,1)S(1)}, u32[]{:S(2)}, u32[]{:S(2)}) collective-permute-start(bf16[512,128]{1,0:T(8,128)(2,1)S(1)} %collective-permute-done.codes_ref), channel_id=1, source_target_pairs={{0,1},{1,0},{2,3},{3,2},{4,5},{5,4},{6,7},{7,6},{8,9},{9,8},{10,11... | collective-permute-start | bytes 393224 | tf_op jit(solution)/shard_map/ppermute | solution.py:395

commit v11 on v10

--- a/solution.py
+++ b/solution.py
@@ -10,8 +10,7 @@
 LANES = 128
 COLS = 256
 ROWS = 16
-HELD = 3
-CHUNK = 128
+HELD = 6
 LOW = -4.0
 VMEM_LIMIT = 40 * 1024 * 1024
 PARAMS = pltpu.CompilerParams(vmem_limit_bytes=VMEM_LIMIT)
@@ -178,12 +177,14 @@
 
 
 def mix(scoring, decoding):
-    done = 0
-    for place, score_chunk in enumerate(scoring):
-        upto = (place + 1) * len(decoding) // len(scoring)
+    whole = sum(weight for weight, _ in scoring)
+    done, behind = 0, 0
+    for weight, score_rows in scoring:
+        behind += weight
+        upto = behind * len(decoding) // whole
         beside = decoding[done : min(upto, done + HELD)]
         held = [(step(), put) for step, put in beside]
-        score_chunk()
+        score_rows()
         for values, put in held:
             put(values)
         run(decoding[done + len(beside) : upto])
@@ -210,36 +211,34 @@
     best_ref[rows, :] = best
 
 
-def own_score(left_ref, chunk, units_ref, block, mark_ref, best_ref, mirror_ref):
-    start = chunk * COLS
+def own_score(left_ref, units_ref, block, mark_ref, best_ref, mirror_ref):
+    above, count = block * COLS, (block + 1) * COLS
     scores = jnp.dot(
-        left_ref[start : start + COLS, :], units_ref[:, :COLS],
-        preferred_element_type=jnp.float32,
+        left_ref[:count, :], units_ref[:, :COLS], preferred_element_type=jnp.float32
     )
     row_ids = lax.broadcasted_iota(jnp.int32, (COLS, LANES), 0)
     lane_ids = lax.broadcasted_iota(jnp.int32, (COLS, LANES), 1)
-    best = best_ref[start : start + COLS, :]
     for part in range(COLS // LANES):
         tile = block * (COLS // LANES) + part
-        piece = scores[:, part * LANES : (part + 1) * LANES]
-        keep = mark_ref[tile][0:1, :] > 0
-        if chunk == block:
-            keep = keep & (row_ids != lane_ids + part * LANES)
-        best = jnp.maximum(best, jnp.where(keep, piece, LOW))
-        if chunk == 0:
-            mirror = jnp.full((8, LANES), LOW, jnp.float32)
-        else:
-            mirror = mirror_ref[tile]
-        if chunk < block:
-            for other in range(COLS // LANES):
-                row_marks = mark_ref[chunk * (COLS // LANES) + other][0:1, :]
-                row_filled = jnp.transpose(jnp.broadcast_to(row_marks, (LANES, LANES))) > 0
-                across = jnp.where(
-                    row_filled, piece[other * LANES : (other + 1) * LANES], LOW
-                )
-                mirror = jnp.maximum(mirror, jnp.max(across, axis=0, keepdims=True))
-        mirror_ref[tile] = mirror
-    best_ref[start : start + COLS, :] = best
+        lanes = slice(part * LANES, (part + 1) * LANES)
+        filled = mark_ref[tile][0:1, :] > 0
+        keep = filled & (row_ids != lane_ids + part * LANES)
+        best_ref[above:count, :] = jnp.maximum(
+            best_ref[above:count, :], jnp.where(keep, scores[above:count, lanes], LOW)
+        )
+        mirror = jnp.full((1, LANES), LOW, jnp.float32)
+        for other in range(above // LANES):
+            rows = slice(other * LANES, (other + 1) * LANES)
+            piece = scores[rows, lanes]
+            best_ref[rows, :] = jnp.maximum(best_ref[rows, :], jnp.where(filled, piece, LOW))
+            row_filled = jnp.transpose(
+                jnp.broadcast_to(mark_ref[other][0:1, :], (LANES, LANES))
+            )
+            mirror = jnp.maximum(
+                mirror,
+                jnp.max(jnp.where(row_filled > 0, piece, LOW), axis=0, keepdims=True),
+            )
+        mirror_ref[tile] = jnp.broadcast_to(mirror, (8, LANES))
 
 
 def marks_of(mark_ref, group):
@@ -269,37 +268,36 @@
             )
         return steps
 
-    def scoring(which, turn, chunks):
-        return [
-            functools.partial(
-                score, left_ref, slice(start, start + CHUNK), units_refs[which],
-                column_of(turn), marks_of(mark_ref, turn * groups + which), best_ref,
-            )
-            for chunk in chunks
-            for start in range(chunk * COLS, (chunk + 1) * COLS, CHUNK)
-        ]
+    def scoring(which, turn, first, last):
+        rows = slice(first * COLS, last * COLS)
+        return last - first, functools.partial(
+            score, left_ref, rows, units_refs[which], column_of(turn),
+            marks_of(mark_ref, turn * groups + which), best_ref,
+        )
 
     if block == 0:
         best_ref[...] = jnp.full(best_ref.shape, LOW, jnp.float32)
         run(decoding(0))
     else:
-        mix(scoring(block - 1, owners - 1, range(block)), decoding(0))
+        mix([scoring(block - 1, owners - 1, 0, block)], decoding(0))
     turn_own(units_ref, left_ref, block)
 
     steps = [
-        functools.partial(
-            own_score, left_ref, chunk, units_ref, block, mark_ref, best_ref, mirror_ref
-        )
-        for chunk in range(block + 1)
+        (
+            block + 1,
+            functools.partial(
+                own_score, left_ref, units_ref, block, mark_ref, best_ref, mirror_ref
+            ),
+        )
     ]
     for which in range(block):
-        steps += scoring(which, 1, [block])
+        steps.append(scoring(which, 1, block, block + 1))
     mix(steps, decoding(1))
 
     def both(turn, _):
-        steps = scoring(block, turn - 1, range(block + 1))
+        steps = [scoring(block, turn - 1, 0, block + 1)]
         for which in range(block):
-            steps += scoring(which, turn, [block])
+            steps.append(scoring(which, turn, block, block + 1))
         mix(steps, decoding(turn))
         return 0
 

time: 35.2 us -> 34.3 us (0.974)
  Pallas kernels: 19.6 us -> 17.3 us
  waiting for transfers between devices: 4.28 us -> 5.68 us
    pallas_call x3, Pallas kernels: 10.3 us -> 8.64 us  [take_in(): pl.pallas_call(functools.partial(next_kernel, block), out_shape=(units_sh...]
    ppermute x3, waiting for transfers between devices: 0.38 us -> 1.78 us  [from_member(): return lax.ppermute(block, 'blk', [(i, i ^ mask) for i in range(members)])]
    pallas_call x1, Pallas kernels: 6.66 us -> 6.1 us  [on_device(): pl.pallas_call(functools.partial(last_kernel, (capacity, clusters, member...]
  transfers between devices with their start and end apart: 4 -> 4, of which waited for: 3 -> 4; matrix products, arithmetic and copies ran while one was open for 3% -> 3% of each run, Pallas kernels for 31% -> 27%
where the time goes in v11:
time: 34.3 us; the launch traced here: 34 us
  Pallas kernels  17.3 us (50%)
  starting transfers between devices  9.8 us (29%)
  waiting for transfers between devices  5.68 us (17%)
  other arithmetic  1.09 us (3%)
    pallas_call x3, Pallas kernels, take_in(): pl.pallas_call(functools.partial(next_kernel, block), out_shape=(units_sh...  8.64 us
    pallas_call x1, Pallas kernels, on_device(): pl.pallas_call(functools.partial(last_kernel, (capacity, clusters, member...  6.1 us
    all_to_all x1, starting transfers between devices, on_device(): lax.all_to_all(packed, 'cluster', split_axis=0, concat_axis=0, tiled=True)  5.19 us
    ppermute x3, starting transfers between devices, from_member(): return lax.ppermute(block, 'blk', [(i, i ^ mask) for i in range(members)])  4.61 us
    all_to_all x1, waiting for transfers between devices, on_device(): lax.all_to_all(packed, 'cluster', split_axis=0, concat_axis=0, tiled=True)  3.91 us
    pallas_call x1, Pallas kernels, on_device(): pl.pallas_call(functools.partial(pack_kernel, devices, capacity), out_sha...  2.08 us
    ppermute x3, waiting for transfers between devices, from_member(): return lax.ppermute(block, 'blk', [(i, i ^ mask) for i in range(members)])  1.78 us
    concatenate x1, other arithmetic, on_device(): jnp.concatenate([codebook, centroids], axis=0)  1.09 us
  transfers between devices with their start and end apart: 4, of which 4 were waited for; matrix products, arithmetic and copies ran while one was open for 3% of the time, Pallas kernels for 27%

profile of v11, /device:TPU:0, one launch (start us, length us, event | category | flops | bytes accessed | tf_op | source)
XLA Modules:
  0.0 34.0 jit_solution(908144096729550668)
XLA Ops:
  0.0 2.1 %pack_rows.1 = bf16[512,128]{1,0:T(8,128)(2,1)} custom-call(s32[64,512]{1,0:T(8,128)} %bitcast.11, s32[1,512]{1,0:T(1,128)} %bitcast.12), custom_call_target="tpu_custom_call" | custom-call | tf_op jit(solution)/shard_map/pack_rows/pallas_call | solution.py:377
  2.1 5.2 %all-to-all-start = ((bf16[8,64,128]{2,1,0:T(8,128)(2,1)}), bf16[8,64,128]{2,1,0:T(8,128)(2,1)S(1)}, u32[]{:S(2)}, u32[]{:S(2)}) async-start(bf16[8,64,128]{2,1,0:T(8,128)(2,1)} %bitcast.10), calls=%async_computation | async-start | bytes 262144 | tf_op jit(solution)/shard_map/all_to_all | solution.py:391
  7.3 1.1 %pad_maximum_fusion.book_ref = bf16[264,1024]{1,0:T(8,128)(2,1)S(1)} fusion(bf16[8,1024]{1,0:T(8,128)(2,1)} %param.7, bf16[256,1024]{1,0:T(8,128)(2,1)} %param.6), kind=kLoop, calls=%fused_computation | loop fusion | flops 1081344 | bytes 1081344 | tf_op jit(solution)/shard_map/concatenate | solution.py:416
  8.4 0.5 %word_table.1 = (bf16[1024,256]{1,0:T(8,128)(2,1)S(1)}, f32[1024,128]{1,0:T(8,128)S(1)}, f32[64,256]{1,0:T(8,128)S(1)}) custom-call(s32[1,1]{1,0:T(1,128)} %bitcast.5.group_ref, bf16[264,1024]{1,0:T(8,128)(2,1)S(1)} %pad_maximum_fusion.book_ref), custom_call_target="tpu_custom_call" | custom-call | flops 1048576 | bytes 1572864 | tf_op jit(solution)/shard_map/word_table/pallas_call | solution.py:403
  8.9 3.9 %all-to-all-done = bf16[8,64,128]{2,1,0:T(8,128)(2,1)S(1)} async-done(((bf16[8,64,128]{2,1,0:T(8,128)(2,1)}), bf16[8,64,128]{2,1,0:T(8,128)(2,1)S(1)}, u32[]{:S(2)}, u32[]{:S(2)}) %all-to-all-start) | async-done | bytes 131104 | tf_op jit(solution)/shard_map/all_to_all | solution.py:391
  12.8 1.6 %collective-permute-start.1 = (bf16[512,128]{1,0:T(8,128)(2,1)S(1)}, bf16[512,128]{1,0:T(8,128)(2,1)S(1)}, u32[]{:S(2)}, u32[]{:S(2)}) collective-permute-start(bf16[512,128]{1,0:T(8,128)(2,1)S(1)} %bitcast.7), channel_id=1, source_target_pairs={{0,1},{1,0},{2,3},{3,2},{4,5},{5,4},{6,7},{7,6},{8,9},{9,8},{10,11... | collective-permute-start | bytes 393224 | tf_op jit(solution)/shard_map/ppermute | solution.py:393
  14.4 2.6 %collective-permute-start = (bf16[512,128]{1,0:T(8,128)(2,1)S(1)}, bf16[512,128]{1,0:T(8,128)(2,1)S(1)}, u32[]{:S(2)}, u32[]{:S(2)}) collective-permute-start(bf16[512,128]{1,0:T(8,128)(2,1)S(1)} %bitcast.8), channel_id=1, source_target_pairs={{0,2},{1,3},{2,0},{3,1},{4,6},{5,7},{6,4},{7,5},{8,10},{9,11},{10,... | collective-permute-start | bytes 393224 | tf_op jit(solution)/shard_map/ppermute | solution.py:393
  17.0 2.2 %rows_0.1 = (bf16[1024,1024]{1,0:T(8,128)(2,1)S(1)}, bf16[1024,1024]{1,0:T(8,128)(2,1)S(1)}, f32[32,8,128]{2,1,0:T(8,128)S(1)}, f32[1024,128]{1,0:T(8,128)S(1)}, f32[8,8,128]{2,1,0:T(8,128)S(1)}) custom-call(s32[1,1]{1,0:T(1,128)} %bitcast.place_ref, bf16[512,128]{1,0:T(8,128)(2,1)S(1)} %bitcast.9, bf16[1024,256]{1,0:T(8,128)(2,1)S(1)} %get-tuple-element.26.refs_0_, ...), custom_call_target="tpu_custom_call" | custom-call | flops 2147483648 | bytes 16777216 | tf_op jit(solution)/shard_map/rows_0/pallas_call | solution.py:440
  19.2 0.4 %collective-permute-done.1.codes_ref = bf16[512,128]{1,0:T(8,128)(2,1)S(1)} collective-permute-done((bf16[512,128]{1,0:T(8,128)(2,1)S(1)}, bf16[512,128]{1,0:T(8,128)(2,1)S(1)}, u32[]{:S(2)}, u32[]{:S(2)}) %collective-permute-start.1) | collective-permute-done | bytes 131104 | tf_op jit(solution)/shard_map/ppermute | solution.py:393
  19.6 2.8 %rows_1.1 = (bf16[1024,1024]{1,0:T(8,128)(2,1)S(1)}, bf16[1024,1024]{1,0:T(8,128)(2,1)S(1)}, f32[32,8,128]{2,1,0:T(8,128)S(1)}, f32[1024,128]{1,0:T(8,128)S(1)}, f32[8,8,128]{2,1,0:T(8,128)S(1)}) custom-call(s32[1,1]{1,0:T(1,128)} %bitcast.place_ref, ...), custom_call_target="tpu_custom_call", output_to_operand_aliasing={{1}: (6, {}), {2}: (7, {}), {3}: (8, {}), {4}: (9, {})} | custom-call | flops 2147483648 | bytes 16777216 | tf_op jit(solution)/shard_map/rows_1/pallas_call | solution.py:440
  22.5 0.4 %collective-permute-done.codes_ref = bf16[512,128]{1,0:T(8,128)(2,1)S(1)} collective-permute-done((bf16[512,128]{1,0:T(8,128)(2,1)S(1)}, bf16[512,128]{1,0:T(8,128)(2,1)S(1)}, u32[]{:S(2)}, u32[]{:S(2)}) %collective-permute-start) | collective-permute-done | bytes 131104 | tf_op jit(solution)/shard_map/ppermute | solution.py:393
  22.9 0.4 %collective-permute-start.2 = (bf16[512,128]{1,0:T(8,128)(2,1)S(1)}, bf16[512,128]{1,0:T(8,128)(2,1)S(1)}, u32[]{:S(2)}, u32[]{:S(2)}) collective-permute-start(bf16[512,128]{1,0:T(8,128)(2,1)S(1)} %collective-permute-done.codes_ref), channel_id=1, source_target_pairs={{0,1},{1,0},{2,3},{3,2},{4,5},{5,4},{6,7},{7,6},{8,9},{9,8},{10,11... | collective-permute-start | bytes 393224 | tf_op jit(solution)/shard_map/ppermute | solution.py:393
  23.3 3.6 %rows_2.1 = (bf16[1024,1024]{1,0:T(8,128)(2,1)S(1)}, bf16[1024,1024]{1,0:T(8,128)(2,1)S(1)}, f32[32,8,128]{2,1,0:T(8,128)S(1)}, f32[1024,128]{1,0:T(8,128)S(1)}, f32[8,8,128]{2,1,0:T(8,128)S(1)}) custom-call(s32[1,1]{1,0:T(1,128)} %bitcast.place_ref, ...), custom_call_target="tpu_custom_call", output_to_operand_aliasing={{1}: (7, {}), {2}: (8, {}), {3}: (9, {}), {4}: (10, {})} | custom-call | flops 2147483648 | bytes 16777216 | tf_op jit(solution)/shard_map/rows_2/pallas_call | solution.py:440
  26.9 1.0 %collective-permute-done.2.codes_ref = bf16[512,128]{1,0:T(8,128)(2,1)S(1)} collective-permute-done((bf16[512,128]{1,0:T(8,128)(2,1)S(1)}, bf16[512,128]{1,0:T(8,128)(2,1)S(1)}, u32[]{:S(2)}, u32[]{:S(2)}) %collective-permute-start.2) | collective-permute-done | bytes 131104 | tf_op jit(solution)/shard_map/ppermute | solution.py:393
  27.9 6.1 %last_rows.1 = (f32[8,128]{1,0:T(8,128)}, bf16[1024,1024]{1,0:T(8,128)(2,1)S(1)}, f32[32,8,128]{2,1,0:T(8,128)S(1)}, f32[1024,128]{1,0:T(8,128)S(1)}, f32[8,8,128]{2,1,0:T(8,128)S(1)}) custom-call(s32[1,1]{1,0:T(1,128)} %bitcast.place_ref, ...), custom_call_target="tpu_custom_call", output_to_operand_aliasing={{1}: (8, {}), {2}: (9, {}), {3}: (10, {}), {4}: (11, {})} | custom-call | flops 8589934592 | bytes 16777216 | tf_op jit(solution)/shard_map/last_rows/pallas_call | solution.py:476
Async XLA Ops:
  2.1 10.7 %all-to-all-start = ((bf16[8,64,128]{2,1,0:T(8,128)(2,1)}), bf16[8,64,128]{2,1,0:T(8,128)(2,1)S(1)}, u32[]{:S(2)}, u32[]{:S(2)}) async-start(bf16[8,64,128]{2,1,0:T(8,128)(2,1)} %bitcast.10), calls=%async_computation | async-start | bytes 262144 | tf_op jit(solution)/shard_map/all_to_all | solution.py:391
  12.8 6.8 %collective-permute-start.1 = (bf16[512,128]{1,0:T(8,128)(2,1)S(1)}, bf16[512,128]{1,0:T(8,128)(2,1)S(1)}, u32[]{:S(2)}, u32[]{:S(2)}) collective-permute-start(bf16[512,128]{1,0:T(8,128)(2,1)S(1)} %bitcast.7), channel_id=1, source_target_pairs={{0,1},{1,0},{2,3},{3,2},{4,5},{5,4},{6,7},{7,6},{8,9},{9,8},{10,11... | collective-permute-start | bytes 393224 | tf_op jit(solution)/shard_map/ppermute | solution.py:393
  14.4 8.5 %collective-permute-start = (bf16[512,128]{1,0:T(8,128)(2,1)S(1)}, bf16[512,128]{1,0:T(8,128)(2,1)S(1)}, u32[]{:S(2)}, u32[]{:S(2)}) collective-permute-start(bf16[512,128]{1,0:T(8,128)(2,1)S(1)} %bitcast.8), channel_id=1, source_target_pairs={{0,2},{1,3},{2,0},{3,1},{4,6},{5,7},{6,4},{7,5},{8,10},{9,11},{10,... | collective-permute-start | bytes 393224 | tf_op jit(solution)/shard_map/ppermute | solution.py:393
  22.9 5.0 %collective-permute-start.2 = (bf16[512,128]{1,0:T(8,128)(2,1)S(1)}, bf16[512,128]{1,0:T(8,128)(2,1)S(1)}, u32[]{:S(2)}, u32[]{:S(2)}) collective-permute-start(bf16[512,128]{1,0:T(8,128)(2,1)S(1)} %collective-permute-done.codes_ref), channel_id=1, source_target_pairs={{0,1},{1,0},{2,3},{3,2},{4,5},{5,4},{6,7},{7,6},{8,9},{9,8},{10,11... | collective-permute-start | bytes 393224 | tf_op jit(solution)/shard_map/ppermute | solution.py:393

commit v12 on v11

--- a/solution.py
+++ b/solution.py
@@ -10,7 +10,7 @@
 LANES = 128
 COLS = 256
 ROWS = 16
-HELD = 6
+HELD = 12
 LOW = -4.0
 VMEM_LIMIT = 40 * 1024 * 1024
 PARAMS = pltpu.CompilerParams(vmem_limit_bytes=VMEM_LIMIT)
@@ -113,33 +113,36 @@
     return jnp.concatenate(parts, axis=0)
 
 
-def unpack_codes(block, norms_ref, code_ref, scale_ref, mark_ref, group, place):
-    turned = jnp.transpose(block.astype(jnp.float32)).astype(jnp.int32)
-    subspaces = turned.shape[0] // 2
-    for half in range(2):
-        part = turned[half * subspaces : (half + 1) * subspaces]
-        code = jnp.maximum(part - 1, 0)
-        code_ref[2 * group + half] = code
-        mark_ref[2 * place + half] = jnp.where(part[0:8] > 0, 1.0, 0.0)
-        low = code & (LANES - 1)
-        squares = jnp.where(
-            code >= LANES,
-            take_lanes(norms_ref[:, LANES:], low),
-            take_lanes(norms_ref[:, :LANES], low),
-        )
-        scale = lax.rsqrt(jnp.sum(squares, axis=0, keepdims=True) + 1e-06)
-        scale_ref[2 * group + half] = jnp.broadcast_to(scale, (8, LANES))
-
-
-def unpack_block(
-    place, first, which, codes_ref, norms_ref, code_ref, scale_ref, mark_ref, owners, groups
+def unpack_step(
+    place, block, turn, codes_ref, norms_ref, code_ref, scale_ref, mark_ref, owners, groups
 ):
-    for turn in range(owners):
+    def step():
         owner = lax.rem(place + turn, owners)
-        unpack_codes(
-            owner_block(codes_ref, owner, owners), norms_ref, code_ref, scale_ref, mark_ref,
-            which * owners + turn, turn * groups + first + which,
-        )
+        rows = owner_block(codes_ref, owner, owners)
+        turned = jnp.transpose(rows.astype(jnp.float32)).astype(jnp.int32)
+        subspaces = turned.shape[0] // 2
+        values = []
+        for half in range(2):
+            part = turned[half * subspaces : (half + 1) * subspaces]
+            code = jnp.maximum(part - 1, 0)
+            low = code & (LANES - 1)
+            squares = jnp.where(
+                code >= LANES,
+                take_lanes(norms_ref[:, LANES:], low),
+                take_lanes(norms_ref[:, :LANES], low),
+            )
+            scale = lax.rsqrt(jnp.sum(squares, axis=0, keepdims=True) + 1e-06)
+            marks = jnp.where(part[0:8] > 0, 1.0, 0.0)
+            values.append((code, jnp.broadcast_to(scale, (8, LANES)), marks))
+        return values
+
+    def put(values):
+        for half, (code, scale, marks) in enumerate(values):
+            code_ref[2 * turn + half] = code
+            scale_ref[2 * turn + half] = scale
+            mark_ref[2 * (turn * groups + block) + half] = marks
+
+    return step, put
 
 
 def decode_steps(code_ref, scale_ref, tile, words_ref, centre_ref, units_ref, start):
@@ -251,9 +254,14 @@
     units_ref = units_refs[block]
     owners = units_ref.shape[1] // COLS
     groups = left_ref.shape[0] // COLS
-    unpack_block(
-        place, block, 0, codes_ref, norms_ref, code_ref, scale_ref, mark_ref, owners, groups
-    )
+    unpacking = [
+        unpack_step(
+            place, block, turn, codes_ref, norms_ref, code_ref, scale_ref, mark_ref,
+            owners, groups,
+        )
+        for turn in range(owners)
+    ]
+    run(unpacking[:1])
 
     def column_of(turn, offset=0):
         column = turn * COLS + offset
@@ -277,9 +285,9 @@
 
     if block == 0:
         best_ref[...] = jnp.full(best_ref.shape, LOW, jnp.float32)
-        run(decoding(0))
+        run(unpacking[1:] + decoding(0))
     else:
-        mix([scoring(block - 1, owners - 1, 0, block)], decoding(0))
+        mix([scoring(block - 1, owners - 1, 0, block)], unpacking[1:] + decoding(0))
     turn_own(units_ref, left_ref, block)
 
     steps = [

time: 34.3 us -> 34.3 us (level)
  no operation moved by 1% of the time
where the time goes in v12:
time: 34.3 us; the launch traced here: 34 us
  Pallas kernels  17.3 us (50%)
  starting transfers between devices  9.8 us (29%)
  waiting for transfers between devices  5.68 us (17%)
  other arithmetic  1.09 us (3%)
    pallas_call x3, Pallas kernels, take_in(): pl.pallas_call(functools.partial(next_kernel, block), out_shape=(units_sh...  8.65 us
    pallas_call x1, Pallas kernels, on_device(): pl.pallas_call(functools.partial(last_kernel, (capacity, clusters, member...  6.1 us
    all_to_all x1, starting transfers between devices, on_device(): lax.all_to_all(packed, 'cluster', split_axis=0, concat_axis=0, tiled=True)  5.19 us
    ppermute x3, starting transfers between devices, from_member(): return lax.ppermute(block, 'blk', [(i, i ^ mask) for i in range(members)])  4.61 us
    all_to_all x1, waiting for transfers between devices, on_device(): lax.all_to_all(packed, 'cluster', split_axis=0, concat_axis=0, tiled=True)  3.91 us
    pallas_call x1, Pallas kernels, on_device(): pl.pallas_call(functools.partial(pack_kernel, devices, capacity), out_sha...  2.08 us
    ppermute x3, waiting for transfers between devices, from_member(): return lax.ppermute(block, 'blk', [(i, i ^ mask) for i in range(members)])  1.77 us
    concatenate x1, other arithmetic, on_device(): jnp.concatenate([codebook, centroids], axis=0)  1.09 us
  transfers between devices with their start and end apart: 4, of which 4 were waited for; matrix products, arithmetic and copies ran while one was open for 3% of the time, Pallas kernels for 27%

profile of v12, /device:TPU:0, one launch (start us, length us, event | category | flops | bytes accessed | tf_op | source)
XLA Modules:
  0.0 34.0 jit_solution(4417852572760480338)
XLA Ops:
  0.0 2.1 %pack_rows.1 = bf16[512,128]{1,0:T(8,128)(2,1)} custom-call(s32[64,512]{1,0:T(8,128)} %bitcast.11, s32[1,512]{1,0:T(1,128)} %bitcast.12), custom_call_target="tpu_custom_call" | custom-call | tf_op jit(solution)/shard_map/pack_rows/pallas_call | solution.py:385
  2.1 5.2 %all-to-all-start = ((bf16[8,64,128]{2,1,0:T(8,128)(2,1)}), bf16[8,64,128]{2,1,0:T(8,128)(2,1)S(1)}, u32[]{:S(2)}, u32[]{:S(2)}) async-start(bf16[8,64,128]{2,1,0:T(8,128)(2,1)} %bitcast.10), calls=%async_computation | async-start | bytes 262144 | tf_op jit(solution)/shard_map/all_to_all | solution.py:399
  7.3 1.1 %pad_maximum_fusion.book_ref = bf16[264,1024]{1,0:T(8,128)(2,1)S(1)} fusion(bf16[8,1024]{1,0:T(8,128)(2,1)} %param.7, bf16[256,1024]{1,0:T(8,128)(2,1)} %param.6), kind=kLoop, calls=%fused_computation | loop fusion | flops 1081344 | bytes 1081344 | tf_op jit(solution)/shard_map/concatenate | solution.py:424
  8.4 0.5 %word_table.1 = (bf16[1024,256]{1,0:T(8,128)(2,1)S(1)}, f32[1024,128]{1,0:T(8,128)S(1)}, f32[64,256]{1,0:T(8,128)S(1)}) custom-call(s32[1,1]{1,0:T(1,128)} %bitcast.5.group_ref, bf16[264,1024]{1,0:T(8,128)(2,1)S(1)} %pad_maximum_fusion.book_ref), custom_call_target="tpu_custom_call" | custom-call | flops 1048576 | bytes 1572864 | tf_op jit(solution)/shard_map/word_table/pallas_call | solution.py:411
  8.9 3.9 %all-to-all-done = bf16[8,64,128]{2,1,0:T(8,128)(2,1)S(1)} async-done(((bf16[8,64,128]{2,1,0:T(8,128)(2,1)}), bf16[8,64,128]{2,1,0:T(8,128)(2,1)S(1)}, u32[]{:S(2)}, u32[]{:S(2)}) %all-to-all-start) | async-done | bytes 131104 | tf_op jit(solution)/shard_map/all_to_all | solution.py:399
  12.8 1.6 %collective-permute-start.1 = (bf16[512,128]{1,0:T(8,128)(2,1)S(1)}, bf16[512,128]{1,0:T(8,128)(2,1)S(1)}, u32[]{:S(2)}, u32[]{:S(2)}) collective-permute-start(bf16[512,128]{1,0:T(8,128)(2,1)S(1)} %bitcast.7), channel_id=1, source_target_pairs={{0,1},{1,0},{2,3},{3,2},{4,5},{5,4},{6,7},{7,6},{8,9},{9,8},{10,11... | collective-permute-start | bytes 393224 | tf_op jit(solution)/shard_map/ppermute | solution.py:401
  14.4 2.6 %collective-permute-start = (bf16[512,128]{1,0:T(8,128)(2,1)S(1)}, bf16[512,128]{1,0:T(8,128)(2,1)S(1)}, u32[]{:S(2)}, u32[]{:S(2)}) collective-permute-start(bf16[512,128]{1,0:T(8,128)(2,1)S(1)} %bitcast.8), channel_id=1, source_target_pairs={{0,2},{1,3},{2,0},{3,1},{4,6},{5,7},{6,4},{7,5},{8,10},{9,11},{10,... | collective-permute-start | bytes 393224 | tf_op jit(solution)/shard_map/ppermute | solution.py:401
  17.0 2.2 %rows_0.1 = (bf16[1024,1024]{1,0:T(8,128)(2,1)S(1)}, bf16[1024,1024]{1,0:T(8,128)(2,1)S(1)}, f32[32,8,128]{2,1,0:T(8,128)S(1)}, f32[1024,128]{1,0:T(8,128)S(1)}, f32[8,8,128]{2,1,0:T(8,128)S(1)}) custom-call(s32[1,1]{1,0:T(1,128)} %bitcast.place_ref, bf16[512,128]{1,0:T(8,128)(2,1)S(1)} %bitcast.9, bf16[1024,256]{1,0:T(8,128)(2,1)S(1)} %get-tuple-element.26.refs_0_, ...), custom_call_target="tpu_custom_call" | custom-call | flops 2147483648 | bytes 16777216 | tf_op jit(solution)/shard_map/rows_0/pallas_call | solution.py:448
  19.2 0.4 %collective-permute-done.1.codes_ref = bf16[512,128]{1,0:T(8,128)(2,1)S(1)} collective-permute-done((bf16[512,128]{1,0:T(8,128)(2,1)S(1)}, bf16[512,128]{1,0:T(8,128)(2,1)S(1)}, u32[]{:S(2)}, u32[]{:S(2)}) %collective-permute-start.1) | collective-permute-done | bytes 131104 | tf_op jit(solution)/shard_map/ppermute | solution.py:401
  19.6 2.9 %rows_1.1 = (bf16[1024,1024]{1,0:T(8,128)(2,1)S(1)}, bf16[1024,1024]{1,0:T(8,128)(2,1)S(1)}, f32[32,8,128]{2,1,0:T(8,128)S(1)}, f32[1024,128]{1,0:T(8,128)S(1)}, f32[8,8,128]{2,1,0:T(8,128)S(1)}) custom-call(s32[1,1]{1,0:T(1,128)} %bitcast.place_ref, ...), custom_call_target="tpu_custom_call", output_to_operand_aliasing={{1}: (6, {}), {2}: (7, {}), {3}: (8, {}), {4}: (9, {})} | custom-call | flops 2147483648 | bytes 16777216 | tf_op jit(solution)/shard_map/rows_1/pallas_call | solution.py:448
  22.5 0.4 %collective-permute-done.codes_ref = bf16[512,128]{1,0:T(8,128)(2,1)S(1)} collective-permute-done((bf16[512,128]{1,0:T(8,128)(2,1)S(1)}, bf16[512,128]{1,0:T(8,128)(2,1)S(1)}, u32[]{:S(2)}, u32[]{:S(2)}) %collective-permute-start) | collective-permute-done | bytes 131104 | tf_op jit(solution)/shard_map/ppermute | solution.py:401
  22.9 0.4 %collective-permute-start.2 = (bf16[512,128]{1,0:T(8,128)(2,1)S(1)}, bf16[512,128]{1,0:T(8,128)(2,1)S(1)}, u32[]{:S(2)}, u32[]{:S(2)}) collective-permute-start(bf16[512,128]{1,0:T(8,128)(2,1)S(1)} %collective-permute-done.codes_ref), channel_id=1, source_target_pairs={{0,1},{1,0},{2,3},{3,2},{4,5},{5,4},{6,7},{7,6},{8,9},{9,8},{10,11... | collective-permute-start | bytes 393224 | tf_op jit(solution)/shard_map/ppermute | solution.py:401
  23.3 3.6 %rows_2.1 = (bf16[1024,1024]{1,0:T(8,128)(2,1)S(1)}, bf16[1024,1024]{1,0:T(8,128)(2,1)S(1)}, f32[32,8,128]{2,1,0:T(8,128)S(1)}, f32[1024,128]{1,0:T(8,128)S(1)}, f32[8,8,128]{2,1,0:T(8,128)S(1)}) custom-call(s32[1,1]{1,0:T(1,128)} %bitcast.place_ref, ...), custom_call_target="tpu_custom_call", output_to_operand_aliasing={{1}: (7, {}), {2}: (8, {}), {3}: (9, {}), {4}: (10, {})} | custom-call | flops 2147483648 | bytes 16777216 | tf_op jit(solution)/shard_map/rows_2/pallas_call | solution.py:448
  26.9 1.0 %collective-permute-done.2.codes_ref = bf16[512,128]{1,0:T(8,128)(2,1)S(1)} collective-permute-done((bf16[512,128]{1,0:T(8,128)(2,1)S(1)}, bf16[512,128]{1,0:T(8,128)(2,1)S(1)}, u32[]{:S(2)}, u32[]{:S(2)}) %collective-permute-start.2) | collective-permute-done | bytes 131104 | tf_op jit(solution)/shard_map/ppermute | solution.py:401
  27.9 6.1 %last_rows.1 = (f32[8,128]{1,0:T(8,128)}, bf16[1024,1024]{1,0:T(8,128)(2,1)S(1)}, f32[32,8,128]{2,1,0:T(8,128)S(1)}, f32[1024,128]{1,0:T(8,128)S(1)}, f32[8,8,128]{2,1,0:T(8,128)S(1)}) custom-call(s32[1,1]{1,0:T(1,128)} %bitcast.place_ref, ...), custom_call_target="tpu_custom_call", output_to_operand_aliasing={{1}: (8, {}), {2}: (9, {}), {3}: (10, {}), {4}: (11, {})} | custom-call | flops 8589934592 | bytes 16777216 | tf_op jit(solution)/shard_map/last_rows/pallas_call | solution.py:484
Async XLA Ops:
  2.1 10.7 %all-to-all-start = ((bf16[8,64,128]{2,1,0:T(8,128)(2,1)}), bf16[8,64,128]{2,1,0:T(8,128)(2,1)S(1)}, u32[]{:S(2)}, u32[]{:S(2)}) async-start(bf16[8,64,128]{2,1,0:T(8,128)(2,1)} %bitcast.10), calls=%async_computation | async-start | bytes 262144 | tf_op jit(solution)/shard_map/all_to_all | solution.py:399
  12.8 6.8 %collective-permute-start.1 = (bf16[512,128]{1,0:T(8,128)(2,1)S(1)}, bf16[512,128]{1,0:T(8,128)(2,1)S(1)}, u32[]{:S(2)}, u32[]{:S(2)}) collective-permute-start(bf16[512,128]{1,0:T(8,128)(2,1)S(1)} %bitcast.7), channel_id=1, source_target_pairs={{0,1},{1,0},{2,3},{3,2},{4,5},{5,4},{6,7},{7,6},{8,9},{9,8},{10,11... | collective-permute-start | bytes 393224 | tf_op jit(solution)/shard_map/ppermute | solution.py:401
  14.4 8.5 %collective-permute-start = (bf16[512,128]{1,0:T(8,128)(2,1)S(1)}, bf16[512,128]{1,0:T(8,128)(2,1)S(1)}, u32[]{:S(2)}, u32[]{:S(2)}) collective-permute-start(bf16[512,128]{1,0:T(8,128)(2,1)S(1)} %bitcast.8), channel_id=1, source_target_pairs={{0,2},{1,3},{2,0},{3,1},{4,6},{5,7},{6,4},{7,5},{8,10},{9,11},{10,... | collective-permute-start | bytes 393224 | tf_op jit(solution)/shard_map/ppermute | solution.py:401
  22.9 5.0 %collective-permute-start.2 = (bf16[512,128]{1,0:T(8,128)(2,1)S(1)}, bf16[512,128]{1,0:T(8,128)(2,1)S(1)}, u32[]{:S(2)}, u32[]{:S(2)}) collective-permute-start(bf16[512,128]{1,0:T(8,128)(2,1)S(1)} %collective-permute-done.codes_ref), channel_id=1, source_target_pairs={{0,1},{1,0},{2,3},{3,2},{4,5},{5,4},{6,7},{7,6},{8,9},{9,8},{10,11... | collective-permute-start | bytes 393224 | tf_op jit(solution)/shard_map/ppermute | solution.py:401

commit v13 on v12

--- a/solution.py
+++ b/solution.py
@@ -285,9 +285,9 @@
 
     if block == 0:
         best_ref[...] = jnp.full(best_ref.shape, LOW, jnp.float32)
-        run(unpacking[1:] + decoding(0))
+        run(unpacking[1:2] + decoding(0))
     else:
-        mix([scoring(block - 1, owners - 1, 0, block)], unpacking[1:] + decoding(0))
+        mix([scoring(block - 1, owners - 1, 0, block)], unpacking[1:2] + decoding(0))
     turn_own(units_ref, left_ref, block)
 
     steps = [
@@ -300,7 +300,7 @@
     ]
     for which in range(block):
         steps.append(scoring(which, 1, block, block + 1))
-    mix(steps, decoding(1))
+    mix(steps, unpacking[2:] + decoding(1))
 
     def both(turn, _):
         steps = [scoring(block, turn - 1, 0, block + 1)]

time: 34.3 us -> 34.1 us (level)
  Pallas kernels: 17.3 us -> 16.9 us
  transfers between devices with their start and end apart: 4 -> 4, of which waited for: 4 -> 4; matrix products, arithmetic and copies ran while one was open for 3% -> 3% of each run, Pallas kernels for 27% -> 26%
where the time goes in v13:
time: 34.1 us; the launch traced here: 33.8 us
  Pallas kernels  16.9 us (50%)
  starting transfers between devices  9.8 us (29%)
  waiting for transfers between devices  5.98 us (18%)
  other arithmetic  1.09 us (3%)
    pallas_call x3, Pallas kernels, take_in(): pl.pallas_call(functools.partial(next_kernel, block), out_shape=(units_sh...  8.35 us
    pallas_call x1, Pallas kernels, on_device(): pl.pallas_call(functools.partial(last_kernel, (capacity, clusters, member...  5.93 us
    all_to_all x1, starting transfers between devices, on_device(): lax.all_to_all(packed, 'cluster', split_axis=0, concat_axis=0, tiled=True)  5.19 us
    ppermute x3, starting transfers between devices, from_member(): return lax.ppermute(block, 'blk', [(i, i ^ mask) for i in range(members)])  4.61 us
    all_to_all x1, waiting for transfers between devices, on_device(): lax.all_to_all(packed, 'cluster', split_axis=0, concat_axis=0, tiled=True)  3.91 us
    pallas_call x1, Pallas kernels, on_device(): pl.pallas_call(functools.partial(pack_kernel, devices, capacity), out_sha...  2.08 us
    ppermute x3, waiting for transfers between devices, from_member(): return lax.ppermute(block, 'blk', [(i, i ^ mask) for i in range(members)])  2.07 us
    concatenate x1, other arithmetic, on_device(): jnp.concatenate([codebook, centroids], axis=0)  1.09 us
  transfers between devices with their start and end apart: 4, of which 4 were waited for; matrix products, arithmetic and copies ran while one was open for 3% of the time, Pallas kernels for 26%

profile of v13, /device:TPU:0, one launch (start us, length us, event | category | flops | bytes accessed | tf_op | source)
XLA Modules:
  0.0 33.8 jit_solution(6637576048212777106)
XLA Ops:
  0.0 2.1 %pack_rows.1 = bf16[512,128]{1,0:T(8,128)(2,1)} custom-call(s32[64,512]{1,0:T(8,128)} %bitcast.11, s32[1,512]{1,0:T(1,128)} %bitcast.12), custom_call_target="tpu_custom_call" | custom-call | tf_op jit(solution)/shard_map/pack_rows/pallas_call | solution.py:385
  2.1 5.2 %all-to-all-start = ((bf16[8,64,128]{2,1,0:T(8,128)(2,1)}), bf16[8,64,128]{2,1,0:T(8,128)(2,1)S(1)}, u32[]{:S(2)}, u32[]{:S(2)}) async-start(bf16[8,64,128]{2,1,0:T(8,128)(2,1)} %bitcast.10), calls=%async_computation | async-start | bytes 262144 | tf_op jit(solution)/shard_map/all_to_all | solution.py:399
  7.3 1.1 %pad_maximum_fusion.book_ref = bf16[264,1024]{1,0:T(8,128)(2,1)S(1)} fusion(bf16[8,1024]{1,0:T(8,128)(2,1)} %param.7, bf16[256,1024]{1,0:T(8,128)(2,1)} %param.6), kind=kLoop, calls=%fused_computation | loop fusion | flops 1081344 | bytes 1081344 | tf_op jit(solution)/shard_map/concatenate | solution.py:424
  8.4 0.5 %word_table.1 = (bf16[1024,256]{1,0:T(8,128)(2,1)S(1)}, f32[1024,128]{1,0:T(8,128)S(1)}, f32[64,256]{1,0:T(8,128)S(1)}) custom-call(s32[1,1]{1,0:T(1,128)} %bitcast.5.group_ref, bf16[264,1024]{1,0:T(8,128)(2,1)S(1)} %pad_maximum_fusion.book_ref), custom_call_target="tpu_custom_call" | custom-call | flops 1048576 | bytes 1572864 | tf_op jit(solution)/shard_map/word_table/pallas_call | solution.py:411
  8.9 3.9 %all-to-all-done = bf16[8,64,128]{2,1,0:T(8,128)(2,1)S(1)} async-done(((bf16[8,64,128]{2,1,0:T(8,128)(2,1)}), bf16[8,64,128]{2,1,0:T(8,128)(2,1)S(1)}, u32[]{:S(2)}, u32[]{:S(2)}) %all-to-all-start) | async-done | bytes 131104 | tf_op jit(solution)/shard_map/all_to_all | solution.py:399
  12.8 1.6 %collective-permute-start.1 = (bf16[512,128]{1,0:T(8,128)(2,1)S(1)}, bf16[512,128]{1,0:T(8,128)(2,1)S(1)}, u32[]{:S(2)}, u32[]{:S(2)}) collective-permute-start(bf16[512,128]{1,0:T(8,128)(2,1)S(1)} %bitcast.7), channel_id=1, source_target_pairs={{0,1},{1,0},{2,3},{3,2},{4,5},{5,4},{6,7},{7,6},{8,9},{9,8},{10,11... | collective-permute-start | bytes 393224 | tf_op jit(solution)/shard_map/ppermute | solution.py:401
  14.4 2.6 %collective-permute-start = (bf16[512,128]{1,0:T(8,128)(2,1)S(1)}, bf16[512,128]{1,0:T(8,128)(2,1)S(1)}, u32[]{:S(2)}, u32[]{:S(2)}) collective-permute-start(bf16[512,128]{1,0:T(8,128)(2,1)S(1)} %bitcast.8), channel_id=1, source_target_pairs={{0,2},{1,3},{2,0},{3,1},{4,6},{5,7},{6,4},{7,5},{8,10},{9,11},{10,... | collective-permute-start | bytes 393224 | tf_op jit(solution)/shard_map/ppermute | solution.py:401
  17.0 2.2 %rows_0.1 = (bf16[1024,1024]{1,0:T(8,128)(2,1)S(1)}, bf16[1024,1024]{1,0:T(8,128)(2,1)S(1)}, f32[32,8,128]{2,1,0:T(8,128)S(1)}, f32[1024,128]{1,0:T(8,128)S(1)}, f32[8,8,128]{2,1,0:T(8,128)S(1)}) custom-call(s32[1,1]{1,0:T(1,128)} %bitcast.place_ref, bf16[512,128]{1,0:T(8,128)(2,1)S(1)} %bitcast.9, bf16[1024,256]{1,0:T(8,128)(2,1)S(1)} %get-tuple-element.26.refs_0_, ...), custom_call_target="tpu_custom_call" | custom-call | flops 2147483648 | bytes 16777216 | tf_op jit(solution)/shard_map/rows_0/pallas_call | solution.py:448
  19.1 0.5 %collective-permute-done.1.codes_ref = bf16[512,128]{1,0:T(8,128)(2,1)S(1)} collective-permute-done((bf16[512,128]{1,0:T(8,128)(2,1)S(1)}, bf16[512,128]{1,0:T(8,128)(2,1)S(1)}, u32[]{:S(2)}, u32[]{:S(2)}) %collective-permute-start.1) | collective-permute-done | bytes 131104 | tf_op jit(solution)/shard_map/ppermute | solution.py:401
  19.6 2.7 %rows_1.1 = (bf16[1024,1024]{1,0:T(8,128)(2,1)S(1)}, bf16[1024,1024]{1,0:T(8,128)(2,1)S(1)}, f32[32,8,128]{2,1,0:T(8,128)S(1)}, f32[1024,128]{1,0:T(8,128)S(1)}, f32[8,8,128]{2,1,0:T(8,128)S(1)}) custom-call(s32[1,1]{1,0:T(1,128)} %bitcast.place_ref, ...), custom_call_target="tpu_custom_call", output_to_operand_aliasing={{1}: (6, {}), {2}: (7, {}), {3}: (8, {}), {4}: (9, {})} | custom-call | flops 2147483648 | bytes 16777216 | tf_op jit(solution)/shard_map/rows_1/pallas_call | solution.py:448
  22.4 0.5 %collective-permute-done.codes_ref = bf16[512,128]{1,0:T(8,128)(2,1)S(1)} collective-permute-done((bf16[512,128]{1,0:T(8,128)(2,1)S(1)}, bf16[512,128]{1,0:T(8,128)(2,1)S(1)}, u32[]{:S(2)}, u32[]{:S(2)}) %collective-permute-start) | collective-permute-done | bytes 131104 | tf_op jit(solution)/shard_map/ppermute | solution.py:401
  22.9 0.4 %collective-permute-start.2 = (bf16[512,128]{1,0:T(8,128)(2,1)S(1)}, bf16[512,128]{1,0:T(8,128)(2,1)S(1)}, u32[]{:S(2)}, u32[]{:S(2)}) collective-permute-start(bf16[512,128]{1,0:T(8,128)(2,1)S(1)} %collective-permute-done.codes_ref), channel_id=1, source_target_pairs={{0,1},{1,0},{2,3},{3,2},{4,5},{5,4},{6,7},{7,6},{8,9},{9,8},{10,11... | collective-permute-start | bytes 393224 | tf_op jit(solution)/shard_map/ppermute | solution.py:401
  23.3 3.4 %rows_2.1 = (bf16[1024,1024]{1,0:T(8,128)(2,1)S(1)}, bf16[1024,1024]{1,0:T(8,128)(2,1)S(1)}, f32[32,8,128]{2,1,0:T(8,128)S(1)}, f32[1024,128]{1,0:T(8,128)S(1)}, f32[8,8,128]{2,1,0:T(8,128)S(1)}) custom-call(s32[1,1]{1,0:T(1,128)} %bitcast.place_ref, ...), custom_call_target="tpu_custom_call", output_to_operand_aliasing={{1}: (7, {}), {2}: (8, {}), {3}: (9, {}), {4}: (10, {})} | custom-call | flops 2147483648 | bytes 16777216 | tf_op jit(solution)/shard_map/rows_2/pallas_call | solution.py:448
  26.8 1.1 %collective-permute-done.2.codes_ref = bf16[512,128]{1,0:T(8,128)(2,1)S(1)} collective-permute-done((bf16[512,128]{1,0:T(8,128)(2,1)S(1)}, bf16[512,128]{1,0:T(8,128)(2,1)S(1)}, u32[]{:S(2)}, u32[]{:S(2)}) %collective-permute-start.2) | collective-permute-done | bytes 131104 | tf_op jit(solution)/shard_map/ppermute | solution.py:401
  27.9 5.9 %last_rows.1 = (f32[8,128]{1,0:T(8,128)}, bf16[1024,1024]{1,0:T(8,128)(2,1)S(1)}, f32[32,8,128]{2,1,0:T(8,128)S(1)}, f32[1024,128]{1,0:T(8,128)S(1)}, f32[8,8,128]{2,1,0:T(8,128)S(1)}) custom-call(s32[1,1]{1,0:T(1,128)} %bitcast.place_ref, ...), custom_call_target="tpu_custom_call", output_to_operand_aliasing={{1}: (8, {}), {2}: (9, {}), {3}: (10, {}), {4}: (11, {})} | custom-call | flops 8589934592 | bytes 16777216 | tf_op jit(solution)/shard_map/last_rows/pallas_call | solution.py:484
Async XLA Ops:
  2.1 10.7 %all-to-all-start = ((bf16[8,64,128]{2,1,0:T(8,128)(2,1)}), bf16[8,64,128]{2,1,0:T(8,128)(2,1)S(1)}, u32[]{:S(2)}, u32[]{:S(2)}) async-start(bf16[8,64,128]{2,1,0:T(8,128)(2,1)} %bitcast.10), calls=%async_computation | async-start | bytes 262144 | tf_op jit(solution)/shard_map/all_to_all | solution.py:399
  12.8 6.8 %collective-permute-start.1 = (bf16[512,128]{1,0:T(8,128)(2,1)S(1)}, bf16[512,128]{1,0:T(8,128)(2,1)S(1)}, u32[]{:S(2)}, u32[]{:S(2)}) collective-permute-start(bf16[512,128]{1,0:T(8,128)(2,1)S(1)} %bitcast.7), channel_id=1, source_target_pairs={{0,1},{1,0},{2,3},{3,2},{4,5},{5,4},{6,7},{7,6},{8,9},{9,8},{10,11... | collective-permute-start | bytes 393224 | tf_op jit(solution)/shard_map/ppermute | solution.py:401
  14.4 8.5 %collective-permute-start = (bf16[512,128]{1,0:T(8,128)(2,1)S(1)}, bf16[512,128]{1,0:T(8,128)(2,1)S(1)}, u32[]{:S(2)}, u32[]{:S(2)}) collective-permute-start(bf16[512,128]{1,0:T(8,128)(2,1)S(1)} %bitcast.8), channel_id=1, source_target_pairs={{0,2},{1,3},{2,0},{3,1},{4,6},{5,7},{6,4},{7,5},{8,10},{9,11},{10,... | collective-permute-start | bytes 393224 | tf_op jit(solution)/shard_map/ppermute | solution.py:401
  22.9 5.0 %collective-permute-start.2 = (bf16[512,128]{1,0:T(8,128)(2,1)S(1)}, bf16[512,128]{1,0:T(8,128)(2,1)S(1)}, u32[]{:S(2)}, u32[]{:S(2)}) collective-permute-start(bf16[512,128]{1,0:T(8,128)(2,1)S(1)} %collective-permute-done.codes_ref), channel_id=1, source_target_pairs={{0,1},{1,0},{2,3},{3,2},{4,5},{5,4},{6,7},{7,6},{8,9},{9,8},{10,11... | collective-permute-start | bytes 393224 | tf_op jit(solution)/shard_map/ppermute | solution.py:401

commit v14 on v13

--- a/solution.py
+++ b/solution.py
@@ -221,6 +221,10 @@
     )
     row_ids = lax.broadcasted_iota(jnp.int32, (COLS, LANES), 0)
     lane_ids = lax.broadcasted_iota(jnp.int32, (COLS, LANES), 1)
+    row_filled = [
+        jnp.transpose(jnp.broadcast_to(mark_ref[other][0:1, :], (LANES, LANES))) > 0
+        for other in range(above // LANES)
+    ]
     for part in range(COLS // LANES):
         tile = block * (COLS // LANES) + part
         lanes = slice(part * LANES, (part + 1) * LANES)
@@ -234,12 +238,9 @@
             rows = slice(other * LANES, (other + 1) * LANES)
             piece = scores[rows, lanes]
             best_ref[rows, :] = jnp.maximum(best_ref[rows, :], jnp.where(filled, piece, LOW))
-            row_filled = jnp.transpose(
-                jnp.broadcast_to(mark_ref[other][0:1, :], (LANES, LANES))
-            )
             mirror = jnp.maximum(
                 mirror,
-                jnp.max(jnp.where(row_filled > 0, piece, LOW), axis=0, keepdims=True),
+                jnp.max(jnp.where(row_filled[other], piece, LOW), axis=0, keepdims=True),
             )
         mirror_ref[tile] = jnp.broadcast_to(mirror, (8, LANES))
 

time: 34.1 us -> 34.2 us (level)
  no operation moved by 1% of the time
where the time goes in v14:
time: 34.2 us; the launch traced here: 33.8 us
  Pallas kernels  16.8 us (49%)
  starting transfers between devices  9.8 us (29%)
  waiting for transfers between devices  6.08 us (18%)
  other arithmetic  1.09 us (3%)
    pallas_call x3, Pallas kernels, take_in(): pl.pallas_call(functools.partial(next_kernel, block), out_shape=(units_sh...  8.25 us
    pallas_call x1, Pallas kernels, on_device(): pl.pallas_call(functools.partial(last_kernel, (capacity, clusters, member...  5.95 us
    all_to_all x1, starting transfers between devices, on_device(): lax.all_to_all(packed, 'cluster', split_axis=0, concat_axis=0, tiled=True)  5.19 us
    ppermute x3, starting transfers between devices, from_member(): return lax.ppermute(block, 'blk', [(i, i ^ mask) for i in range(members)])  4.61 us
    all_to_all x1, waiting for transfers between devices, on_device(): lax.all_to_all(packed, 'cluster', split_axis=0, concat_axis=0, tiled=True)  3.91 us
    ppermute x3, waiting for transfers between devices, from_member(): return lax.ppermute(block, 'blk', [(i, i ^ mask) for i in range(members)])  2.17 us
    pallas_call x1, Pallas kernels, on_device(): pl.pallas_call(functools.partial(pack_kernel, devices, capacity), out_sha...  2.08 us
    concatenate x1, other arithmetic, on_device(): jnp.concatenate([codebook, centroids], axis=0)  1.09 us
  transfers between devices with their start and end apart: 4, of which 4 were waited for; matrix products, arithmetic and copies ran while one was open for 3% of the time, Pallas kernels for 26%

profile of v14, /device:TPU:0, one launch (start us, length us, event | category | flops | bytes accessed | tf_op | source)
XLA Modules:
  0.0 33.8 jit_solution(9229808263835678015)
XLA Ops:
  0.0 2.1 %pack_rows.1 = bf16[512,128]{1,0:T(8,128)(2,1)} custom-call(s32[64,512]{1,0:T(8,128)} %bitcast.11, s32[1,512]{1,0:T(1,128)} %bitcast.12), custom_call_target="tpu_custom_call" | custom-call | tf_op jit(solution)/shard_map/pack_rows/pallas_call | solution.py:386
  2.1 5.2 %all-to-all-start = ((bf16[8,64,128]{2,1,0:T(8,128)(2,1)}), bf16[8,64,128]{2,1,0:T(8,128)(2,1)S(1)}, u32[]{:S(2)}, u32[]{:S(2)}) async-start(bf16[8,64,128]{2,1,0:T(8,128)(2,1)} %bitcast.10), calls=%async_computation | async-start | bytes 262144 | tf_op jit(solution)/shard_map/all_to_all | solution.py:400
  7.3 1.1 %pad_maximum_fusion.book_ref = bf16[264,1024]{1,0:T(8,128)(2,1)S(1)} fusion(bf16[8,1024]{1,0:T(8,128)(2,1)} %param.7, bf16[256,1024]{1,0:T(8,128)(2,1)} %param.6), kind=kLoop, calls=%fused_computation | loop fusion | flops 1081344 | bytes 1081344 | tf_op jit(solution)/shard_map/concatenate | solution.py:425
  8.4 0.5 %word_table.1 = (bf16[1024,256]{1,0:T(8,128)(2,1)S(1)}, f32[1024,128]{1,0:T(8,128)S(1)}, f32[64,256]{1,0:T(8,128)S(1)}) custom-call(s32[1,1]{1,0:T(1,128)} %bitcast.5.group_ref, bf16[264,1024]{1,0:T(8,128)(2,1)S(1)} %pad_maximum_fusion.book_ref), custom_call_target="tpu_custom_call" | custom-call | flops 1048576 | bytes 1572864 | tf_op jit(solution)/shard_map/word_table/pallas_call | solution.py:412
  8.9 3.9 %all-to-all-done = bf16[8,64,128]{2,1,0:T(8,128)(2,1)S(1)} async-done(((bf16[8,64,128]{2,1,0:T(8,128)(2,1)}), bf16[8,64,128]{2,1,0:T(8,128)(2,1)S(1)}, u32[]{:S(2)}, u32[]{:S(2)}) %all-to-all-start) | async-done | bytes 131104 | tf_op jit(solution)/shard_map/all_to_all | solution.py:400
  12.8 1.6 %collective-permute-start.1 = (bf16[512,128]{1,0:T(8,128)(2,1)S(1)}, bf16[512,128]{1,0:T(8,128)(2,1)S(1)}, u32[]{:S(2)}, u32[]{:S(2)}) collective-permute-start(bf16[512,128]{1,0:T(8,128)(2,1)S(1)} %bitcast.7), channel_id=1, source_target_pairs={{0,1},{1,0},{2,3},{3,2},{4,5},{5,4},{6,7},{7,6},{8,9},{9,8},{10,11... | collective-permute-start | bytes 393224 | tf_op jit(solution)/shard_map/ppermute | solution.py:402
  14.4 2.6 %collective-permute-start = (bf16[512,128]{1,0:T(8,128)(2,1)S(1)}, bf16[512,128]{1,0:T(8,128)(2,1)S(1)}, u32[]{:S(2)}, u32[]{:S(2)}) collective-permute-start(bf16[512,128]{1,0:T(8,128)(2,1)S(1)} %bitcast.8), channel_id=1, source_target_pairs={{0,2},{1,3},{2,0},{3,1},{4,6},{5,7},{6,4},{7,5},{8,10},{9,11},{10,... | collective-permute-start | bytes 393224 | tf_op jit(solution)/shard_map/ppermute | solution.py:402
  17.0 2.2 %rows_0.1 = (bf16[1024,1024]{1,0:T(8,128)(2,1)S(1)}, bf16[1024,1024]{1,0:T(8,128)(2,1)S(1)}, f32[32,8,128]{2,1,0:T(8,128)S(1)}, f32[1024,128]{1,0:T(8,128)S(1)}, f32[8,8,128]{2,1,0:T(8,128)S(1)}) custom-call(s32[1,1]{1,0:T(1,128)} %bitcast.place_ref, bf16[512,128]{1,0:T(8,128)(2,1)S(1)} %bitcast.9, bf16[1024,256]{1,0:T(8,128)(2,1)S(1)} %get-tuple-element.26.refs_0_, ...), custom_call_target="tpu_custom_call" | custom-call | flops 2147483648 | bytes 16777216 | tf_op jit(solution)/shard_map/rows_0/pallas_call | solution.py:449
  19.1 0.5 %collective-permute-done.1.codes_ref = bf16[512,128]{1,0:T(8,128)(2,1)S(1)} collective-permute-done((bf16[512,128]{1,0:T(8,128)(2,1)S(1)}, bf16[512,128]{1,0:T(8,128)(2,1)S(1)}, u32[]{:S(2)}, u32[]{:S(2)}) %collective-permute-start.1) | collective-permute-done | bytes 131104 | tf_op jit(solution)/shard_map/ppermute | solution.py:402
  19.6 2.7 %rows_1.1 = (bf16[1024,1024]{1,0:T(8,128)(2,1)S(1)}, bf16[1024,1024]{1,0:T(8,128)(2,1)S(1)}, f32[32,8,128]{2,1,0:T(8,128)S(1)}, f32[1024,128]{1,0:T(8,128)S(1)}, f32[8,8,128]{2,1,0:T(8,128)S(1)}) custom-call(s32[1,1]{1,0:T(1,128)} %bitcast.place_ref, ...), custom_call_target="tpu_custom_call", output_to_operand_aliasing={{1}: (6, {}), {2}: (7, {}), {3}: (8, {}), {4}: (9, {})} | custom-call | flops 2147483648 | bytes 16777216 | tf_op jit(solution)/shard_map/rows_1/pallas_call | solution.py:449
  22.4 0.5 %collective-permute-done.codes_ref = bf16[512,128]{1,0:T(8,128)(2,1)S(1)} collective-permute-done((bf16[512,128]{1,0:T(8,128)(2,1)S(1)}, bf16[512,128]{1,0:T(8,128)(2,1)S(1)}, u32[]{:S(2)}, u32[]{:S(2)}) %collective-permute-start) | collective-permute-done | bytes 131104 | tf_op jit(solution)/shard_map/ppermute | solution.py:402
  22.9 0.4 %collective-permute-start.2 = (bf16[512,128]{1,0:T(8,128)(2,1)S(1)}, bf16[512,128]{1,0:T(8,128)(2,1)S(1)}, u32[]{:S(2)}, u32[]{:S(2)}) collective-permute-start(bf16[512,128]{1,0:T(8,128)(2,1)S(1)} %collective-permute-done.codes_ref), channel_id=1, source_target_pairs={{0,1},{1,0},{2,3},{3,2},{4,5},{5,4},{6,7},{7,6},{8,9},{9,8},{10,11... | collective-permute-start | bytes 393224 | tf_op jit(solution)/shard_map/ppermute | solution.py:402
  23.3 3.4 %rows_2.1 = (bf16[1024,1024]{1,0:T(8,128)(2,1)S(1)}, bf16[1024,1024]{1,0:T(8,128)(2,1)S(1)}, f32[32,8,128]{2,1,0:T(8,128)S(1)}, f32[1024,128]{1,0:T(8,128)S(1)}, f32[8,8,128]{2,1,0:T(8,128)S(1)}) custom-call(s32[1,1]{1,0:T(1,128)} %bitcast.place_ref, ...), custom_call_target="tpu_custom_call", output_to_operand_aliasing={{1}: (7, {}), {2}: (8, {}), {3}: (9, {}), {4}: (10, {})} | custom-call | flops 2147483648 | bytes 16777216 | tf_op jit(solution)/shard_map/rows_2/pallas_call | solution.py:449
  26.7 1.1 %collective-permute-done.2.codes_ref = bf16[512,128]{1,0:T(8,128)(2,1)S(1)} collective-permute-done((bf16[512,128]{1,0:T(8,128)(2,1)S(1)}, bf16[512,128]{1,0:T(8,128)(2,1)S(1)}, u32[]{:S(2)}, u32[]{:S(2)}) %collective-permute-start.2) | collective-permute-done | bytes 131104 | tf_op jit(solution)/shard_map/ppermute | solution.py:402
  27.9 5.9 %last_rows.1 = (f32[8,128]{1,0:T(8,128)}, bf16[1024,1024]{1,0:T(8,128)(2,1)S(1)}, f32[32,8,128]{2,1,0:T(8,128)S(1)}, f32[1024,128]{1,0:T(8,128)S(1)}, f32[8,8,128]{2,1,0:T(8,128)S(1)}) custom-call(s32[1,1]{1,0:T(1,128)} %bitcast.place_ref, ...), custom_call_target="tpu_custom_call", output_to_operand_aliasing={{1}: (8, {}), {2}: (9, {}), {3}: (10, {}), {4}: (11, {})} | custom-call | flops 8589934592 | bytes 16777216 | tf_op jit(solution)/shard_map/last_rows/pallas_call | solution.py:485
Async XLA Ops:
  2.1 10.7 %all-to-all-start = ((bf16[8,64,128]{2,1,0:T(8,128)(2,1)}), bf16[8,64,128]{2,1,0:T(8,128)(2,1)S(1)}, u32[]{:S(2)}, u32[]{:S(2)}) async-start(bf16[8,64,128]{2,1,0:T(8,128)(2,1)} %bitcast.10), calls=%async_computation | async-start | bytes 262144 | tf_op jit(solution)/shard_map/all_to_all | solution.py:400
  12.8 6.8 %collective-permute-start.1 = (bf16[512,128]{1,0:T(8,128)(2,1)S(1)}, bf16[512,128]{1,0:T(8,128)(2,1)S(1)}, u32[]{:S(2)}, u32[]{:S(2)}) collective-permute-start(bf16[512,128]{1,0:T(8,128)(2,1)S(1)} %bitcast.7), channel_id=1, source_target_pairs={{0,1},{1,0},{2,3},{3,2},{4,5},{5,4},{6,7},{7,6},{8,9},{9,8},{10,11... | collective-permute-start | bytes 393224 | tf_op jit(solution)/shard_map/ppermute | solution.py:402
  14.4 8.5 %collective-permute-start = (bf16[512,128]{1,0:T(8,128)(2,1)S(1)}, bf16[512,128]{1,0:T(8,128)(2,1)S(1)}, u32[]{:S(2)}, u32[]{:S(2)}) collective-permute-start(bf16[512,128]{1,0:T(8,128)(2,1)S(1)} %bitcast.8), channel_id=1, source_target_pairs={{0,2},{1,3},{2,0},{3,1},{4,6},{5,7},{6,4},{7,5},{8,10},{9,11},{10,... | collective-permute-start | bytes 393224 | tf_op jit(solution)/shard_map/ppermute | solution.py:402
  22.9 5.0 %collective-permute-start.2 = (bf16[512,128]{1,0:T(8,128)(2,1)S(1)}, bf16[512,128]{1,0:T(8,128)(2,1)S(1)}, u32[]{:S(2)}, u32[]{:S(2)}) collective-permute-start(bf16[512,128]{1,0:T(8,128)(2,1)S(1)} %collective-permute-done.codes_ref), channel_id=1, source_target_pairs={{0,1},{1,0},{2,3},{3,2},{4,5},{5,4},{6,7},{7,6},{8,9},{9,8},{10,11... | collective-permute-start | bytes 393224 | tf_op jit(solution)/shard_map/ppermute | solution.py:402
